TPU v7x, 256 devices: a whole 4x4x8 slice. The times are simulated.
256 devices in a mesh: seq: 64 (over y, z, core), grp: 4 (over x).
Axes of the slice: x: 4, y: 4, z: 8, core: 2. Of those that a mesh axis runs over, the one named last changes fastest.
Arguments:
- queries: bfloat16 [16384, 8192], P(('grp', 'seq')), parts along dimension 0, may hold values from -6 to 6, as said below
- key_heads: bfloat16 [16384, 1024], P(('grp', 'seq')), parts along dimension 0, may hold values from -6 to 6, as said below
- value_heads: bfloat16 [16384, 1024], P(('grp', 'seq')), parts along dimension 0, may hold values from -6 to 6
- doc_lengths: int32 [32], P('grp'), parts along dimension 0, may hold values from 1 to 1024, 4096 in all
Outputs:
- attended: bfloat16 [16384, 8192], P(('grp', 'seq')), parts along dimension 0
There are 4 independent parts, one for each index of `grp`. A program takes and returns all parts, laid end to end along the dimension named above; each array names one. Nothing has to cross between parts.
Inputs may be any that keep to these rules, and one draw needn't show every extreme that they name: `doc_lengths`: 8 documents, each of 1 to 1024 tokens, together 4096 tokens; one document has exactly 1024 tokens. `queries`: real values. `key_heads`: real values.
All inputs are finite; a program needn't handle non-finite values.
Results may differ from a plain program's by a relative error of at most 0.007.
Values may be sent and summed in bfloat16 or wider, within the bound.
No kernel may reach another device: no remote copies, remote signals or barrier semaphores. Data moves between devices by JAX's collectives and lax.ppermute only.
A program may use at most 128 MiB of HBM per device.

v0:
```python
import functools

import jax
import jax.numpy as jnp
from jax import lax
from jax.experimental import pallas as pl
from jax.experimental.pallas import tpu as pltpu
from jax.sharding import PartitionSpec as P

HK = 8
GROUP = 8
DH = 128
HQ = 64
ROWS = 64
COLS = GROUP * ROWS
NEG = -1e30
SCALE = DH ** (-0.5)

CHIPS = 32
NEAR = 4
FAR = 8


def chip_route(ahead):
    return [(2 * c + k, 2 * ((c + ahead) % CHIPS) + k) for c in range(CHIPS) for k in range(2)]


SIBLING = [(i, i ^ 1) for i in range(2 * CHIPS)]


def flash_kernel(n_shards, first, last, distances, *refs):
    here_ref, docs_ref, q_ref = refs[:3]
    refs = refs[3:]
    kv = refs[: 2 * n_shards]
    refs = refs[2 * n_shards :]
    if first:
        m_in = l_in = acc_in = None
    else:
        m_in, l_in, acc_in = refs[:3]
        refs = refs[3:]
    if last:
        (out_ref,) = refs
    else:
        m_out, l_out, acc_out = refs

    here = here_ref[0]
    core = lax.rem(here, 2)
    col = lax.broadcasted_iota(jnp.int32, (1, COLS), 1)
    q_pos = here * ROWS + lax.rem(col, ROWS)
    start = jnp.zeros_like(q_pos)
    end = jnp.int32(0)
    for d in range(8):
        end = end + docs_ref[d]
        start = jnp.where(q_pos >= end, end, start)
    n_keys = n_shards * ROWS
    row = lax.broadcasted_iota(jnp.int32, (ROWS, 1), 0)
    k_pos = jnp.concatenate([here_off(here, core, d) * ROWS + row for d in distances], axis=0)
    visible = (k_pos >= start) & (k_pos <= q_pos)

    for h in range(HK):
        cols = slice(h * DH, (h + 1) * DH)
        keys = jnp.concatenate([kv[2 * s][:, cols] for s in range(n_shards)], axis=0)
        values = jnp.concatenate([kv[2 * s + 1][:, cols] for s in range(n_shards)], axis=0)
        q = jnp.concatenate(
            [q_ref[:, (h * GROUP + g) * DH : (h * GROUP + g + 1) * DH] for g in range(GROUP)], axis=0
        )
        scores = lax.dot_general(keys, q, (((1,), (1,)), ((), ())), preferred_element_type=jnp.float32)
        scores = jnp.where(visible, scores * SCALE, NEG)
        top = jnp.max(scores, axis=0, keepdims=True)
        if not first:
            old = m_in[h : h + 1, :]
            top = jnp.maximum(top, old)
        weights = jnp.exp(scores - top)
        total = jnp.sum(weights, axis=0, keepdims=True)
        part = lax.dot_general(
            values, weights.astype(jnp.bfloat16), (((0,), (0,)), ((), ())), preferred_element_type=jnp.float32
        )
        if not first:
            factor = jnp.exp(old - top)
            total = total + l_in[h : h + 1, :] * factor
            part = part + acc_in[h] * factor
        if last:
            result = (part / total).T.astype(jnp.bfloat16)
            for g in range(GROUP):
                out_ref[:, (h * GROUP + g) * DH : (h * GROUP + g + 1) * DH] = result[g * ROWS : (g + 1) * ROWS, :]
        else:
            m_out[h : h + 1, :] = top
            l_out[h : h + 1, :] = total
            acc_out[h] = part


def here_off(here, core, distance):
    chips, sibling = distance
    return here - 2 * chips + (1 - 2 * core if sibling else 0)


def flash(here, docs, q, shards, distances, state, last):
    first = state is None
    n = len(distances)
    vmem = pl.BlockSpec(memory_space=pltpu.VMEM)
    smem = pl.BlockSpec(memory_space=pltpu.SMEM)
    operands = [here, docs, q] + list(shards) + ([] if first else list(state))
    specs = [smem, smem] + [vmem] * (len(operands) - 2)
    if last:
        out_shape = jax.ShapeDtypeStruct((ROWS, HQ * DH), jnp.bfloat16)
        out_specs = vmem
    else:
        out_shape = (
            jax.ShapeDtypeStruct((HK, COLS), jnp.float32),
            jax.ShapeDtypeStruct((HK, COLS), jnp.float32),
            jax.ShapeDtypeStruct((HK, DH, COLS), jnp.float32),
        )
        out_specs = (vmem, vmem, vmem)
    return pl.pallas_call(
        functools.partial(flash_kernel, n, first, last, tuple(distances)),
        out_shape=out_shape,
        in_specs=specs,
        out_specs=out_specs,
        compiler_params=pltpu.CompilerParams(vmem_limit_bytes=48 * 1024 * 1024),
        cost_estimate=pl.CostEstimate(
            flops=4 * n * ROWS * HQ * ROWS * DH, bytes_accessed=2 << 20, transcendentals=n * ROWS * HQ * ROWS
        ),
    )(*operands)


def per_device(queries, key_heads, value_heads, doc_lengths):
    here = lax.axis_index("seq").astype(jnp.int32).reshape(1)

    def send(block, ahead):
        return lax.ppermute(block, "seq", chip_route(ahead))

    def swap(blocks):
        n = len(blocks)
        got = lax.ppermute(jnp.concatenate(blocks, axis=0), "seq", SIBLING)
        return [got[i * ROWS : (i + 1) * ROWS] for i in range(n)]

    own = (key_heads, value_heads)
    near, far = own, own
    shards = [list(own) + swap(own)]
    distances = [[(0, False), (0, True)]]
    for step in range(NEAR):
        near = tuple(send(x, 1) for x in near)
        far = tuple(send(x, FAR if step == 0 else -1) for x in far)
        both = list(near) + list(far)
        shards.append(both + swap(both))
        distances.append([(step + 1, False), (FAR - step, False), (step + 1, True), (FAR - step, True)])

    early = sum(shards[:NEAR], [])
    early_at = sum(distances[:NEAR], [])
    state = flash(here, doc_lengths, queries, early, early_at, None, False)
    return flash(here, doc_lengths, queries, shards[NEAR], distances[NEAR], state, True)


def solution(mesh):
    return jax.shard_map(
        per_device,
        mesh=mesh,
        in_specs=(
            P(("grp", "seq"), None),
            P(("grp", "seq"), None),
            P(("grp", "seq"), None),
            P("grp"),
        ),
        out_specs=P(("grp", "seq"), None),
        check_vma=False,
    )
```

profile of v0, /device:TPU:1, one launch (start us, length us, event | category | flops | bytes accessed | tf_op | source)
XLA Modules:
  0.0 66.3 jit_solution(3272500070746775310)
XLA Ops:
  0.0 2.1 %collective-permute-start.8 = (bf16[64,1024]{1,0:T(8,128)(2,1)}, bf16[64,1024]{1,0:T(8,128)(2,1)S(1)}, u32[]{:S(2)}, u32[]{:S(2)}) collective-permute-start(bf16[64,1024]{1,0:T(8,128)(2,1)} %refs_3_.1), channel_id=1, source_target_pairs={{0,64},{4,68},{8,72},{12,76},{16,80},{20,84},{24,88},{28,92},{32,9... | collective-permute-start | bytes 393224 | tf_op jit(solution)/shard_map/ppermute | solution.py:130
  2.1 1.3 %collective-permute-start.12 = (bf16[64,1024]{1,0:T(8,128)(2,1)}, bf16[64,1024]{1,0:T(8,128)(2,1)S(1)}, u32[]{:S(2)}, u32[]{:S(2)}) collective-permute-start(bf16[64,1024]{1,0:T(8,128)(2,1)} %refs_4_.1), channel_id=1, source_target_pairs={{0,64},{4,68},{8,72},{12,76},{16,80},{20,84},{24,88},{28,92},{32,9... | collective-permute-start | bytes 393224 | tf_op jit(solution)/shard_map/ppermute | solution.py:130
  3.4 1.6 %collective-permute-start = (bf16[64,1024]{1,0:T(8,128)(2,1)}, bf16[64,1024]{1,0:T(8,128)(2,1)S(1)}, u32[]{:S(2)}, u32[]{:S(2)}) collective-permute-start(bf16[64,1024]{1,0:T(8,128)(2,1)} %refs_3_.1), channel_id=1, source_target_pairs={{0,8},{4,12},{8,16},{12,20},{16,24},{20,28},{24,32},{28,36},{32,40... | collective-permute-start | bytes 393224 | tf_op jit(solution)/shard_map/ppermute | solution.py:130
  5.1 1.6 %collective-permute-start.4 = (bf16[64,1024]{1,0:T(8,128)(2,1)}, bf16[64,1024]{1,0:T(8,128)(2,1)S(1)}, u32[]{:S(2)}, u32[]{:S(2)}) collective-permute-start(bf16[64,1024]{1,0:T(8,128)(2,1)} %refs_4_.1), channel_id=1, source_target_pairs={{0,8},{4,12},{8,16},{12,20},{16,24},{20,28},{24,32},{28,36},{32,40... | collective-permute-start | bytes 393224 | tf_op jit(solution)/shard_map/ppermute | solution.py:130
  6.7 0.0 collective-permute-done.8.refs_9_
  6.7 6.7 %collective-permute-start.9 = (bf16[64,1024]{1,0:T(8,128)(2,1)S(1)}, bf16[64,1024]{1,0:T(8,128)(2,1)S(1)}, u32[]{:S(2)}, u32[]{:S(2)}) collective-permute-start(bf16[64,1024]{1,0:T(8,128)(2,1)S(1)} %collective-permute-done.8.refs_9_), channel_id=1, source_target_pairs={{0,248},{4,252},{8,0},{12,4},{16,8},{20,12},{24,16},{28,20},{32,24... | collective-permute-start | bytes 393224 | tf_op jit(solution)/shard_map/ppermute | solution.py:130
  13.4 1.0 %pad_maximum_fusion.4 = bf16[128,1024]{1,0:T(8,128)(2,1)S(1)} fusion(bf16[64,1024]{1,0:T(8,128)(2,1)} %refs_4_.1, bf16[64,1024]{1,0:T(8,128)(2,1)} %refs_3_.1), kind=kLoop, calls=%fused_computation.4 | loop fusion | flops 524288 | bytes 524288 | tf_op jit(solution)/shard_map/concatenate | solution.py:134
  14.4 3.1 %collective-permute-start.17 = (bf16[128,1024]{1,0:T(8,128)(2,1)S(1)}, bf16[128,1024]{1,0:T(8,128)(2,1)S(1)}, u32[]{:S(2)}, u32[]{:S(2)}) collective-permute-start(bf16[128,1024]{1,0:T(8,128)(2,1)S(1)} %pad_maximum_fusion.4), channel_id=1, source_target_pairs={{0,4},{4,0},{8,12},{12,8},{16,20},{20,16},{24,28},{28,24},{32,36},... | collective-permute-start | bytes 786440 | tf_op jit(solution)/shard_map/ppermute | solution.py:134
  17.5 0.0 collective-permute-done.12.refs_10_
  17.5 0.7 %collective-permute-start.13 = (bf16[64,1024]{1,0:T(8,128)(2,1)S(1)}, bf16[64,1024]{1,0:T(8,128)(2,1)S(1)}, u32[]{:S(2)}, u32[]{:S(2)}) collective-permute-start(bf16[64,1024]{1,0:T(8,128)(2,1)S(1)} %collective-permute-done.12.refs_10_), channel_id=1, source_target_pairs={{0,248},{4,252},{8,0},{12,4},{16,8},{20,12},{24,16},{28,20},{32,24... | collective-permute-start | bytes 393224 | tf_op jit(solution)/shard_map/ppermute | solution.py:130
  18.2 0.0 collective-permute-done.refs_7_
  18.2 0.7 %collective-permute-start.1 = (bf16[64,1024]{1,0:T(8,128)(2,1)S(1)}, bf16[64,1024]{1,0:T(8,128)(2,1)S(1)}, u32[]{:S(2)}, u32[]{:S(2)}) collective-permute-start(bf16[64,1024]{1,0:T(8,128)(2,1)S(1)} %collective-permute-done.refs_7_), channel_id=1, source_target_pairs={{0,8},{4,12},{8,16},{12,20},{16,24},{20,28},{24,32},{28,36},{32,40... | collective-permute-start | bytes 393224 | tf_op jit(solution)/shard_map/ppermute | solution.py:130
  19.0 0.0 collective-permute-done.4.refs_8_
  19.0 0.1 collective-permute-start.5
  19.1 0.0 collective-permute-done.9.refs_17_
  19.1 4.7 %collective-permute-start.10 = (bf16[64,1024]{1,0:T(8,128)(2,1)S(1)}, bf16[64,1024]{1,0:T(8,128)(2,1)S(1)}, u32[]{:S(2)}, u32[]{:S(2)}) collective-permute-start(bf16[64,1024]{1,0:T(8,128)(2,1)S(1)} %collective-permute-done.9.refs_17_), channel_id=1, source_target_pairs={{0,248},{4,252},{8,0},{12,4},{16,8},{20,12},{24,16},{28,20},{32,24... | collective-permute-start | bytes 393224 | tf_op jit(solution)/shard_map/ppermute | solution.py:130
  23.8 0.0 collective-permute-done.13.refs_18_
  23.8 2.8 %collective-permute-start.14 = (bf16[64,1024]{1,0:T(8,128)(2,1)S(1)}, bf16[64,1024]{1,0:T(8,128)(2,1)S(1)}, u32[]{:S(2)}, u32[]{:S(2)}) collective-permute-start(bf16[64,1024]{1,0:T(8,128)(2,1)S(1)} %collective-permute-done.13.refs_18_), channel_id=1, source_target_pairs={{0,248},{4,252},{8,0},{12,4},{16,8},{20,12},{24,16},{28,20},{32,24... | collective-permute-start | bytes 393224 | tf_op jit(solution)/shard_map/ppermute | solution.py:130
  26.6 0.0 collective-permute-done.1.refs_15_
  26.6 0.0 collective-permute-start.2
  26.6 2.5 %collective-permute-done.5.refs_16_ = bf16[64,1024]{1,0:T(8,128)(2,1)S(1)} collective-permute-done((bf16[64,1024]{1,0:T(8,128)(2,1)S(1)}, bf16[64,1024]{1,0:T(8,128)(2,1)S(1)}, u32[]{:S(2)}, u32[]{:S(2)}) %collective-permute-start.5) | collective-permute-done | bytes 131104 | tf_op jit(solution)/shard_map/ppermute | solution.py:130
  29.1 0.0 collective-permute-start.6
  29.1 0.0 collective-permute-done.10.refs_25_
  29.1 4.8 %collective-permute-start.11 = (bf16[64,1024]{1,0:T(8,128)(2,1)S(1)}, bf16[64,1024]{1,0:T(8,128)(2,1)S(1)}, u32[]{:S(2)}, u32[]{:S(2)}) collective-permute-start(bf16[64,1024]{1,0:T(8,128)(2,1)S(1)} %collective-permute-done.10.refs_25_), channel_id=1, source_target_pairs={{0,248},{4,252},{8,0},{12,4},{16,8},{20,12},{24,16},{28,20},{32,24... | collective-permute-start | bytes 393224 | tf_op jit(solution)/shard_map/ppermute | solution.py:130
  33.9 0.0 collective-permute-done.17
  33.9 1.8 %collective-permute-start.18 = (bf16[256,1024]{1,0:T(8,128)(2,1)S(1)}, bf16[256,1024]{1,0:T(8,128)(2,1)S(1)}, u32[]{:S(2)}, u32[]{:S(2)}) collective-permute-start(bf16[256,1024]{1,0:T(8,128)(2,1)S(1)} %pad_maximum_fusion.1), channel_id=1, source_target_pairs={{0,4},{4,0},{8,12},{12,8},{16,20},{20,16},{24,28},{28,24},{32,36},... | collective-permute-start | bytes 1572872 | tf_op jit(solution)/shard_map/ppermute | solution.py:134
  35.8 0.0 collective-permute-done.14.refs_26_
  35.8 0.1 collective-permute-start.19
  35.9 0.0 collective-permute-done.2.refs_23_
  35.9 0.3 collective-permute-start.15
  36.2 1.6 %collective-permute-done.6.refs_24_ = bf16[64,1024]{1,0:T(8,128)(2,1)S(1)} collective-permute-done((bf16[64,1024]{1,0:T(8,128)(2,1)S(1)}, bf16[64,1024]{1,0:T(8,128)(2,1)S(1)}, u32[]{:S(2)}, u32[]{:S(2)}) %collective-permute-start.6) | collective-permute-done | bytes 131104 | tf_op jit(solution)/shard_map/ppermute | solution.py:130
  37.8 0.0 collective-permute-start.3
  37.8 0.0 collective-permute-done.11.refs_5_
  37.8 0.0 collective-permute-start.7
  37.9 0.0 copy-start.1
  37.9 0.0 copy-start.2
  37.9 0.0 copy-start.3
  38.0 0.0 copy-start.4
  38.0 2.0 %collective-permute-done.15.refs_6_ = bf16[64,1024]{1,0:T(8,128)(2,1)S(1)} collective-permute-done((bf16[64,1024]{1,0:T(8,128)(2,1)S(1)}, bf16[64,1024]{1,0:T(8,128)(2,1)S(1)}, u32[]{:S(2)}, u32[]{:S(2)}) %collective-permute-start.15) | collective-permute-done | bytes 131104 | tf_op jit(solution)/shard_map/ppermute | solution.py:130
  40.0 2.6 %collective-permute-start.20 = (bf16[256,1024]{1,0:T(8,128)(2,1)S(1)}, bf16[256,1024]{1,0:T(8,128)(2,1)S(1)}, u32[]{:S(2)}, u32[]{:S(2)}) collective-permute-start(bf16[256,1024]{1,0:T(8,128)(2,1)S(1)} %pad_maximum_fusion.3), channel_id=1, source_target_pairs={{0,4},{4,0},{8,12},{12,8},{16,20},{20,16},{24,28},{28,24},{32,36},... | collective-permute-start | bytes 1572872 | tf_op jit(solution)/shard_map/ppermute | solution.py:134
  42.6 2.3 %collective-permute-done.3.refs_3_ = bf16[64,1024]{1,0:T(8,128)(2,1)S(1)} collective-permute-done((bf16[64,1024]{1,0:T(8,128)(2,1)S(1)}, bf16[64,1024]{1,0:T(8,128)(2,1)S(1)}, u32[]{:S(2)}, u32[]{:S(2)}) %collective-permute-start.3) | collective-permute-done | bytes 131104 | tf_op jit(solution)/shard_map/ppermute | solution.py:130
  45.0 2.5 %collective-permute-done.7.refs_4_ = bf16[64,1024]{1,0:T(8,128)(2,1)S(1)} collective-permute-done((bf16[64,1024]{1,0:T(8,128)(2,1)S(1)}, bf16[64,1024]{1,0:T(8,128)(2,1)S(1)}, u32[]{:S(2)}, u32[]{:S(2)}) %collective-permute-start.7) | collective-permute-done | bytes 131104 | tf_op jit(solution)/shard_map/ppermute | solution.py:130
  47.5 2.8 %collective-permute-start.16 = (bf16[256,1024]{1,0:T(8,128)(2,1)S(1)}, bf16[256,1024]{1,0:T(8,128)(2,1)S(1)}, u32[]{:S(2)}, u32[]{:S(2)}) collective-permute-start(bf16[256,1024]{1,0:T(8,128)(2,1)S(1)} %pad_maximum_fusion), channel_id=1, source_target_pairs={{0,4},{4,0},{8,12},{12,8},{16,20},{20,16},{24,28},{28,24},{32,36},... | collective-permute-start | bytes 1572872 | tf_op jit(solution)/shard_map/ppermute | solution.py:134
  50.2 0.0 collective-permute-done.18
  50.3 0.0 collective-permute-done.19
  50.3 0.0 collective-permute-done.20
  50.4 0.0 copy-done.1
  50.4 0.0 copy-done.2
  50.4 0.0 copy-done.3
  50.4 0.0 copy-done.4
  50.4 9.6 %shard_map.46 = (f32[8,512]{1,0:T(8,128)S(1)}, f32[8,512]{1,0:T(8,128)S(1)}, f32[8,128,512]{2,1,0:T(8,128)}) custom-call(s32[1]{0:T(128)} %bitcast.refs_0_, s32[8]{0:T(128)S(1)} %copy-done.4, bf16[64,8192]{1,0:T(8,128)(2,1)S(1)} %copy-done.1, bf16[64,1024]{1,0:T(8,128)(2,1)S(1)} %copy-done.2, bf16[64,1024]{1,0:T(8,128)(2,1)S(1)} %copy-done.3, ...), custom_call_target="tpu_custom_call" | custom-call | flops 1879048192 | bytes 2097152 | tf_op jit(solution)/shard_map/pallas_call | solution.py:114
  60.0 0.0 collective-permute-done.16
  60.0 0.0 copy-start
  60.0 1.6 %copy-done = f32[8,128,512]{2,1,0:T(8,128)S(1)} copy-done((f32[8,128,512]{2,1,0:T(8,128)S(1)}, f32[8,128,512]{2,1,0:T(8,128)}, u32[]{:S(2)}) %copy-start) | copy-done | bytes 2097176
  61.6 4.6 %shard_map.47 = bf16[64,8192]{1,0:T(8,128)(2,1)} custom-call(s32[1]{0:T(128)} %bitcast.refs_0_, s32[8]{0:T(128)S(1)} %copy-done.4, bf16[64,8192]{1,0:T(8,128)(2,1)S(1)} %copy-done.1, bf16[64,1024]{1,0:T(8,128)(2,1)S(1)} %collective-permute-done.3.refs_3_, bf16[64,1024]{1,0:T(8,128)(2,1)S(1)} %collective-permute-done.7.refs_4_, ...), custom_call_target="tpu_custom_call" | custom-call | flops 536870912 | bytes 2097152 | tf_op jit(solution)/shard_map/pallas_call | solution.py:114
  (9 shorter events, 0.3 us)
Async XLA Ops:
  0.0 6.7 %collective-permute-start.8 = (bf16[64,1024]{1,0:T(8,128)(2,1)}, bf16[64,1024]{1,0:T(8,128)(2,1)S(1)}, u32[]{:S(2)}, u32[]{:S(2)}) collective-permute-start(bf16[64,1024]{1,0:T(8,128)(2,1)} %refs_3_.1), channel_id=1, source_target_pairs={{0,64},{4,68},{8,72},{12,76},{16,80},{20,84},{24,88},{28,92},{32,9... | collective-permute-start | bytes 393224 | tf_op jit(solution)/shard_map/ppermute | solution.py:130
  2.1 15.4 %collective-permute-start.12 = (bf16[64,1024]{1,0:T(8,128)(2,1)}, bf16[64,1024]{1,0:T(8,128)(2,1)S(1)}, u32[]{:S(2)}, u32[]{:S(2)}) collective-permute-start(bf16[64,1024]{1,0:T(8,128)(2,1)} %refs_4_.1), channel_id=1, source_target_pairs={{0,64},{4,68},{8,72},{12,76},{16,80},{20,84},{24,88},{28,92},{32,9... | collective-permute-start | bytes 393224 | tf_op jit(solution)/shard_map/ppermute | solution.py:130
  3.4 14.8 %collective-permute-start = (bf16[64,1024]{1,0:T(8,128)(2,1)}, bf16[64,1024]{1,0:T(8,128)(2,1)S(1)}, u32[]{:S(2)}, u32[]{:S(2)}) collective-permute-start(bf16[64,1024]{1,0:T(8,128)(2,1)} %refs_3_.1), channel_id=1, source_target_pairs={{0,8},{4,12},{8,16},{12,20},{16,24},{20,28},{24,32},{28,36},{32,40... | collective-permute-start | bytes 393224 | tf_op jit(solution)/shard_map/ppermute | solution.py:130
  5.1 13.9 %collective-permute-start.4 = (bf16[64,1024]{1,0:T(8,128)(2,1)}, bf16[64,1024]{1,0:T(8,128)(2,1)S(1)}, u32[]{:S(2)}, u32[]{:S(2)}) collective-permute-start(bf16[64,1024]{1,0:T(8,128)(2,1)} %refs_4_.1), channel_id=1, source_target_pairs={{0,8},{4,12},{8,16},{12,20},{16,24},{20,28},{24,32},{28,36},{32,40... | collective-permute-start | bytes 393224 | tf_op jit(solution)/shard_map/ppermute | solution.py:130
  6.7 12.4 %collective-permute-start.9 = (bf16[64,1024]{1,0:T(8,128)(2,1)S(1)}, bf16[64,1024]{1,0:T(8,128)(2,1)S(1)}, u32[]{:S(2)}, u32[]{:S(2)}) collective-permute-start(bf16[64,1024]{1,0:T(8,128)(2,1)S(1)} %collective-permute-done.8.refs_9_), channel_id=1, source_target_pairs={{0,248},{4,252},{8,0},{12,4},{16,8},{20,12},{24,16},{28,20},{32,24... | collective-permute-start | bytes 393224 | tf_op jit(solution)/shard_map/ppermute | solution.py:130
  14.4 19.5 %collective-permute-start.17 = (bf16[128,1024]{1,0:T(8,128)(2,1)S(1)}, bf16[128,1024]{1,0:T(8,128)(2,1)S(1)}, u32[]{:S(2)}, u32[]{:S(2)}) collective-permute-start(bf16[128,1024]{1,0:T(8,128)(2,1)S(1)} %pad_maximum_fusion.4), channel_id=1, source_target_pairs={{0,4},{4,0},{8,12},{12,8},{16,20},{20,16},{24,28},{28,24},{32,36},... | collective-permute-start | bytes 786440 | tf_op jit(solution)/shard_map/ppermute | solution.py:134
  17.5 6.3 %collective-permute-start.13 = (bf16[64,1024]{1,0:T(8,128)(2,1)S(1)}, bf16[64,1024]{1,0:T(8,128)(2,1)S(1)}, u32[]{:S(2)}, u32[]{:S(2)}) collective-permute-start(bf16[64,1024]{1,0:T(8,128)(2,1)S(1)} %collective-permute-done.12.refs_10_), channel_id=1, source_target_pairs={{0,248},{4,252},{8,0},{12,4},{16,8},{20,12},{24,16},{28,20},{32,24... | collective-permute-start | bytes 393224 | tf_op jit(solution)/shard_map/ppermute | solution.py:130
  18.2 8.4 %collective-permute-start.1 = (bf16[64,1024]{1,0:T(8,128)(2,1)S(1)}, bf16[64,1024]{1,0:T(8,128)(2,1)S(1)}, u32[]{:S(2)}, u32[]{:S(2)}) collective-permute-start(bf16[64,1024]{1,0:T(8,128)(2,1)S(1)} %collective-permute-done.refs_7_), channel_id=1, source_target_pairs={{0,8},{4,12},{8,16},{12,20},{16,24},{20,28},{24,32},{28,36},{32,40... | collective-permute-start | bytes 393224 | tf_op jit(solution)/shard_map/ppermute | solution.py:130
  19.0 10.1 %collective-permute-start.5 = (bf16[64,1024]{1,0:T(8,128)(2,1)S(1)}, bf16[64,1024]{1,0:T(8,128)(2,1)S(1)}, u32[]{:S(2)}, u32[]{:S(2)}) collective-permute-start(bf16[64,1024]{1,0:T(8,128)(2,1)S(1)} %collective-permute-done.4.refs_8_), channel_id=1, source_target_pairs={{0,8},{4,12},{8,16},{12,20},{16,24},{20,28},{24,32},{28,36},{32,40... | collective-permute-start | bytes 393224 | tf_op jit(solution)/shard_map/ppermute | solution.py:130
  19.1 10.0 %collective-permute-start.10 = (bf16[64,1024]{1,0:T(8,128)(2,1)S(1)}, bf16[64,1024]{1,0:T(8,128)(2,1)S(1)}, u32[]{:S(2)}, u32[]{:S(2)}) collective-permute-start(bf16[64,1024]{1,0:T(8,128)(2,1)S(1)} %collective-permute-done.9.refs_17_), channel_id=1, source_target_pairs={{0,248},{4,252},{8,0},{12,4},{16,8},{20,12},{24,16},{28,20},{32,24... | collective-permute-start | bytes 393224 | tf_op jit(solution)/shard_map/ppermute | solution.py:130
  23.8 12.0 %collective-permute-start.14 = (bf16[64,1024]{1,0:T(8,128)(2,1)S(1)}, bf16[64,1024]{1,0:T(8,128)(2,1)S(1)}, u32[]{:S(2)}, u32[]{:S(2)}) collective-permute-start(bf16[64,1024]{1,0:T(8,128)(2,1)S(1)} %collective-permute-done.13.refs_18_), channel_id=1, source_target_pairs={{0,248},{4,252},{8,0},{12,4},{16,8},{20,12},{24,16},{28,20},{32,24... | collective-permute-start | bytes 393224 | tf_op jit(solution)/shard_map/ppermute | solution.py:130
  26.6 9.3 %collective-permute-start.2 = (bf16[64,1024]{1,0:T(8,128)(2,1)S(1)}, bf16[64,1024]{1,0:T(8,128)(2,1)S(1)}, u32[]{:S(2)}, u32[]{:S(2)}) collective-permute-start(bf16[64,1024]{1,0:T(8,128)(2,1)S(1)} %collective-permute-done.1.refs_15_), channel_id=1, source_target_pairs={{0,8},{4,12},{8,16},{12,20},{16,24},{20,28},{24,32},{28,36},{32,40... | collective-permute-start | bytes 393224 | tf_op jit(solution)/shard_map/ppermute | solution.py:130
  29.1 8.7 %collective-permute-start.6 = (bf16[64,1024]{1,0:T(8,128)(2,1)S(1)}, bf16[64,1024]{1,0:T(8,128)(2,1)S(1)}, u32[]{:S(2)}, u32[]{:S(2)}) collective-permute-start(bf16[64,1024]{1,0:T(8,128)(2,1)S(1)} %collective-permute-done.5.refs_16_), channel_id=1, source_target_pairs={{0,8},{4,12},{8,16},{12,20},{16,24},{20,28},{24,32},{28,36},{32,40... | collective-permute-start | bytes 393224 | tf_op jit(solution)/shard_map/ppermute | solution.py:130
  29.1 8.7 %collective-permute-start.11 = (bf16[64,1024]{1,0:T(8,128)(2,1)S(1)}, bf16[64,1024]{1,0:T(8,128)(2,1)S(1)}, u32[]{:S(2)}, u32[]{:S(2)}) collective-permute-start(bf16[64,1024]{1,0:T(8,128)(2,1)S(1)} %collective-permute-done.10.refs_25_), channel_id=1, source_target_pairs={{0,248},{4,252},{8,0},{12,4},{16,8},{20,12},{24,16},{28,20},{32,24... | collective-permute-start | bytes 393224 | tf_op jit(solution)/shard_map/ppermute | solution.py:130
  33.9 16.3 %collective-permute-start.18 = (bf16[256,1024]{1,0:T(8,128)(2,1)S(1)}, bf16[256,1024]{1,0:T(8,128)(2,1)S(1)}, u32[]{:S(2)}, u32[]{:S(2)}) collective-permute-start(bf16[256,1024]{1,0:T(8,128)(2,1)S(1)} %pad_maximum_fusion.1), channel_id=1, source_target_pairs={{0,4},{4,0},{8,12},{12,8},{16,20},{20,16},{24,28},{28,24},{32,36},... | collective-permute-start | bytes 1572872 | tf_op jit(solution)/shard_map/ppermute | solution.py:134
  35.8 14.5 %collective-permute-start.19 = (bf16[256,1024]{1,0:T(8,128)(2,1)S(1)}, bf16[256,1024]{1,0:T(8,128)(2,1)S(1)}, u32[]{:S(2)}, u32[]{:S(2)}) collective-permute-start(bf16[256,1024]{1,0:T(8,128)(2,1)S(1)} %pad_maximum_fusion.2), channel_id=1, source_target_pairs={{0,4},{4,0},{8,12},{12,8},{16,20},{20,16},{24,28},{28,24},{32,36},... | collective-permute-start | bytes 1572872 | tf_op jit(solution)/shard_map/ppermute | solution.py:134
  35.9 4.1 %collective-permute-start.15 = (bf16[64,1024]{1,0:T(8,128)(2,1)S(1)}, bf16[64,1024]{1,0:T(8,128)(2,1)S(1)}, u32[]{:S(2)}, u32[]{:S(2)}) collective-permute-start(bf16[64,1024]{1,0:T(8,128)(2,1)S(1)} %collective-permute-done.14.refs_26_), channel_id=1, source_target_pairs={{0,248},{4,252},{8,0},{12,4},{16,8},{20,12},{24,16},{28,20},{32,24... | collective-permute-start | bytes 393224 | tf_op jit(solution)/shard_map/ppermute | solution.py:130
  37.8 7.1 %collective-permute-start.3 = (bf16[64,1024]{1,0:T(8,128)(2,1)S(1)}, bf16[64,1024]{1,0:T(8,128)(2,1)S(1)}, u32[]{:S(2)}, u32[]{:S(2)}) collective-permute-start(bf16[64,1024]{1,0:T(8,128)(2,1)S(1)} %collective-permute-done.2.refs_23_), channel_id=1, source_target_pairs={{0,8},{4,12},{8,16},{12,20},{16,24},{20,28},{24,32},{28,36},{32,40... | collective-permute-start | bytes 393224 | tf_op jit(solution)/shard_map/ppermute | solution.py:130
  37.8 9.6 %collective-permute-start.7 = (bf16[64,1024]{1,0:T(8,128)(2,1)S(1)}, bf16[64,1024]{1,0:T(8,128)(2,1)S(1)}, u32[]{:S(2)}, u32[]{:S(2)}) collective-permute-start(bf16[64,1024]{1,0:T(8,128)(2,1)S(1)} %collective-permute-done.6.refs_24_), channel_id=1, source_target_pairs={{0,8},{4,12},{8,16},{12,20},{16,24},{20,28},{24,32},{28,36},{32,40... | collective-permute-start | bytes 393224 | tf_op jit(solution)/shard_map/ppermute | solution.py:130
  37.9 12.5 %copy-start.1 = (bf16[64,8192]{1,0:T(8,128)(2,1)S(1)}, bf16[64,8192]{1,0:T(8,128)(2,1)}, u32[]{:S(2)}) copy-start(bf16[64,8192]{1,0:T(8,128)(2,1)} %refs_2_.3) | copy-start | bytes 3145732
  37.9 12.5 %copy-start.2 = (bf16[64,1024]{1,0:T(8,128)(2,1)S(1)}, bf16[64,1024]{1,0:T(8,128)(2,1)}, u32[]{:S(2)}) copy-start(bf16[64,1024]{1,0:T(8,128)(2,1)} %refs_3_.1) | copy-start | bytes 393220
  37.9 12.5 %copy-start.3 = (bf16[64,1024]{1,0:T(8,128)(2,1)S(1)}, bf16[64,1024]{1,0:T(8,128)(2,1)}, u32[]{:S(2)}) copy-start(bf16[64,1024]{1,0:T(8,128)(2,1)} %refs_4_.1) | copy-start | bytes 393220
  38.0 12.4 %copy-start.4 = (s32[8]{0:T(128)S(1)}, s32[8]{0:T(128)}, u32[]{:S(2)}) copy-start(s32[8]{0:T(128)} %refs_1_.3) | copy-start | bytes 100
  40.0 10.3 %collective-permute-start.20 = (bf16[256,1024]{1,0:T(8,128)(2,1)S(1)}, bf16[256,1024]{1,0:T(8,128)(2,1)S(1)}, u32[]{:S(2)}, u32[]{:S(2)}) collective-permute-start(bf16[256,1024]{1,0:T(8,128)(2,1)S(1)} %pad_maximum_fusion.3), channel_id=1, source_target_pairs={{0,4},{4,0},{8,12},{12,8},{16,20},{20,16},{24,28},{28,24},{32,36},... | collective-permute-start | bytes 1572872 | tf_op jit(solution)/shard_map/ppermute | solution.py:134
  47.5 12.5 %collective-permute-start.16 = (bf16[256,1024]{1,0:T(8,128)(2,1)S(1)}, bf16[256,1024]{1,0:T(8,128)(2,1)S(1)}, u32[]{:S(2)}, u32[]{:S(2)}) collective-permute-start(bf16[256,1024]{1,0:T(8,128)(2,1)S(1)} %pad_maximum_fusion), channel_id=1, source_target_pairs={{0,4},{4,0},{8,12},{12,8},{16,20},{20,16},{24,28},{28,24},{32,36},... | collective-permute-start | bytes 1572872 | tf_op jit(solution)/shard_map/ppermute | solution.py:134
  60.0 1.6 %copy-start = (f32[8,128,512]{2,1,0:T(8,128)S(1)}, f32[8,128,512]{2,1,0:T(8,128)}, u32[]{:S(2)}) copy-start(f32[8,128,512]{2,1,0:T(8,128)} %get-tuple-element.10.refs_13_) | copy-start | bytes 6291460
where the time goes:
time: 66.4 us; the launch traced here: 66.3 us
  starting transfers between devices  38 us (57%)
  Pallas kernels  14.2 us (21%)
  waiting for transfers between devices  11 us (17%)
  local copies, waits for them, and re-layouts  1.77 us (3%)
  other arithmetic  1.13 us (2%)
    ppermute x16, starting transfers between devices, send(): return lax.ppermute(block, 'seq', chip_route(ahead))  27.6 us
    pallas_call x2, Pallas kernels, flash(): pl.pallas_call(functools.partial(flash_kernel, n, first, last, tuple(dist...  14.2 us
    ppermute x16, waiting for transfers between devices, send(): return lax.ppermute(block, 'seq', chip_route(ahead))  11 us
    ppermute x5, starting transfers between devices, swap(): got = lax.ppermute(jnp.concatenate(blocks, axis=0), 'seq', SIBLING)  10.4 us
    unnamed x10, local copies, waits for them, and re-layouts  1.61 us
  transfers between devices with their start and end apart: 21, of which 5 were waited for; matrix products, arithmetic and copies ran while one was open for 2% of the time, Pallas kernels for 14%

commit v1 on v0

v1 whole, which is shorter than its diff:
```python
import functools

import jax
import jax.numpy as jnp
from jax import lax
from jax.experimental import pallas as pl
from jax.experimental.pallas import tpu as pltpu
from jax.sharding import PartitionSpec as P

HK = 8
GROUP = 8
DH = 128
HQ = 64
ROWS = 64
DOCS = 8
COLS = GROUP * ROWS
WIDE = GROUP * DH
NEG = -1e30
RATE = DH ** (-0.5) * 1.4426950408889634

CHIPS = 32
NEAR = 4
FAR = 8


def chip_route(ahead):
    return [(2 * c + k, 2 * ((c + ahead) % CHIPS) + k) for c in range(CHIPS) for k in range(2)]


SIBLING = [(i, i ^ 1) for i in range(2 * CHIPS)]


def bands(docs_ref):
    lane = lax.broadcasted_iota(jnp.int32, (ROWS, DH), 1)
    low = jnp.where(lane == ROWS + DOCS, -(1 << 30), 1 << 30)
    high = jnp.where(lane == ROWS + DOCS, 0, 1 << 30)
    end = jnp.int32(0)
    for d in range(DOCS):
        begin, end = end, end + docs_ref[d]
        low = jnp.where(lane == ROWS + d, begin, low)
        high = jnp.where(lane == ROWS + d, end, high)
    return lane, low, high


def query_marks(here, docs_ref):
    lane, low, high = bands(docs_ref)
    row = lax.broadcasted_iota(jnp.int32, (ROWS, DH), 0)
    pos = here * ROWS + row
    start = jnp.zeros_like(pos)
    end = jnp.int32(0)
    for d in range(DOCS):
        end = end + docs_ref[d]
        start = jnp.where(pos >= end, end, start)
    own = (lane <= row) & (here * ROWS + lane >= start)
    other = ((pos >= low) & (pos < high)) | (lane > ROWS + DOCS)
    marks = jnp.where(lane < ROWS, jnp.where(own, 0.0, NEG), jnp.where(other, 0.0, NEG))
    return marks.astype(jnp.bfloat16)


def key_marks(here, docs_ref, places):
    lane, low, high = bands(docs_ref)
    row = lax.broadcasted_iota(jnp.int32, (ROWS, DH), 0)
    core = lax.rem(here, 2)
    marks = []
    for chips, sibling in places:
        if chips == 0 and not sibling:
            hit = lane == row
        else:
            place = here - 2 * chips
            if sibling:
                place = place + 1 - 2 * core
            if chips == 0:
                place = jnp.where(core == 0, -1, place)
            pos = place * ROWS + row
            hit = (pos >= low) & (pos < high)
        marks.append(jnp.where(hit, 1.0, 0.0).astype(jnp.bfloat16))
    return jnp.concatenate(marks, axis=0)


def flash_kernel(places, first, last, *refs):
    n = len(places)
    here_ref, docs_ref, q_ref = refs[:3]
    kv, refs = refs[3 : 3 + 2 * n], refs[3 + 2 * n :]
    if not first:
        m_in, l_in, acc_in = refs[:3]
        refs = refs[3:]
    if last:
        out_ref, staged, sems = refs
    else:
        m_out, l_out, acc_out = refs

    here = here_ref[0]
    q_marks = jnp.concatenate([query_marks(here, docs_ref)] * GROUP, axis=0)
    k_marks = key_marks(here, docs_ref, places)
    copies = []
    for h in range(HK):
        cols = slice(h * DH, (h + 1) * DH)
        wide = slice(h * WIDE, (h + 1) * WIDE)
        keys = jnp.concatenate([kv[2 * s][:, cols] for s in range(n)], axis=0)
        values = jnp.concatenate([kv[2 * s + 1][:, cols] for s in range(n)], axis=0)
        q = jnp.concatenate([q_ref[:, h * WIDE + g * DH : h * WIDE + (g + 1) * DH] for g in range(GROUP)], axis=0)
        scores = lax.dot_general(
            jnp.concatenate([keys, k_marks], axis=1),
            jnp.concatenate([q, q_marks], axis=1),
            (((1,), (1,)), ((), ())),
            preferred_element_type=jnp.float32,
        )
        top = jnp.max(scores, axis=0, keepdims=True)
        if not first:
            old = m_in[h : h + 1, :]
            top = jnp.maximum(top, old)
        weights = jnp.exp2(scores * RATE - top * RATE)
        total = jnp.sum(weights, axis=0, keepdims=True)
        part = lax.dot_general(
            values, weights.astype(jnp.bfloat16), (((0,), (0,)), ((), ())), preferred_element_type=jnp.float32
        )
        if not first:
            factor = jnp.exp2((old - top) * RATE)
            total = total + l_in[h : h + 1, :] * factor
            part = part + acc_in[h] * factor
        if last:
            result = (part / total).T.astype(jnp.bfloat16)
            for g in range(GROUP):
                staged[:, h * WIDE + g * DH : h * WIDE + (g + 1) * DH] = result[g * ROWS : (g + 1) * ROWS, :]
            copies.append(pltpu.make_async_copy(staged.at[:, wide], out_ref.at[:, wide], sems.at[h]))
            copies[-1].start()
        else:
            m_out[h : h + 1, :] = top
            l_out[h : h + 1, :] = total
            acc_out[h] = part
    for copy in copies:
        copy.wait()


def flash(here, docs, q, shards, places, state, last):
    n = len(places)
    first = state is None
    vmem = pl.BlockSpec(memory_space=pltpu.VMEM)
    smem = pl.BlockSpec(memory_space=pltpu.SMEM)
    operands = [here, docs, q] + list(shards) + ([] if first else list(state))
    if last:
        out_shape = jax.ShapeDtypeStruct((ROWS, HQ * DH), jnp.bfloat16)
        out_specs = pl.BlockSpec(memory_space=pl.ANY)
        scratch = [pltpu.VMEM((ROWS, HQ * DH), jnp.bfloat16), pltpu.SemaphoreType.DMA((HK,))]
    else:
        out_shape = (
            jax.ShapeDtypeStruct((HK, COLS), jnp.float32),
            jax.ShapeDtypeStruct((HK, COLS), jnp.float32),
            jax.ShapeDtypeStruct((HK, DH, COLS), jnp.float32),
        )
        out_specs = (vmem, vmem, vmem)
        scratch = []
    return pl.pallas_call(
        functools.partial(flash_kernel, tuple(places), first, last),
        out_shape=out_shape,
        in_specs=[smem, smem] + [vmem] * (len(operands) - 2),
        out_specs=out_specs,
        scratch_shapes=scratch,
        compiler_params=pltpu.CompilerParams(vmem_limit_bytes=16 * 1024 * 1024),
        cost_estimate=pl.CostEstimate(
            flops=4 * n * ROWS * HQ * ROWS * DH, bytes_accessed=2 << 20, transcendentals=n * ROWS * HQ * ROWS
        ),
    )(*operands)


def per_device(queries, key_heads, value_heads, doc_lengths):
    here = lax.axis_index("seq").astype(jnp.int32).reshape(1)

    def send(block, ahead):
        return lax.ppermute(block, "seq", chip_route(ahead))

    def swap(blocks):
        got = lax.ppermute(jnp.concatenate(blocks, axis=0), "seq", SIBLING)
        return [got[i * ROWS : (i + 1) * ROWS] for i in range(len(blocks))]

    own = (key_heads, value_heads)
    near, far = own, own
    shards = list(own)
    places = [0]
    for step in range(NEAR):
        near = tuple(send(x, 1) for x in near)
        far = tuple(send(x, FAR if step == 0 else -1) for x in far)
        if step < NEAR - 1:
            shards += list(near + far)
            places += [step + 1, FAR - step]
    both = near + far
    both_at = [NEAR, FAR - NEAR + 1]

    def at(chips, sibling):
        return [(c, sibling) for c in chips]

    state = flash(here, doc_lengths, queries, shards, at(places, False), None, False)
    state = flash(here, doc_lengths, queries, swap(shards), at(places, True), state, False)
    both, state = lax.optimization_barrier((both, state))
    return flash(
        here, doc_lengths, queries, list(both) + swap(both), at(both_at, False) + at(both_at, True), state, True
    )


def solution(mesh):
    return jax.shard_map(
        per_device,
        mesh=mesh,
        in_specs=(
            P(("grp", "seq"), None),
            P(("grp", "seq"), None),
            P(("grp", "seq"), None),
            P("grp"),
        ),
        out_specs=P(("grp", "seq"), None),
        check_vma=False,
    )
```

time: 66.4 us -> 70 us (1.054)
  local copies, waits for them, and re-layouts: 1.77 us -> 12.8 us
  starting transfers between devices: 38 us -> 32.1 us
  waiting for transfers between devices: 11 us -> 9.82 us
  other arithmetic: 1.13 us -> 0.04 us
  Pallas kernels: 14.2 us -> 14.9 us
    unnamed x10 -> x21, local copies, waits for them, and re-layouts: 1.61 us -> 10.4 us
    ppermute x5 -> x2, starting transfers between devices: 10.4 us -> 5.36 us  [swap(): got = lax.ppermute(jnp.concatenate(blocks, axis=0), 'seq', SIBLING)]
    ppermute x16, waiting for transfers between devices: 11 us -> 8.28 us  [send(): return lax.ppermute(block, 'seq', chip_route(ahead))]
    slice x5 -> x2, local copies, waits for them, and re-layouts: 0.16 us -> 1.71 us  [swap(): return [got[i * ROWS:(i + 1) * ROWS] for i in range(len(blocks))]]
    ppermute x5 -> x2, waiting for transfers between devices: 0.01 us -> 1.54 us  [swap(): got = lax.ppermute(jnp.concatenate(blocks, axis=0), 'seq', SIBLING)]
    concatenate x5 -> x1, other arithmetic: 1.13 us -> 0.04 us  [swap(): got = lax.ppermute(jnp.concatenate(blocks, axis=0), 'seq', SIBLING)]
    ppermute x16, starting transfers between devices: 27.6 us -> 26.7 us  [send(): return lax.ppermute(block, 'seq', chip_route(ahead))]
    pallas_call x2 -> x3, Pallas kernels: 14.2 us -> 14.9 us  [flash(): pl.pallas_call(functools.partial(flash_kernel, tuple(places), first, last...]
  transfers between devices with their start and end apart: 21 -> 18, of which waited for: 5 -> 3; matrix products, arithmetic and copies ran while one was open for 2% -> 17% of each run, Pallas kernels for 14% -> 15%
where the time goes in v1:
time: 70 us; the launch traced here: 69.8 us
  starting transfers between devices  32.1 us (46%)
  Pallas kernels  14.9 us (21%)
  local copies, waits for them, and re-layouts  12.8 us (18%)
  waiting for transfers between devices  9.82 us (14%)
    ppermute x16, starting transfers between devices, send(): return lax.ppermute(block, 'seq', chip_route(ahead))  26.7 us
    pallas_call x3, Pallas kernels, flash(): pl.pallas_call(functools.partial(flash_kernel, tuple(places), first, last...  14.9 us
    unnamed x21, local copies, waits for them, and re-layouts  10.4 us
    ppermute x16, waiting for transfers between devices, send(): return lax.ppermute(block, 'seq', chip_route(ahead))  8.28 us
    ppermute x2, starting transfers between devices, swap(): got = lax.ppermute(jnp.concatenate(blocks, axis=0), 'seq', SIBLING)  5.36 us
    slice x2, local copies, waits for them, and re-layouts, swap(): return [got[i * ROWS:(i + 1) * ROWS] for i in range(len(blocks))]  1.71 us
    ppermute x2, waiting for transfers between devices, swap(): got = lax.ppermute(jnp.concatenate(blocks, axis=0), 'seq', SIBLING)  1.54 us
  transfers between devices with their start and end apart: 18, of which 3 were waited for; matrix products, arithmetic and copies ran while one was open for 17% of the time, Pallas kernels for 15%

profile of v1, /device:TPU:1, one launch (start us, length us, event | category | flops | bytes accessed | tf_op | source)
XLA Modules:
  0.0 69.8 jit_solution(4634415562928496106)
XLA Ops:
  0.0 0.0 copy-start.1
  0.0 0.0 copy-start.2
  0.0 0.0 copy-start.3
  0.0 0.0 copy-start
  0.0 2.2 %collective-permute-start.8 = (bf16[64,1024]{1,0:T(8,128)(2,1)}, bf16[64,1024]{1,0:T(8,128)(2,1)S(1)}, u32[]{:S(2)}, u32[]{:S(2)}) collective-permute-start(bf16[64,1024]{1,0:T(8,128)(2,1)} %refs_3_.1), channel_id=1, source_target_pairs={{0,64},{4,68},{8,72},{12,76},{16,80},{20,84},{24,88},{28,92},{32,9... | collective-permute-start | bytes 393224 | tf_op jit(solution)/shard_map/ppermute | solution.py:170
  2.2 1.6 %collective-permute-start = (bf16[64,1024]{1,0:T(8,128)(2,1)}, bf16[64,1024]{1,0:T(8,128)(2,1)S(1)}, u32[]{:S(2)}, u32[]{:S(2)}) collective-permute-start(bf16[64,1024]{1,0:T(8,128)(2,1)} %refs_3_.1), channel_id=1, source_target_pairs={{0,8},{4,12},{8,16},{12,20},{16,24},{20,28},{24,32},{28,36},{32,40... | collective-permute-start | bytes 393224 | tf_op jit(solution)/shard_map/ppermute | solution.py:170
  3.9 1.3 %collective-permute-start.12 = (bf16[64,1024]{1,0:T(8,128)(2,1)}, bf16[64,1024]{1,0:T(8,128)(2,1)S(1)}, u32[]{:S(2)}, u32[]{:S(2)}) collective-permute-start(bf16[64,1024]{1,0:T(8,128)(2,1)} %refs_4_.1), channel_id=1, source_target_pairs={{0,64},{4,68},{8,72},{12,76},{16,80},{20,84},{24,88},{28,92},{32,9... | collective-permute-start | bytes 393224 | tf_op jit(solution)/shard_map/ppermute | solution.py:170
  5.2 1.6 %collective-permute-start.4 = (bf16[64,1024]{1,0:T(8,128)(2,1)}, bf16[64,1024]{1,0:T(8,128)(2,1)S(1)}, u32[]{:S(2)}, u32[]{:S(2)}) collective-permute-start(bf16[64,1024]{1,0:T(8,128)(2,1)} %refs_4_.1), channel_id=1, source_target_pairs={{0,8},{4,12},{8,16},{12,20},{16,24},{20,28},{24,32},{28,36},{32,40... | collective-permute-start | bytes 393224 | tf_op jit(solution)/shard_map/ppermute | solution.py:170
  6.8 1.6 %constant_dynamic-update-slice_fusion.13 = bf16[896,1024]{1,0:T(8,128)(2,1)} fusion(bf16[64,1024]{1,0:T(8,128)(2,1)} %refs_3_.1), kind=kLoop, calls=%fused_computation.14 | loop fusion | bytes 262144
  8.4 1.6 %constant_dynamic-update-slice_fusion.12 = bf16[896,1024]{1,0:T(8,128)(2,1)} fusion(bf16[896,1024]{1,0:T(8,128)(2,1)} %constant_dynamic-update-slice_fusion.13, bf16[64,1024]{1,0:T(8,128)(2,1)} %refs_4_.1), kind=kLoop, calls=%fused_computation.13 | loop fusion | bytes 262144
  9.9 0.0 collective-permute-done.8.refs_7_
  9.9 3.6 %collective-permute-start.9 = (bf16[64,1024]{1,0:T(8,128)(2,1)S(1)}, bf16[64,1024]{1,0:T(8,128)(2,1)S(1)}, u32[]{:S(2)}, u32[]{:S(2)}) collective-permute-start(bf16[64,1024]{1,0:T(8,128)(2,1)S(1)} %collective-permute-done.8.refs_7_), channel_id=1, source_target_pairs={{0,248},{4,252},{8,0},{12,4},{16,8},{20,12},{24,16},{28,20},{32,24... | collective-permute-start | bytes 393224 | tf_op jit(solution)/shard_map/ppermute | solution.py:170
  13.5 0.0 collective-permute-done.refs_5_
  13.5 0.0 collective-permute-start.1
  13.5 2.9 %collective-permute-done.12.refs_8_ = bf16[64,1024]{1,0:T(8,128)(2,1)S(1)} collective-permute-done((bf16[64,1024]{1,0:T(8,128)(2,1)}, bf16[64,1024]{1,0:T(8,128)(2,1)S(1)}, u32[]{:S(2)}, u32[]{:S(2)}) %collective-permute-start.12) | collective-permute-done | bytes 131104 | tf_op jit(solution)/shard_map/ppermute | solution.py:170
  16.4 1.9 %collective-permute-start.13 = (bf16[64,1024]{1,0:T(8,128)(2,1)S(1)}, bf16[64,1024]{1,0:T(8,128)(2,1)S(1)}, u32[]{:S(2)}, u32[]{:S(2)}) collective-permute-start(bf16[64,1024]{1,0:T(8,128)(2,1)S(1)} %collective-permute-done.12.refs_8_), channel_id=1, source_target_pairs={{0,248},{4,252},{8,0},{12,4},{16,8},{20,12},{24,16},{28,20},{32,24... | collective-permute-start | bytes 393224 | tf_op jit(solution)/shard_map/ppermute | solution.py:170
  18.3 0.0 collective-permute-done.4.refs_6_
  18.3 0.0 collective-permute-start.5
  18.3 0.7 constant_dynamic-update-slice_fusion.11
  19.0 0.7 constant_dynamic-update-slice_fusion.10
  19.7 0.7 constant_dynamic-update-slice_fusion.9
  20.3 0.7 constant_dynamic-update-slice_fusion.8
  21.0 0.0 collective-permute-done.9.refs_11_
  21.0 4.8 %collective-permute-start.10 = (bf16[64,1024]{1,0:T(8,128)(2,1)S(1)}, bf16[64,1024]{1,0:T(8,128)(2,1)S(1)}, u32[]{:S(2)}, u32[]{:S(2)}) collective-permute-start(bf16[64,1024]{1,0:T(8,128)(2,1)S(1)} %collective-permute-done.9.refs_11_), channel_id=1, source_target_pairs={{0,248},{4,252},{8,0},{12,4},{16,8},{20,12},{24,16},{28,20},{32,24... | collective-permute-start | bytes 393224 | tf_op jit(solution)/shard_map/ppermute | solution.py:170
  25.8 0.0 collective-permute-done.1.refs_9_
  25.8 0.0 collective-permute-start.2
  25.8 0.0 collective-permute-done.13.refs_12_
  25.8 4.8 %collective-permute-start.14 = (bf16[64,1024]{1,0:T(8,128)(2,1)S(1)}, bf16[64,1024]{1,0:T(8,128)(2,1)S(1)}, u32[]{:S(2)}, u32[]{:S(2)}) collective-permute-start(bf16[64,1024]{1,0:T(8,128)(2,1)S(1)} %collective-permute-done.13.refs_12_), channel_id=1, source_target_pairs={{0,248},{4,252},{8,0},{12,4},{16,8},{20,12},{24,16},{28,20},{32,24... | collective-permute-start | bytes 393224 | tf_op jit(solution)/shard_map/ppermute | solution.py:170
  30.6 0.0 collective-permute-done.5.refs_10_
  30.6 0.0 collective-permute-start.6
  30.6 0.7 constant_dynamic-update-slice_fusion.7
  31.2 0.7 constant_dynamic-update-slice_fusion.6
  31.9 0.7 constant_dynamic-update-slice_fusion.5
  32.5 0.7 constant_dynamic-update-slice_fusion.4
  33.2 0.0 collective-permute-done.2.refs_13_
  33.2 0.6 constant_dynamic-update-slice_fusion.3
  33.9 5.4 %collective-permute-done.6.refs_14_ = bf16[64,1024]{1,0:T(8,128)(2,1)S(1)} collective-permute-done((bf16[64,1024]{1,0:T(8,128)(2,1)S(1)}, bf16[64,1024]{1,0:T(8,128)(2,1)S(1)}, u32[]{:S(2)}, u32[]{:S(2)}) %collective-permute-start.6) | collective-permute-done | bytes 131104 | tf_op jit(solution)/shard_map/ppermute | solution.py:170
  39.2 0.6 constant_dynamic-update-slice_fusion.2
  39.9 0.0 collective-permute-done.10.refs_15_
  39.9 0.7 constant_dynamic-update-slice_fusion.1
  40.5 0.0 collective-permute-done.14.refs_16_
  40.5 0.7 constant_dynamic-update-slice_fusion
  41.2 4.4 %collective-permute-start.16 = (bf16[896,1024]{1,0:T(8,128)(2,1)}, bf16[896,1024]{1,0:T(8,128)(2,1)}, u32[]{:S(2)}, u32[]{:S(2)}) collective-permute-start(bf16[896,1024]{1,0:T(8,128)(2,1)} %constant_dynamic-update-slice_fusion), channel_id=1, source_target_pairs={{0,4},{4,0},{8,12},{12,8},{16,20},{20,16},{24,28},{28,24},{32,36},... | collective-permute-start | bytes 5505032 | tf_op jit(solution)/shard_map/ppermute | solution.py:173
  45.6 0.1 collective-permute-start.11
  45.7 1.4 %collective-permute-start.3 = (bf16[64,1024]{1,0:T(8,128)(2,1)S(1)}, bf16[64,1024]{1,0:T(8,128)(2,1)S(1)}, u32[]{:S(2)}, u32[]{:S(2)}) collective-permute-start(bf16[64,1024]{1,0:T(8,128)(2,1)S(1)} %collective-permute-done.2.refs_13_), channel_id=1, source_target_pairs={{0,8},{4,12},{8,16},{12,20},{16,24},{20,28},{24,32},{28,36},{32,40... | collective-permute-start | bytes 393224 | tf_op jit(solution)/shard_map/ppermute | solution.py:170
  47.1 3.4 %collective-permute-start.15 = (bf16[64,1024]{1,0:T(8,128)(2,1)S(1)}, bf16[64,1024]{1,0:T(8,128)(2,1)S(1)}, u32[]{:S(2)}, u32[]{:S(2)}) collective-permute-start(bf16[64,1024]{1,0:T(8,128)(2,1)S(1)} %collective-permute-done.14.refs_16_), channel_id=1, source_target_pairs={{0,248},{4,252},{8,0},{12,4},{16,8},{20,12},{24,16},{28,20},{32,24... | collective-permute-start | bytes 393224 | tf_op jit(solution)/shard_map/ppermute | solution.py:170
  50.5 0.0 collective-permute-start.7
  50.5 0.0 copy-done.1
  50.5 0.0 copy-done.2
  50.5 0.0 copy-done.3
  50.5 0.0 copy-done
  50.5 5.1 %shard_map.46 = (f32[8,512]{1,0:T(8,128)S(1)}, f32[8,512]{1,0:T(8,128)S(1)}, f32[8,128,512]{2,1,0:T(8,128)S(1)}) custom-call(s32[1]{0:T(128)} %bitcast.refs_0_, s32[8]{0:T(128)S(1)} %copy-done.3, bf16[64,8192]{1,0:T(8,128)(2,1)S(1)} %copy-done, bf16[64,1024]{1,0:T(8,128)(2,1)S(1)} %copy-done.1, bf16[64,1024]{1,0:T(8,128)(2,1)S(1)} %copy-done.2, ...), custom_call_target="tpu_custom_call" | custom-call | flops 939524096 | bytes 2097152 | tf_op jit(solution)/shard_map/pallas_call | solution.py:153
  55.6 0.0 collective-permute-done.16
  55.6 1.7 %fusion = (bf16[64,1024]{1,0:T(8,128)(2,1)S(1)}, bf16[64,1024]{1,0:T(8,128)(2,1)S(1)}, bf16[64,1024]{1,0:T(8,128)(2,1)S(1)}, bf16[64,1024]{1,0:T(8,128)(2,1)S(1)...) fusion(bf16[896,1024]{1,0:T(8,128)(2,1)} %collective-permute-do, ...), kind=kLoop, calls=%fused_computation.15 | loop fusion | bytes 3670016 | tf_op jit(solution)/shard_map/slice | solution.py:174
  57.3 5.1 %shard_map.47 = (f32[8,512]{1,0:T(8,128)S(1)}, f32[8,512]{1,0:T(8,128)S(1)}, f32[8,128,512]{2,1,0:T(8,128)S(1)}) custom-call(s32[1]{0:T(128)} %bitcast.refs_0_, s32[8]{0:T(128)S(1)} %copy-done.3, bf16[64,8192]{1,0:T(8,128)(2,1)S(1)} %copy-done, bf16[64,1024]{1,0:T(8,128)(2,1)S(1)} %get-tuple-element.44.refs_3_, ...), custom_call_target="tpu_custom_call" | custom-call | flops 939524096 | bytes 2097152 | tf_op jit(solution)/shard_map/pallas_call | solution.py:153
  62.4 0.0 collective-permute-done.11.refs_5_
  62.4 0.0 collective-permute-done.3.refs_3_
  62.4 0.0 collective-permute-done.15.refs_6_
  62.4 0.0 collective-permute-done.7.refs_4_
  62.5 0.9 %collective-permute-start.17 = (bf16[256,1024]{1,0:T(8,128)(2,1)S(1)}, bf16[256,1024]{1,0:T(8,128)(2,1)S(1)}, u32[]{:S(2)}, u32[]{:S(2)}) collective-permute-start(bf16[256,1024]{1,0:T(8,128)(2,1)S(1)} %pad_maximum_fusion), channel_id=1, source_target_pairs={{0,4},{4,0},{8,12},{12,8},{16,20},{20,16},{24,28},{28,24},{32,36},... | collective-permute-start | bytes 1572872 | tf_op jit(solution)/shard_map/ppermute | solution.py:173
  63.4 1.5 %collective-permute-done.17 = bf16[256,1024]{1,0:T(8,128)(2,1)S(1)} collective-permute-done((bf16[256,1024]{1,0:T(8,128)(2,1)S(1)}, bf16[256,1024]{1,0:T(8,128)(2,1)S(1)}, u32[]{:S(2)}, u32[]{:S(2)}) %collective-permute-start.17) | collective-permute-done | bytes 524320 | tf_op jit(solution)/shard_map/ppermute | solution.py:173
  65.0 4.7 %shard_map.48 = bf16[64,8192]{1,0:T(8,128)(2,1)} custom-call(s32[1]{0:T(128)} %bitcast.refs_0_, s32[8]{0:T(128)S(1)} %copy-done.3, bf16[64,8192]{1,0:T(8,128)(2,1)S(1)} %copy-done, bf16[64,1024]{1,0:T(8,128)(2,1)S(1)} %collective-permute-done.3.refs_3_, bf16[64,1024]{1,0:T(8,128)(2,1)S(1)} %collective-permute-done.7.refs_4_, ...), custom_call_target="tpu_custom_call" | custom-call | flops 536870912 | bytes 2097152 | tf_op jit(solution)/shard_map/pallas_call | solution.py:153
  (2 shorter events, 0.1 us)
Async XLA Ops:
  0.0 50.5 %copy-start.1 = (bf16[64,1024]{1,0:T(8,128)(2,1)S(1)}, bf16[64,1024]{1,0:T(8,128)(2,1)}, u32[]{:S(2)}) copy-start(bf16[64,1024]{1,0:T(8,128)(2,1)} %refs_3_.1) | copy-start | bytes 393220
  0.0 50.5 %copy-start.2 = (bf16[64,1024]{1,0:T(8,128)(2,1)S(1)}, bf16[64,1024]{1,0:T(8,128)(2,1)}, u32[]{:S(2)}) copy-start(bf16[64,1024]{1,0:T(8,128)(2,1)} %refs_4_.1) | copy-start | bytes 393220
  0.0 50.5 %copy-start.3 = (s32[8]{0:T(128)S(1)}, s32[8]{0:T(128)}, u32[]{:S(2)}) copy-start(s32[8]{0:T(128)} %refs_1_.5) | copy-start | bytes 100
  0.0 50.5 %copy-start = (bf16[64,8192]{1,0:T(8,128)(2,1)S(1)}, bf16[64,8192]{1,0:T(8,128)(2,1)}, u32[]{:S(2)}) copy-start(bf16[64,8192]{1,0:T(8,128)(2,1)} %refs_2_.5) | copy-start | bytes 3145732
  0.0 9.9 %collective-permute-start.8 = (bf16[64,1024]{1,0:T(8,128)(2,1)}, bf16[64,1024]{1,0:T(8,128)(2,1)S(1)}, u32[]{:S(2)}, u32[]{:S(2)}) collective-permute-start(bf16[64,1024]{1,0:T(8,128)(2,1)} %refs_3_.1), channel_id=1, source_target_pairs={{0,64},{4,68},{8,72},{12,76},{16,80},{20,84},{24,88},{28,92},{32,9... | collective-permute-start | bytes 393224 | tf_op jit(solution)/shard_map/ppermute | solution.py:170
  2.2 11.3 %collective-permute-start = (bf16[64,1024]{1,0:T(8,128)(2,1)}, bf16[64,1024]{1,0:T(8,128)(2,1)S(1)}, u32[]{:S(2)}, u32[]{:S(2)}) collective-permute-start(bf16[64,1024]{1,0:T(8,128)(2,1)} %refs_3_.1), channel_id=1, source_target_pairs={{0,8},{4,12},{8,16},{12,20},{16,24},{20,28},{24,32},{28,36},{32,40... | collective-permute-start | bytes 393224 | tf_op jit(solution)/shard_map/ppermute | solution.py:170
  3.9 12.6 %collective-permute-start.12 = (bf16[64,1024]{1,0:T(8,128)(2,1)}, bf16[64,1024]{1,0:T(8,128)(2,1)S(1)}, u32[]{:S(2)}, u32[]{:S(2)}) collective-permute-start(bf16[64,1024]{1,0:T(8,128)(2,1)} %refs_4_.1), channel_id=1, source_target_pairs={{0,64},{4,68},{8,72},{12,76},{16,80},{20,84},{24,88},{28,92},{32,9... | collective-permute-start | bytes 393224 | tf_op jit(solution)/shard_map/ppermute | solution.py:170
  5.2 13.2 %collective-permute-start.4 = (bf16[64,1024]{1,0:T(8,128)(2,1)}, bf16[64,1024]{1,0:T(8,128)(2,1)S(1)}, u32[]{:S(2)}, u32[]{:S(2)}) collective-permute-start(bf16[64,1024]{1,0:T(8,128)(2,1)} %refs_4_.1), channel_id=1, source_target_pairs={{0,8},{4,12},{8,16},{12,20},{16,24},{20,28},{24,32},{28,36},{32,40... | collective-permute-start | bytes 393224 | tf_op jit(solution)/shard_map/ppermute | solution.py:170
  9.9 11.1 %collective-permute-start.9 = (bf16[64,1024]{1,0:T(8,128)(2,1)S(1)}, bf16[64,1024]{1,0:T(8,128)(2,1)S(1)}, u32[]{:S(2)}, u32[]{:S(2)}) collective-permute-start(bf16[64,1024]{1,0:T(8,128)(2,1)S(1)} %collective-permute-done.8.refs_7_), channel_id=1, source_target_pairs={{0,248},{4,252},{8,0},{12,4},{16,8},{20,12},{24,16},{28,20},{32,24... | collective-permute-start | bytes 393224 | tf_op jit(solution)/shard_map/ppermute | solution.py:170
  13.5 12.2 %collective-permute-start.1 = (bf16[64,1024]{1,0:T(8,128)(2,1)S(1)}, bf16[64,1024]{1,0:T(8,128)(2,1)S(1)}, u32[]{:S(2)}, u32[]{:S(2)}) collective-permute-start(bf16[64,1024]{1,0:T(8,128)(2,1)S(1)} %collective-permute-done.refs_5_), channel_id=1, source_target_pairs={{0,8},{4,12},{8,16},{12,20},{16,24},{20,28},{24,32},{28,36},{32,40... | collective-permute-start | bytes 393224 | tf_op jit(solution)/shard_map/ppermute | solution.py:170
  16.4 9.4 %collective-permute-start.13 = (bf16[64,1024]{1,0:T(8,128)(2,1)S(1)}, bf16[64,1024]{1,0:T(8,128)(2,1)S(1)}, u32[]{:S(2)}, u32[]{:S(2)}) collective-permute-start(bf16[64,1024]{1,0:T(8,128)(2,1)S(1)} %collective-permute-done.12.refs_8_), channel_id=1, source_target_pairs={{0,248},{4,252},{8,0},{12,4},{16,8},{20,12},{24,16},{28,20},{32,24... | collective-permute-start | bytes 393224 | tf_op jit(solution)/shard_map/ppermute | solution.py:170
  18.3 12.2 %collective-permute-start.5 = (bf16[64,1024]{1,0:T(8,128)(2,1)S(1)}, bf16[64,1024]{1,0:T(8,128)(2,1)S(1)}, u32[]{:S(2)}, u32[]{:S(2)}) collective-permute-start(bf16[64,1024]{1,0:T(8,128)(2,1)S(1)} %collective-permute-done.4.refs_6_), channel_id=1, source_target_pairs={{0,8},{4,12},{8,16},{12,20},{16,24},{20,28},{24,32},{28,36},{32,40... | collective-permute-start | bytes 393224 | tf_op jit(solution)/shard_map/ppermute | solution.py:170
  21.0 18.9 %collective-permute-start.10 = (bf16[64,1024]{1,0:T(8,128)(2,1)S(1)}, bf16[64,1024]{1,0:T(8,128)(2,1)S(1)}, u32[]{:S(2)}, u32[]{:S(2)}) collective-permute-start(bf16[64,1024]{1,0:T(8,128)(2,1)S(1)} %collective-permute-done.9.refs_11_), channel_id=1, source_target_pairs={{0,248},{4,252},{8,0},{12,4},{16,8},{20,12},{24,16},{28,20},{32,24... | collective-permute-start | bytes 393224 | tf_op jit(solution)/shard_map/ppermute | solution.py:170
  25.8 7.5 %collective-permute-start.2 = (bf16[64,1024]{1,0:T(8,128)(2,1)S(1)}, bf16[64,1024]{1,0:T(8,128)(2,1)S(1)}, u32[]{:S(2)}, u32[]{:S(2)}) collective-permute-start(bf16[64,1024]{1,0:T(8,128)(2,1)S(1)} %collective-permute-done.1.refs_9_), channel_id=1, source_target_pairs={{0,8},{4,12},{8,16},{12,20},{16,24},{20,28},{24,32},{28,36},{32,40... | collective-permute-start | bytes 393224 | tf_op jit(solution)/shard_map/ppermute | solution.py:170
  25.8 14.8 %collective-permute-start.14 = (bf16[64,1024]{1,0:T(8,128)(2,1)S(1)}, bf16[64,1024]{1,0:T(8,128)(2,1)S(1)}, u32[]{:S(2)}, u32[]{:S(2)}) collective-permute-start(bf16[64,1024]{1,0:T(8,128)(2,1)S(1)} %collective-permute-done.13.refs_12_), channel_id=1, source_target_pairs={{0,248},{4,252},{8,0},{12,4},{16,8},{20,12},{24,16},{28,20},{32,24... | collective-permute-start | bytes 393224 | tf_op jit(solution)/shard_map/ppermute | solution.py:170
  30.6 8.7 %collective-permute-start.6 = (bf16[64,1024]{1,0:T(8,128)(2,1)S(1)}, bf16[64,1024]{1,0:T(8,128)(2,1)S(1)}, u32[]{:S(2)}, u32[]{:S(2)}) collective-permute-start(bf16[64,1024]{1,0:T(8,128)(2,1)S(1)} %collective-permute-done.5.refs_10_), channel_id=1, source_target_pairs={{0,8},{4,12},{8,16},{12,20},{16,24},{20,28},{24,32},{28,36},{32,40... | collective-permute-start | bytes 393224 | tf_op jit(solution)/shard_map/ppermute | solution.py:170
  41.2 14.4 %collective-permute-start.16 = (bf16[896,1024]{1,0:T(8,128)(2,1)}, bf16[896,1024]{1,0:T(8,128)(2,1)}, u32[]{:S(2)}, u32[]{:S(2)}) collective-permute-start(bf16[896,1024]{1,0:T(8,128)(2,1)} %constant_dynamic-update-slice_fusion), channel_id=1, source_target_pairs={{0,4},{4,0},{8,12},{12,8},{16,20},{20,16},{24,28},{28,24},{32,36},... | collective-permute-start | bytes 5505032 | tf_op jit(solution)/shard_map/ppermute | solution.py:173
  45.6 16.8 %collective-permute-start.11 = (bf16[64,1024]{1,0:T(8,128)(2,1)S(1)}, bf16[64,1024]{1,0:T(8,128)(2,1)S(1)}, u32[]{:S(2)}, u32[]{:S(2)}) collective-permute-start(bf16[64,1024]{1,0:T(8,128)(2,1)S(1)} %collective-permute-done.10.refs_15_), channel_id=1, source_target_pairs={{0,248},{4,252},{8,0},{12,4},{16,8},{20,12},{24,16},{28,20},{32,24... | collective-permute-start | bytes 393224 | tf_op jit(solution)/shard_map/ppermute | solution.py:170
  45.7 16.7 %collective-permute-start.3 = (bf16[64,1024]{1,0:T(8,128)(2,1)S(1)}, bf16[64,1024]{1,0:T(8,128)(2,1)S(1)}, u32[]{:S(2)}, u32[]{:S(2)}) collective-permute-start(bf16[64,1024]{1,0:T(8,128)(2,1)S(1)} %collective-permute-done.2.refs_13_), channel_id=1, source_target_pairs={{0,8},{4,12},{8,16},{12,20},{16,24},{20,28},{24,32},{28,36},{32,40... | collective-permute-start | bytes 393224 | tf_op jit(solution)/shard_map/ppermute | solution.py:170
  47.1 15.3 %collective-permute-start.15 = (bf16[64,1024]{1,0:T(8,128)(2,1)S(1)}, bf16[64,1024]{1,0:T(8,128)(2,1)S(1)}, u32[]{:S(2)}, u32[]{:S(2)}) collective-permute-start(bf16[64,1024]{1,0:T(8,128)(2,1)S(1)} %collective-permute-done.14.refs_16_), channel_id=1, source_target_pairs={{0,248},{4,252},{8,0},{12,4},{16,8},{20,12},{24,16},{28,20},{32,24... | collective-permute-start | bytes 393224 | tf_op jit(solution)/shard_map/ppermute | solution.py:170
  50.5 11.9 %collective-permute-start.7 = (bf16[64,1024]{1,0:T(8,128)(2,1)S(1)}, bf16[64,1024]{1,0:T(8,128)(2,1)S(1)}, u32[]{:S(2)}, u32[]{:S(2)}) collective-permute-start(bf16[64,1024]{1,0:T(8,128)(2,1)S(1)} %collective-permute-done.6.refs_14_), channel_id=1, source_target_pairs={{0,8},{4,12},{8,16},{12,20},{16,24},{20,28},{24,32},{28,36},{32,40... | collective-permute-start | bytes 393224 | tf_op jit(solution)/shard_map/ppermute | solution.py:170
  62.5 2.5 %collective-permute-start.17 = (bf16[256,1024]{1,0:T(8,128)(2,1)S(1)}, bf16[256,1024]{1,0:T(8,128)(2,1)S(1)}, u32[]{:S(2)}, u32[]{:S(2)}) collective-permute-start(bf16[256,1024]{1,0:T(8,128)(2,1)S(1)} %pad_maximum_fusion), channel_id=1, source_target_pairs={{0,4},{4,0},{8,12},{12,8},{16,20},{20,16},{24,28},{28,24},{32,36},... | collective-permute-start | bytes 1572872 | tf_op jit(solution)/shard_map/ppermute | solution.py:173

commit v2 on v1

--- a/solution.py
+++ b/solution.py
@@ -77,10 +77,10 @@
     return jnp.concatenate(marks, axis=0)
 
 
-def flash_kernel(places, first, last, *refs):
-    n = len(places)
+def flash_kernel(blocks, places, first, last, *refs):
+    n_kv = 1 + max(max(k[0], v[0]) for k, v in blocks)
     here_ref, docs_ref, q_ref = refs[:3]
-    kv, refs = refs[3 : 3 + 2 * n], refs[3 + 2 * n :]
+    kv, refs = refs[3 : 3 + n_kv], refs[3 + n_kv :]
     if not first:
         m_in, l_in, acc_in = refs[:3]
         refs = refs[3:]
@@ -92,30 +92,40 @@
     here = here_ref[0]
     q_marks = jnp.concatenate([query_marks(here, docs_ref)] * GROUP, axis=0)
     k_marks = key_marks(here, docs_ref, places)
+
+    def shards(which, h):
+        parts = [kv[pair[which][0]][pair[which][1] : pair[which][1] + ROWS, h * DH : (h + 1) * DH] for pair in blocks]
+        return jnp.concatenate(parts, axis=0)
+
+    scores = []
+    for h in range(HK):
+        q = jnp.concatenate([q_ref[:, h * WIDE + g * DH : h * WIDE + (g + 1) * DH] for g in range(GROUP)], axis=0)
+        scores.append(
+            lax.dot_general(
+                jnp.concatenate([shards(0, h), k_marks], axis=1),
+                jnp.concatenate([q, q_marks], axis=1),
+                (((1,), (1,)), ((), ())),
+                preferred_element_type=jnp.float32,
+            )
+        )
+    tops, totals, weights = [], [], []
+    for h in range(HK):
+        top = jnp.max(scores[h], axis=0, keepdims=True)
+        if not first:
+            top = jnp.maximum(top, m_in[h : h + 1, :])
+        weight = jnp.exp2(scores[h] * RATE - top * RATE)
+        tops.append(top)
+        totals.append(jnp.sum(weight, axis=0, keepdims=True))
+        weights.append(weight.astype(jnp.bfloat16))
     copies = []
     for h in range(HK):
-        cols = slice(h * DH, (h + 1) * DH)
         wide = slice(h * WIDE, (h + 1) * WIDE)
-        keys = jnp.concatenate([kv[2 * s][:, cols] for s in range(n)], axis=0)
-        values = jnp.concatenate([kv[2 * s + 1][:, cols] for s in range(n)], axis=0)
-        q = jnp.concatenate([q_ref[:, h * WIDE + g * DH : h * WIDE + (g + 1) * DH] for g in range(GROUP)], axis=0)
-        scores = lax.dot_general(
-            jnp.concatenate([keys, k_marks], axis=1),
-            jnp.concatenate([q, q_marks], axis=1),
-            (((1,), (1,)), ((), ())),
-            preferred_element_type=jnp.float32,
-        )
-        top = jnp.max(scores, axis=0, keepdims=True)
-        if not first:
-            old = m_in[h : h + 1, :]
-            top = jnp.maximum(top, old)
-        weights = jnp.exp2(scores * RATE - top * RATE)
-        total = jnp.sum(weights, axis=0, keepdims=True)
+        total = totals[h]
         part = lax.dot_general(
-            values, weights.astype(jnp.bfloat16), (((0,), (0,)), ((), ())), preferred_element_type=jnp.float32
+            shards(1, h), weights[h], (((0,), (0,)), ((), ())), preferred_element_type=jnp.float32
         )
         if not first:
-            factor = jnp.exp2((old - top) * RATE)
+            factor = jnp.exp2((m_in[h : h + 1, :] - tops[h]) * RATE)
             total = total + l_in[h : h + 1, :] * factor
             part = part + acc_in[h] * factor
         if last:
@@ -125,22 +135,26 @@
             copies.append(pltpu.make_async_copy(staged.at[:, wide], out_ref.at[:, wide], sems.at[h]))
             copies[-1].start()
         else:
-            m_out[h : h + 1, :] = top
+            m_out[h : h + 1, :] = tops[h]
             l_out[h : h + 1, :] = total
             acc_out[h] = part
     for copy in copies:
         copy.wait()
 
 
-def flash(here, docs, q, shards, places, state, last):
+VMEM = pl.BlockSpec(memory_space=pltpu.VMEM)
+SMEM = pl.BlockSpec(memory_space=pltpu.SMEM)
+HBM = pl.BlockSpec(memory_space=pl.ANY)
+PARAMS = pltpu.CompilerParams(vmem_limit_bytes=16 * 1024 * 1024)
+
+
+def flash(here, docs, q, arrays, blocks, places, state, last):
     n = len(places)
     first = state is None
-    vmem = pl.BlockSpec(memory_space=pltpu.VMEM)
-    smem = pl.BlockSpec(memory_space=pltpu.SMEM)
-    operands = [here, docs, q] + list(shards) + ([] if first else list(state))
+    operands = [here, docs, q] + list(arrays) + ([] if first else list(state))
     if last:
         out_shape = jax.ShapeDtypeStruct((ROWS, HQ * DH), jnp.bfloat16)
-        out_specs = pl.BlockSpec(memory_space=pl.ANY)
+        out_specs = HBM
         scratch = [pltpu.VMEM((ROWS, HQ * DH), jnp.bfloat16), pltpu.SemaphoreType.DMA((HK,))]
     else:
         out_shape = (
@@ -148,52 +162,87 @@
             jax.ShapeDtypeStruct((HK, COLS), jnp.float32),
             jax.ShapeDtypeStruct((HK, DH, COLS), jnp.float32),
         )
-        out_specs = (vmem, vmem, vmem)
+        out_specs = (VMEM, VMEM, VMEM)
         scratch = []
     return pl.pallas_call(
-        functools.partial(flash_kernel, tuple(places), first, last),
+        functools.partial(flash_kernel, tuple(blocks), tuple(places), first, last),
         out_shape=out_shape,
-        in_specs=[smem, smem] + [vmem] * (len(operands) - 2),
+        in_specs=[SMEM, SMEM] + [VMEM] * (len(operands) - 2),
         out_specs=out_specs,
         scratch_shapes=scratch,
-        compiler_params=pltpu.CompilerParams(vmem_limit_bytes=16 * 1024 * 1024),
+        compiler_params=PARAMS,
         cost_estimate=pl.CostEstimate(
-            flops=4 * n * ROWS * HQ * ROWS * DH, bytes_accessed=2 << 20, transcendentals=n * ROWS * HQ * ROWS
+            flops=4 * n * ROWS * HQ * ROWS * DH, bytes_accessed=1 << 16, transcendentals=n * ROWS * HQ * ROWS
         ),
     )(*operands)
 
 
+def pack_kernel(n, *refs):
+    out_ref = refs[-1]
+    for i in range(n):
+        out_ref[i * ROWS : (i + 1) * ROWS, :] = refs[i][...]
+
+
+def pack(blocks, after):
+    n = len(blocks)
+    return pl.pallas_call(
+        functools.partial(pack_kernel, n),
+        out_shape=jax.ShapeDtypeStruct((n * ROWS, HK * DH), jnp.bfloat16),
+        in_specs=[VMEM] * n + [HBM],
+        out_specs=VMEM,
+        compiler_params=PARAMS,
+        cost_estimate=pl.CostEstimate(flops=0, bytes_accessed=1 << 16, transcendentals=0),
+    )(*blocks, after)
+
+
+def apart(n):
+    return [((2 * s, 0), (2 * s + 1, 0)) for s in range(n)]
+
+
+def stacked(n, array=0):
+    return [((array, 2 * s * ROWS), (array, (2 * s + 1) * ROWS)) for s in range(n)]
+
+
 def per_device(queries, key_heads, value_heads, doc_lengths):
     here = lax.axis_index("seq").astype(jnp.int32).reshape(1)
 
     def send(block, ahead):
         return lax.ppermute(block, "seq", chip_route(ahead))
 
-    def swap(blocks):
-        got = lax.ppermute(jnp.concatenate(blocks, axis=0), "seq", SIBLING)
-        return [got[i * ROWS : (i + 1) * ROWS] for i in range(len(blocks))]
+    def swap(block):
+        return lax.ppermute(block, "seq", SIBLING)
 
     own = (key_heads, value_heads)
     near, far = own, own
     shards = list(own)
-    places = [0]
+    chips = [0]
     for step in range(NEAR):
         near = tuple(send(x, 1) for x in near)
         far = tuple(send(x, FAR if step == 0 else -1) for x in far)
         if step < NEAR - 1:
             shards += list(near + far)
-            places += [step + 1, FAR - step]
-    both = near + far
-    both_at = [NEAR, FAR - NEAR + 1]
+            chips += [step + 1, FAR - step]
+    end = near + far
+    end_chips = [NEAR, FAR - NEAR + 1]
 
     def at(chips, sibling):
         return [(c, sibling) for c in chips]
 
-    state = flash(here, doc_lengths, queries, shards, at(places, False), None, False)
-    state = flash(here, doc_lengths, queries, swap(shards), at(places, True), state, False)
-    both, state = lax.optimization_barrier((both, state))
+    n = len(chips)
+    other = swap(pack(shards, far[0]))
+    state = flash(here, doc_lengths, queries, shards, apart(n), at(chips, False), None, False)
+    state = flash(here, doc_lengths, queries, [other], stacked(n), at(chips, True), state, False)
+    end, state = lax.optimization_barrier((end, state))
+    other = swap(jnp.concatenate(end, axis=0))
     return flash(
-        here, doc_lengths, queries, list(both) + swap(both), at(both_at, False) + at(both_at, True), state, True
+        here,
+        doc_lengths,
+        queries,
+        list(end) + [other],
+        apart(2) + stacked(2, 4),
+        at(end_chips, False) + at(end_chips, True),
+        state,
+        True,
     )
 
 

time: 70 us -> 71.8 us (1.026)
  starting transfers between devices: 32.1 us -> 39.8 us
  Pallas kernels: 14.9 us -> 11.9 us
  local copies, waits for them, and re-layouts: 12.8 us -> 10.9 us
  waiting for transfers between devices: 9.82 us -> 8.43 us
    ppermute x16, starting transfers between devices: 26.7 us -> 35 us  [send(): return lax.ppermute(block, 'seq', chip_route(ahead))]
    pallas_call x3 -> x4, Pallas kernels: 14.9 us -> 11.9 us  [the longest x3 10.5 us: flash(): pl.pallas_call(functools.partial(flash_kernel, tuple(blocks), tuple(place...]
    slice x2 -> x0, local copies, waits for them, and re-layouts: 1.71 us -> none  [swap(): return [got[i * ROWS:(i + 1) * ROWS] for i in range(len(blocks))]]
    ppermute x16, waiting for transfers between devices: 8.28 us -> 6.81 us  [send(): return lax.ppermute(block, 'seq', chip_route(ahead))]
    unnamed x21 -> x52, local copies, waits for them, and re-layouts: 10.4 us -> 10.9 us
  transfers between devices with their start and end apart: 18 -> 18, of which waited for: 3 -> 3; matrix products, arithmetic and copies ran while one was open for 17% -> 0% of each run, Pallas kernels for 15% -> 10%
where the time goes in v2:
time: 71.8 us; the launch traced here: 71.5 us
  starting transfers between devices  39.8 us (55%)
  Pallas kernels  11.9 us (17%)
  local copies, waits for them, and re-layouts  10.9 us (15%)
  waiting for transfers between devices  8.43 us (12%)
    ppermute x16, starting transfers between devices, send(): return lax.ppermute(block, 'seq', chip_route(ahead))  35 us
    unnamed x52, local copies, waits for them, and re-layouts  10.9 us
    pallas_call x3, Pallas kernels, flash(): pl.pallas_call(functools.partial(flash_kernel, tuple(blocks), tuple(place...  10.5 us
    ppermute x16, waiting for transfers between devices, send(): return lax.ppermute(block, 'seq', chip_route(ahead))  6.81 us
    ppermute x2, starting transfers between devices, swap(): return lax.ppermute(block, 'seq', SIBLING)  4.8 us
    ppermute x2, waiting for transfers between devices, swap(): return lax.ppermute(block, 'seq', SIBLING)  1.62 us
  transfers between devices with their start and end apart: 18, of which 3 were waited for; matrix products, arithmetic and copies ran while one was open for 0% of the time, Pallas kernels for 10%

profile of v2, /device:TPU:1, one launch (start us, length us, event | category | flops | bytes accessed | tf_op | source)
XLA Modules:
  0.0 71.5 jit_solution(15255129205924412215)
XLA Ops:
  0.0 2.1 %collective-permute-start.8 = (bf16[64,1024]{1,0:T(8,128)(2,1)}, bf16[64,1024]{1,0:T(8,128)(2,1)S(1)}, u32[]{:S(2)}, u32[]{:S(2)}) collective-permute-start(bf16[64,1024]{1,0:T(8,128)(2,1)} %refs_3_.1), channel_id=1, source_target_pairs={{0,64},{4,68},{8,72},{12,76},{16,80},{20,84},{24,88},{28,92},{32,9... | collective-permute-start | bytes 393224 | tf_op jit(solution)/shard_map/ppermute | solution.py:210
  2.1 1.6 %collective-permute-start = (bf16[64,1024]{1,0:T(8,128)(2,1)}, bf16[64,1024]{1,0:T(8,128)(2,1)S(1)}, u32[]{:S(2)}, u32[]{:S(2)}) collective-permute-start(bf16[64,1024]{1,0:T(8,128)(2,1)} %refs_3_.1), channel_id=1, source_target_pairs={{0,8},{4,12},{8,16},{12,20},{16,24},{20,28},{24,32},{28,36},{32,40... | collective-permute-start | bytes 393224 | tf_op jit(solution)/shard_map/ppermute | solution.py:210
  3.8 1.3 %collective-permute-start.12 = (bf16[64,1024]{1,0:T(8,128)(2,1)}, bf16[64,1024]{1,0:T(8,128)(2,1)S(1)}, u32[]{:S(2)}, u32[]{:S(2)}) collective-permute-start(bf16[64,1024]{1,0:T(8,128)(2,1)} %refs_4_.1), channel_id=1, source_target_pairs={{0,64},{4,68},{8,72},{12,76},{16,80},{20,84},{24,88},{28,92},{32,9... | collective-permute-start | bytes 393224 | tf_op jit(solution)/shard_map/ppermute | solution.py:210
  5.1 1.6 %collective-permute-start.4 = (bf16[64,1024]{1,0:T(8,128)(2,1)}, bf16[64,1024]{1,0:T(8,128)(2,1)S(1)}, u32[]{:S(2)}, u32[]{:S(2)}) collective-permute-start(bf16[64,1024]{1,0:T(8,128)(2,1)} %refs_4_.1), channel_id=1, source_target_pairs={{0,8},{4,12},{8,16},{12,20},{16,24},{20,28},{24,32},{28,36},{32,40... | collective-permute-start | bytes 393224 | tf_op jit(solution)/shard_map/ppermute | solution.py:210
  6.7 0.0 collective-permute-done.8.refs_4_.refs_7_
  6.7 6.7 %collective-permute-start.9 = (bf16[64,1024]{1,0:T(8,128)(2,1)S(1)}, bf16[64,1024]{1,0:T(8,128)(2,1)S(1)}, u32[]{:S(2)}, u32[]{:S(2)}) collective-permute-start(bf16[64,1024]{1,0:T(8,128)(2,1)S(1)} %collective-permute-done.8.refs_4_.refs_7_), channel_id=1, source_target_pairs={{0,248},{4,252},{8,0},{12,4},{16,8},{20,12},{24,16},{28,20},{32,24... | collective-permute-start | bytes 393224 | tf_op jit(solution)/shard_map/ppermute | solution.py:210
  13.4 0.0 collective-permute-done.refs_2_.refs_5_
  13.4 0.0 collective-permute-start.1
  13.4 2.9 %collective-permute-done.12.refs_5_.refs_8_ = bf16[64,1024]{1,0:T(8,128)(2,1)S(1)} collective-permute-done((bf16[64,1024]{1,0:T(8,128)(2,1)}, bf16[64,1024]{1,0:T(8,128)(2,1)S(1)}, u32[]{:S(2)}, u32[]{:S(2)}) %collective-permute-start.12) | collective-permute-done | bytes 131104 | tf_op jit(solution)/shard_map/ppermute | solution.py:210
  16.3 1.9 %collective-permute-start.13 = (bf16[64,1024]{1,0:T(8,128)(2,1)S(1)}, bf16[64,1024]{1,0:T(8,128)(2,1)S(1)}, u32[]{:S(2)}, u32[]{:S(2)}) collective-permute-start(bf16[64,1024]{1,0:T(8,128)(2,1)S(1)} %collective-permute-done.12.refs_5_.refs_8_), channel_id=1, source_target_pairs={{0,248},{4,252},{8,0},{12,4},{16,8},{20,12},{24,16},{28,20},{32,24... | collective-permute-start | bytes 393224 | tf_op jit(solution)/shard_map/ppermute | solution.py:210
  18.2 0.0 collective-permute-done.4.refs_3_.refs_6_
  18.2 0.0 collective-permute-start.5
  18.2 0.0 collective-permute-done.9.refs_8_.refs_11_
  18.3 0.0 copy-start.9
  18.3 4.8 %collective-permute-start.10 = (bf16[64,1024]{1,0:T(8,128)(2,1)S(1)}, bf16[64,1024]{1,0:T(8,128)(2,1)S(1)}, u32[]{:S(2)}, u32[]{:S(2)}) collective-permute-start(bf16[64,1024]{1,0:T(8,128)(2,1)S(1)} %collective-permute-done.9.refs_8_.refs_11_), channel_id=1, source_target_pairs={{0,248},{4,252},{8,0},{12,4},{16,8},{20,12},{24,16},{28,20},{32,24... | collective-permute-start | bytes 393224 | tf_op jit(solution)/shard_map/ppermute | solution.py:210
  23.0 0.0 collective-permute-done.1.refs_6_.refs_9_
  23.0 0.0 collective-permute-start.2
  23.0 0.0 collective-permute-done.13.refs_9_.refs_12_
  23.1 0.0 copy-start.13
  23.1 4.8 %collective-permute-start.14 = (bf16[64,1024]{1,0:T(8,128)(2,1)S(1)}, bf16[64,1024]{1,0:T(8,128)(2,1)S(1)}, u32[]{:S(2)}, u32[]{:S(2)}) collective-permute-start(bf16[64,1024]{1,0:T(8,128)(2,1)S(1)} %collective-permute-done.13.refs_9_.refs_12_), channel_id=1, source_target_pairs={{0,248},{4,252},{8,0},{12,4},{16,8},{20,12},{24,16},{28,20},{32,24... | collective-permute-start | bytes 393224 | tf_op jit(solution)/shard_map/ppermute | solution.py:210
  27.8 0.0 collective-permute-done.5.refs_7_.refs_10_
  27.8 0.0 collective-permute-start.6
  27.8 0.0 collective-permute-done.10.refs_12_.refs_15_
  27.9 0.0 copy-start.23
  27.9 4.8 %collective-permute-start.11 = (bf16[64,1024]{1,0:T(8,128)(2,1)S(1)}, bf16[64,1024]{1,0:T(8,128)(2,1)S(1)}, u32[]{:S(2)}, u32[]{:S(2)}) collective-permute-start(bf16[64,1024]{1,0:T(8,128)(2,1)S(1)} %collective-permute-done.10.refs_12_.refs_15_), channel_id=1, source_target_pairs={{0,248},{4,252},{8,0},{12,4},{16,8},{20,12},{24,16},{28,20},{32,24... | collective-permute-start | bytes 393224 | tf_op jit(solution)/shard_map/ppermute | solution.py:210
  32.6 0.0 collective-permute-done.2.refs_10_.refs_13_
  32.6 0.0 collective-permute-done.14.refs_13_.refs_16_
  32.6 3.9 %collective-permute-done.6.refs_11_.refs_14_ = bf16[64,1024]{1,0:T(8,128)(2,1)S(1)} collective-permute-done((bf16[64,1024]{1,0:T(8,128)(2,1)S(1)}, bf16[64,1024]{1,0:T(8,128)(2,1)S(1)}, u32[]{:S(2)}, u32[]{:S(2)}) %collective-permute-start.6) | collective-permute-done | bytes 131104 | tf_op jit(solution)/shard_map/ppermute | solution.py:210
  36.5 0.0 collective-permute-done.11.refs_14_.refs_5_
  36.6 1.0 %copy-done.1 = bf16[64,1024]{1,0:T(8,128)(2,1)S(1)} copy-done((bf16[64,1024]{1,0:T(8,128)(2,1)S(1)}, bf16[64,1024]{1,0:T(8,128)(2,1)}, u32[]{:S(2)}) %copy-start.1) | copy-done | bytes 131096
  37.5 0.9 %copy-done.3 = bf16[64,1024]{1,0:T(8,128)(2,1)S(1)} copy-done((bf16[64,1024]{1,0:T(8,128)(2,1)S(1)}, bf16[64,1024]{1,0:T(8,128)(2,1)}, u32[]{:S(2)}) %copy-start.3) | copy-done | bytes 131096
  38.4 1.4 %shard_map.46 = bf16[896,1024]{1,0:T(8,128)(2,1)} custom-call(bf16[64,1024]{1,0:T(8,128)(2,1)S(1)} %copy-done.1, bf16[64,1024]{1,0:T(8,128)(2,1)S(1)} %copy-done.3, bf16[64,1024]{1,0:T(8,128)(2,1)S(1)} %collective-permute-done.refs_2_.refs_5_, bf16[64,1024]{1,0:T(8,128)(2,1)S(1)} %collective-permute-done.4.refs_3_.refs_6_, ...), custom_call_target="tpu_custom_call" | custom-call | bytes 65536 | tf_op jit(solution)/shard_map/pallas_call | solution.py:188
  39.8 4.4 %collective-permute-start.16 = (bf16[896,1024]{1,0:T(8,128)(2,1)}, bf16[896,1024]{1,0:T(8,128)(2,1)S(1)}, u32[]{:S(2)}, u32[]{:S(2)}) collective-permute-start(bf16[896,1024]{1,0:T(8,128)(2,1)} %shard_map.46), channel_id=1, source_target_pairs={{0,4},{4,0},{8,12},{12,8},{16,20},{20,16},{24,28},{28,24},{32,36},... | collective-permute-start | bytes 5505032 | tf_op jit(solution)/shard_map/ppermute | solution.py:213
  44.2 0.0 copy-done.7
  44.2 0.0 copy-done.17
  44.2 0.0 copy-done.23
  44.2 0.0 copy-done.15
  44.3 0.0 copy-done.19
  44.3 0.0 copy-done.21
  44.3 0.1 collective-permute-start.3
  44.4 5.3 %collective-permute-start.15 = (bf16[64,1024]{1,0:T(8,128)(2,1)}, bf16[64,1024]{1,0:T(8,128)(2,1)S(1)}, u32[]{:S(2)}, u32[]{:S(2)}) collective-permute-start(bf16[64,1024]{1,0:T(8,128)(2,1)} %copy-done.19), channel_id=1, source_target_pairs={{0,248},{4,252},{8,0},{12,4},{16,8},{20,12},{24,16},{28,20},{32,24... | collective-permute-start | bytes 393224 | tf_op jit(solution)/shard_map/ppermute | solution.py:210
  49.6 0.0 collective-permute-start.7
  49.7 0.0 copy-done.4
  49.7 0.0 copy-done.25
  49.7 0.0 copy-start.6
  49.7 0.9 %copy-done.6 = bf16[64,1024]{1,0:T(8,128)(2,1)S(1)} copy-done((bf16[64,1024]{1,0:T(8,128)(2,1)S(1)}, bf16[64,1024]{1,0:T(8,128)(2,1)}, u32[]{:S(2)}) %copy-start.6) | copy-done | bytes 131096
  50.6 0.9 %copy-done.8 = bf16[64,1024]{1,0:T(8,128)(2,1)S(1)} copy-done((bf16[64,1024]{1,0:T(8,128)(2,1)S(1)}, bf16[64,1024]{1,0:T(8,128)(2,1)}, u32[]{:S(2)}) %copy-start.8) | copy-done | bytes 131096
  51.5 0.9 %copy-done.10 = bf16[64,1024]{1,0:T(8,128)(2,1)S(1)} copy-done((bf16[64,1024]{1,0:T(8,128)(2,1)S(1)}, bf16[64,1024]{1,0:T(8,128)(2,1)}, u32[]{:S(2)}) %copy-start.10) | copy-done | bytes 131096
  52.4 0.9 %copy-done.12 = bf16[64,1024]{1,0:T(8,128)(2,1)S(1)} copy-done((bf16[64,1024]{1,0:T(8,128)(2,1)S(1)}, bf16[64,1024]{1,0:T(8,128)(2,1)}, u32[]{:S(2)}) %copy-start.12) | copy-done | bytes 131096
  53.3 0.9 %copy-done.14 = bf16[64,1024]{1,0:T(8,128)(2,1)S(1)} copy-done((bf16[64,1024]{1,0:T(8,128)(2,1)S(1)}, bf16[64,1024]{1,0:T(8,128)(2,1)}, u32[]{:S(2)}) %copy-start.14) | copy-done | bytes 131096
  54.2 0.9 %copy-done.16 = bf16[64,1024]{1,0:T(8,128)(2,1)S(1)} copy-done((bf16[64,1024]{1,0:T(8,128)(2,1)S(1)}, bf16[64,1024]{1,0:T(8,128)(2,1)}, u32[]{:S(2)}) %copy-start.16) | copy-done | bytes 131096
  55.1 0.9 %copy-done.18 = bf16[64,1024]{1,0:T(8,128)(2,1)S(1)} copy-done((bf16[64,1024]{1,0:T(8,128)(2,1)S(1)}, bf16[64,1024]{1,0:T(8,128)(2,1)}, u32[]{:S(2)}) %copy-start.18) | copy-done | bytes 131096
  56.0 0.9 %copy-done.20 = bf16[64,1024]{1,0:T(8,128)(2,1)S(1)} copy-done((bf16[64,1024]{1,0:T(8,128)(2,1)S(1)}, bf16[64,1024]{1,0:T(8,128)(2,1)}, u32[]{:S(2)}) %copy-start.20) | copy-done | bytes 131096
  56.9 0.9 %copy-done.22 = bf16[64,1024]{1,0:T(8,128)(2,1)S(1)} copy-done((bf16[64,1024]{1,0:T(8,128)(2,1)S(1)}, bf16[64,1024]{1,0:T(8,128)(2,1)}, u32[]{:S(2)}) %copy-start.22) | copy-done | bytes 131096
  57.8 0.9 %copy-done.24 = bf16[64,1024]{1,0:T(8,128)(2,1)S(1)} copy-done((bf16[64,1024]{1,0:T(8,128)(2,1)S(1)}, bf16[64,1024]{1,0:T(8,128)(2,1)}, u32[]{:S(2)}) %copy-start.24) | copy-done | bytes 131096
  58.7 3.5 %shard_map.47 = (f32[8,512]{1,0:T(8,128)S(1)}, f32[8,512]{1,0:T(8,128)S(1)}, f32[8,128,512]{2,1,0:T(8,128)S(1)}) custom-call(s32[1]{0:T(128)} %bitcast.refs_0_, s32[8]{0:T(128)S(1)} %copy-done.25, bf16[64,8192]{1,0:T(8,128)(2,1)S(1)} %copy-done, bf16[64,1024]{1,0:T(8,128)(2,1)S(1)} %copy-done.2, bf16[64,1024]{1,0:T(8,128)(2,1)S(1)} %copy-done.4, ...), custom_call_target="tpu_custom_call" | custom-call | flops 939524096 | bytes 65536 | tf_op jit(solution)/shard_map/pallas_call | solution.py:167
  62.2 0.0 collective-permute-done.16.refs_3_
  62.3 3.6 %shard_map.48 = (f32[8,512]{1,0:T(8,128)S(1)}, f32[8,512]{1,0:T(8,128)S(1)}, f32[8,128,512]{2,1,0:T(8,128)S(1)}) custom-call(s32[1]{0:T(128)} %bitcast.refs_0_, s32[8]{0:T(128)S(1)} %copy-done.25, bf16[64,8192]{1,0:T(8,128)(2,1)S(1)} %copy-done, bf16[896,1024]{1,0:T(8,128)(2,1)S(1)} %collective-permute-done.16.refs_3_, ...), custom_call_target="tpu_custom_call" | custom-call | flops 939524096 | bytes 65536 | tf_op jit(solution)/shard_map/pallas_call | solution.py:167
  65.8 0.0 collective-permute-done.3.refs_3_
  65.9 0.0 collective-permute-done.15.refs_6_
  65.9 0.0 collective-permute-done.7.refs_4_
  65.9 0.4 collective-permute-start.17
  66.3 1.6 %collective-permute-done.17.refs_7_ = bf16[256,1024]{1,0:T(8,128)(2,1)S(1)} collective-permute-done((bf16[256,1024]{1,0:T(8,128)(2,1)S(1)}, bf16[256,1024]{1,0:T(8,128)(2,1)S(1)}, u32[]{:S(2)}, u32[]{:S(2)}) %collective-permute-start.17) | collective-permute-done | bytes 524320 | tf_op jit(solution)/shard_map/ppermute | solution.py:213
  67.9 3.4 %shard_map.49 = bf16[64,8192]{1,0:T(8,128)(2,1)} custom-call(s32[1]{0:T(128)} %bitcast.refs_0_, s32[8]{0:T(128)S(1)} %copy-done.25, bf16[64,8192]{1,0:T(8,128)(2,1)S(1)} %copy-done, bf16[64,1024]{1,0:T(8,128)(2,1)S(1)} %collective-permute-done.3.refs_3_, bf16[64,1024]{1,0:T(8,128)(2,1)S(1)} %collective-permute-done.7.refs_4_, ...), custom_call_target="tpu_custom_call" | custom-call | flops 536870912 | bytes 65536 | tf_op jit(solution)/shard_map/pallas_call | solution.py:167
  (29 shorter events, 0.1 us)
Async XLA Ops:
  0.0 49.7 %copy-start = (bf16[64,8192]{1,0:T(8,128)(2,1)S(1)}, bf16[64,8192]{1,0:T(8,128)(2,1)}, u32[]{:S(2)}) copy-start(bf16[64,8192]{1,0:T(8,128)(2,1)} %refs_2_.5) | copy-start | bytes 3145732
  0.0 6.7 %collective-permute-start.8 = (bf16[64,1024]{1,0:T(8,128)(2,1)}, bf16[64,1024]{1,0:T(8,128)(2,1)S(1)}, u32[]{:S(2)}, u32[]{:S(2)}) collective-permute-start(bf16[64,1024]{1,0:T(8,128)(2,1)} %refs_3_.1), channel_id=1, source_target_pairs={{0,64},{4,68},{8,72},{12,76},{16,80},{20,84},{24,88},{28,92},{32,9... | collective-permute-start | bytes 393224 | tf_op jit(solution)/shard_map/ppermute | solution.py:210
  2.1 11.3 %collective-permute-start = (bf16[64,1024]{1,0:T(8,128)(2,1)}, bf16[64,1024]{1,0:T(8,128)(2,1)S(1)}, u32[]{:S(2)}, u32[]{:S(2)}) collective-permute-start(bf16[64,1024]{1,0:T(8,128)(2,1)} %refs_3_.1), channel_id=1, source_target_pairs={{0,8},{4,12},{8,16},{12,20},{16,24},{20,28},{24,32},{28,36},{32,40... | collective-permute-start | bytes 393224 | tf_op jit(solution)/shard_map/ppermute | solution.py:210
  3.8 12.6 %collective-permute-start.12 = (bf16[64,1024]{1,0:T(8,128)(2,1)}, bf16[64,1024]{1,0:T(8,128)(2,1)S(1)}, u32[]{:S(2)}, u32[]{:S(2)}) collective-permute-start(bf16[64,1024]{1,0:T(8,128)(2,1)} %refs_4_.1), channel_id=1, source_target_pairs={{0,64},{4,68},{8,72},{12,76},{16,80},{20,84},{24,88},{28,92},{32,9... | collective-permute-start | bytes 393224 | tf_op jit(solution)/shard_map/ppermute | solution.py:210
  5.1 13.2 %collective-permute-start.4 = (bf16[64,1024]{1,0:T(8,128)(2,1)}, bf16[64,1024]{1,0:T(8,128)(2,1)S(1)}, u32[]{:S(2)}, u32[]{:S(2)}) collective-permute-start(bf16[64,1024]{1,0:T(8,128)(2,1)} %refs_4_.1), channel_id=1, source_target_pairs={{0,8},{4,12},{8,16},{12,20},{16,24},{20,28},{24,32},{28,36},{32,40... | collective-permute-start | bytes 393224 | tf_op jit(solution)/shard_map/ppermute | solution.py:210
  6.7 11.5 %collective-permute-start.9 = (bf16[64,1024]{1,0:T(8,128)(2,1)S(1)}, bf16[64,1024]{1,0:T(8,128)(2,1)S(1)}, u32[]{:S(2)}, u32[]{:S(2)}) collective-permute-start(bf16[64,1024]{1,0:T(8,128)(2,1)S(1)} %collective-permute-done.8.refs_4_.refs_7_), channel_id=1, source_target_pairs={{0,248},{4,252},{8,0},{12,4},{16,8},{20,12},{24,16},{28,20},{32,24... | collective-permute-start | bytes 393224 | tf_op jit(solution)/shard_map/ppermute | solution.py:210
  13.4 9.6 %collective-permute-start.1 = (bf16[64,1024]{1,0:T(8,128)(2,1)S(1)}, bf16[64,1024]{1,0:T(8,128)(2,1)S(1)}, u32[]{:S(2)}, u32[]{:S(2)}) collective-permute-start(bf16[64,1024]{1,0:T(8,128)(2,1)S(1)} %collective-permute-done.refs_2_.refs_5_), channel_id=1, source_target_pairs={{0,8},{4,12},{8,16},{12,20},{16,24},{20,28},{24,32},{28,36},{32,40... | collective-permute-start | bytes 393224 | tf_op jit(solution)/shard_map/ppermute | solution.py:210
  16.3 23.5 %copy-start.5 = (bf16[64,1024]{1,0:T(8,128)(2,1)}, bf16[64,1024]{1,0:T(8,128)(2,1)S(1)}, u32[]{:S(2)}) copy-start(bf16[64,1024]{1,0:T(8,128)(2,1)S(1)} %collective-permute-done.12.refs_5_.refs_8_) | copy-start | bytes 393220
  16.3 6.7 %collective-permute-start.13 = (bf16[64,1024]{1,0:T(8,128)(2,1)S(1)}, bf16[64,1024]{1,0:T(8,128)(2,1)S(1)}, u32[]{:S(2)}, u32[]{:S(2)}) collective-permute-start(bf16[64,1024]{1,0:T(8,128)(2,1)S(1)} %collective-permute-done.12.refs_5_.refs_8_), channel_id=1, source_target_pairs={{0,248},{4,252},{8,0},{12,4},{16,8},{20,12},{24,16},{28,20},{32,24... | collective-permute-start | bytes 393224 | tf_op jit(solution)/shard_map/ppermute | solution.py:210
  18.2 26.0 %copy-start.7 = (bf16[64,1024]{1,0:T(8,128)(2,1)}, bf16[64,1024]{1,0:T(8,128)(2,1)S(1)}, u32[]{:S(2)}) copy-start(bf16[64,1024]{1,0:T(8,128)(2,1)S(1)} %collective-permute-done.4.refs_3_.refs_6_) | copy-start | bytes 393220
  18.2 9.6 %collective-permute-start.5 = (bf16[64,1024]{1,0:T(8,128)(2,1)S(1)}, bf16[64,1024]{1,0:T(8,128)(2,1)S(1)}, u32[]{:S(2)}, u32[]{:S(2)}) collective-permute-start(bf16[64,1024]{1,0:T(8,128)(2,1)S(1)} %collective-permute-done.4.refs_3_.refs_6_), channel_id=1, source_target_pairs={{0,8},{4,12},{8,16},{12,20},{16,24},{20,28},{24,32},{28,36},{32,40... | collective-permute-start | bytes 393224 | tf_op jit(solution)/shard_map/ppermute | solution.py:210
  18.3 26.0 %copy-start.9 = (bf16[64,1024]{1,0:T(8,128)(2,1)}, bf16[64,1024]{1,0:T(8,128)(2,1)S(1)}, u32[]{:S(2)}) copy-start(bf16[64,1024]{1,0:T(8,128)(2,1)S(1)} %collective-permute-done.9.refs_8_.refs_11_) | copy-start | bytes 393220
  18.3 9.6 %collective-permute-start.10 = (bf16[64,1024]{1,0:T(8,128)(2,1)S(1)}, bf16[64,1024]{1,0:T(8,128)(2,1)S(1)}, u32[]{:S(2)}, u32[]{:S(2)}) collective-permute-start(bf16[64,1024]{1,0:T(8,128)(2,1)S(1)} %collective-permute-done.9.refs_8_.refs_11_), channel_id=1, source_target_pairs={{0,248},{4,252},{8,0},{12,4},{16,8},{20,12},{24,16},{28,20},{32,24... | collective-permute-start | bytes 393224 | tf_op jit(solution)/shard_map/ppermute | solution.py:210
  23.0 21.2 %copy-start.11 = (bf16[64,1024]{1,0:T(8,128)(2,1)}, bf16[64,1024]{1,0:T(8,128)(2,1)S(1)}, u32[]{:S(2)}) copy-start(bf16[64,1024]{1,0:T(8,128)(2,1)S(1)} %collective-permute-done.1.refs_6_.refs_9_) | copy-start | bytes 393220
  23.0 9.6 %collective-permute-start.2 = (bf16[64,1024]{1,0:T(8,128)(2,1)S(1)}, bf16[64,1024]{1,0:T(8,128)(2,1)S(1)}, u32[]{:S(2)}, u32[]{:S(2)}) collective-permute-start(bf16[64,1024]{1,0:T(8,128)(2,1)S(1)} %collective-permute-done.1.refs_6_.refs_9_), channel_id=1, source_target_pairs={{0,8},{4,12},{8,16},{12,20},{16,24},{20,28},{24,32},{28,36},{32,40... | collective-permute-start | bytes 393224 | tf_op jit(solution)/shard_map/ppermute | solution.py:210
  23.1 21.2 %copy-start.13 = (bf16[64,1024]{1,0:T(8,128)(2,1)}, bf16[64,1024]{1,0:T(8,128)(2,1)S(1)}, u32[]{:S(2)}) copy-start(bf16[64,1024]{1,0:T(8,128)(2,1)S(1)} %collective-permute-done.13.refs_9_.refs_12_) | copy-start | bytes 393220
  23.1 9.6 %collective-permute-start.14 = (bf16[64,1024]{1,0:T(8,128)(2,1)S(1)}, bf16[64,1024]{1,0:T(8,128)(2,1)S(1)}, u32[]{:S(2)}, u32[]{:S(2)}) collective-permute-start(bf16[64,1024]{1,0:T(8,128)(2,1)S(1)} %collective-permute-done.13.refs_9_.refs_12_), channel_id=1, source_target_pairs={{0,248},{4,252},{8,0},{12,4},{16,8},{20,12},{24,16},{28,20},{32,24... | collective-permute-start | bytes 393224 | tf_op jit(solution)/shard_map/ppermute | solution.py:210
  27.8 16.4 %copy-start.17 = (bf16[64,1024]{1,0:T(8,128)(2,1)}, bf16[64,1024]{1,0:T(8,128)(2,1)S(1)}, u32[]{:S(2)}) copy-start(bf16[64,1024]{1,0:T(8,128)(2,1)S(1)} %collective-permute-done.5.refs_7_.refs_10_) | copy-start | bytes 393220
  27.8 8.7 %collective-permute-start.6 = (bf16[64,1024]{1,0:T(8,128)(2,1)S(1)}, bf16[64,1024]{1,0:T(8,128)(2,1)S(1)}, u32[]{:S(2)}, u32[]{:S(2)}) collective-permute-start(bf16[64,1024]{1,0:T(8,128)(2,1)S(1)} %collective-permute-done.5.refs_7_.refs_10_), channel_id=1, source_target_pairs={{0,8},{4,12},{8,16},{12,20},{16,24},{20,28},{24,32},{28,36},{32,40... | collective-permute-start | bytes 393224 | tf_op jit(solution)/shard_map/ppermute | solution.py:210
  27.9 16.4 %copy-start.23 = (bf16[64,1024]{1,0:T(8,128)(2,1)}, bf16[64,1024]{1,0:T(8,128)(2,1)S(1)}, u32[]{:S(2)}) copy-start(bf16[64,1024]{1,0:T(8,128)(2,1)S(1)} %collective-permute-done.10.refs_12_.refs_15_) | copy-start | bytes 393220
  27.9 8.7 %collective-permute-start.11 = (bf16[64,1024]{1,0:T(8,128)(2,1)S(1)}, bf16[64,1024]{1,0:T(8,128)(2,1)S(1)}, u32[]{:S(2)}, u32[]{:S(2)}) collective-permute-start(bf16[64,1024]{1,0:T(8,128)(2,1)S(1)} %collective-permute-done.10.refs_12_.refs_15_), channel_id=1, source_target_pairs={{0,248},{4,252},{8,0},{12,4},{16,8},{20,12},{24,16},{28,20},{32,24... | collective-permute-start | bytes 393224 | tf_op jit(solution)/shard_map/ppermute | solution.py:210
  32.6 11.6 %copy-start.15 = (bf16[64,1024]{1,0:T(8,128)(2,1)}, bf16[64,1024]{1,0:T(8,128)(2,1)S(1)}, u32[]{:S(2)}) copy-start(bf16[64,1024]{1,0:T(8,128)(2,1)S(1)} %collective-permute-done.2.refs_10_.refs_13_) | copy-start | bytes 393220
  32.6 11.6 %copy-start.19 = (bf16[64,1024]{1,0:T(8,128)(2,1)}, bf16[64,1024]{1,0:T(8,128)(2,1)S(1)}, u32[]{:S(2)}) copy-start(bf16[64,1024]{1,0:T(8,128)(2,1)S(1)} %collective-permute-done.14.refs_13_.refs_16_) | copy-start | bytes 393220
  36.5 7.7 %copy-start.21 = (bf16[64,1024]{1,0:T(8,128)(2,1)}, bf16[64,1024]{1,0:T(8,128)(2,1)S(1)}, u32[]{:S(2)}) copy-start(bf16[64,1024]{1,0:T(8,128)(2,1)S(1)} %collective-permute-done.6.refs_11_.refs_14_) | copy-start | bytes 393220
  36.6 1.0 %copy-start.1 = (bf16[64,1024]{1,0:T(8,128)(2,1)S(1)}, bf16[64,1024]{1,0:T(8,128)(2,1)}, u32[]{:S(2)}) copy-start(bf16[64,1024]{1,0:T(8,128)(2,1)} %refs_3_.1) | copy-start | bytes 393220
  37.5 0.9 %copy-start.3 = (bf16[64,1024]{1,0:T(8,128)(2,1)S(1)}, bf16[64,1024]{1,0:T(8,128)(2,1)}, u32[]{:S(2)}) copy-start(bf16[64,1024]{1,0:T(8,128)(2,1)} %refs_4_.1) | copy-start | bytes 393220
  38.4 11.2 %copy-start.2 = (bf16[64,1024]{1,0:T(8,128)(2,1)S(1)}, bf16[64,1024]{1,0:T(8,128)(2,1)}, u32[]{:S(2)}) copy-start(bf16[64,1024]{1,0:T(8,128)(2,1)} %refs_3_.1) | copy-start | bytes 393220
  38.4 11.2 %copy-start.4 = (bf16[64,1024]{1,0:T(8,128)(2,1)S(1)}, bf16[64,1024]{1,0:T(8,128)(2,1)}, u32[]{:S(2)}) copy-start(bf16[64,1024]{1,0:T(8,128)(2,1)} %refs_4_.1) | copy-start | bytes 393220
  38.4 11.3 %copy-start.25 = (s32[8]{0:T(128)S(1)}, s32[8]{0:T(128)}, u32[]{:S(2)}) copy-start(s32[8]{0:T(128)} %refs_1_.7) | copy-start | bytes 100
  39.8 22.5 %collective-permute-start.16 = (bf16[896,1024]{1,0:T(8,128)(2,1)}, bf16[896,1024]{1,0:T(8,128)(2,1)S(1)}, u32[]{:S(2)}, u32[]{:S(2)}) collective-permute-start(bf16[896,1024]{1,0:T(8,128)(2,1)} %shard_map.46), channel_id=1, source_target_pairs={{0,4},{4,0},{8,12},{12,8},{16,20},{20,16},{24,28},{28,24},{32,36},... | collective-permute-start | bytes 5505032 | tf_op jit(solution)/shard_map/ppermute | solution.py:213
  44.3 21.6 %collective-permute-start.3 = (bf16[64,1024]{1,0:T(8,128)(2,1)}, bf16[64,1024]{1,0:T(8,128)(2,1)S(1)}, u32[]{:S(2)}, u32[]{:S(2)}) collective-permute-start(bf16[64,1024]{1,0:T(8,128)(2,1)} %copy-done.15), channel_id=1, source_target_pairs={{0,8},{4,12},{8,16},{12,20},{16,24},{20,28},{24,32},{28,36},{32,40... | collective-permute-start | bytes 393224 | tf_op jit(solution)/shard_map/ppermute | solution.py:210
  44.4 21.5 %collective-permute-start.15 = (bf16[64,1024]{1,0:T(8,128)(2,1)}, bf16[64,1024]{1,0:T(8,128)(2,1)S(1)}, u32[]{:S(2)}, u32[]{:S(2)}) collective-permute-start(bf16[64,1024]{1,0:T(8,128)(2,1)} %copy-done.19), channel_id=1, source_target_pairs={{0,248},{4,252},{8,0},{12,4},{16,8},{20,12},{24,16},{28,20},{32,24... | collective-permute-start | bytes 393224 | tf_op jit(solution)/shard_map/ppermute | solution.py:210
  49.6 16.2 %collective-permute-start.7 = (bf16[64,1024]{1,0:T(8,128)(2,1)}, bf16[64,1024]{1,0:T(8,128)(2,1)S(1)}, u32[]{:S(2)}, u32[]{:S(2)}) collective-permute-start(bf16[64,1024]{1,0:T(8,128)(2,1)} %copy-done.21), channel_id=1, source_target_pairs={{0,8},{4,12},{8,16},{12,20},{16,24},{20,28},{24,32},{28,36},{32,40... | collective-permute-start | bytes 393224 | tf_op jit(solution)/shard_map/ppermute | solution.py:210
  49.7 0.9 %copy-start.6 = (bf16[64,1024]{1,0:T(8,128)(2,1)S(1)}, bf16[64,1024]{1,0:T(8,128)(2,1)}, u32[]{:S(2)}) copy-start(bf16[64,1024]{1,0:T(8,128)(2,1)} %copy-done.5) | copy-start | bytes 393220
  50.6 0.9 %copy-start.8 = (bf16[64,1024]{1,0:T(8,128)(2,1)S(1)}, bf16[64,1024]{1,0:T(8,128)(2,1)}, u32[]{:S(2)}) copy-start(bf16[64,1024]{1,0:T(8,128)(2,1)} %copy-done.7) | copy-start | bytes 393220
  51.5 0.9 %copy-start.10 = (bf16[64,1024]{1,0:T(8,128)(2,1)S(1)}, bf16[64,1024]{1,0:T(8,128)(2,1)}, u32[]{:S(2)}) copy-start(bf16[64,1024]{1,0:T(8,128)(2,1)} %copy-done.9) | copy-start | bytes 393220
  52.4 0.9 %copy-start.12 = (bf16[64,1024]{1,0:T(8,128)(2,1)S(1)}, bf16[64,1024]{1,0:T(8,128)(2,1)}, u32[]{:S(2)}) copy-start(bf16[64,1024]{1,0:T(8,128)(2,1)} %copy-done.11) | copy-start | bytes 393220
  53.3 0.9 %copy-start.14 = (bf16[64,1024]{1,0:T(8,128)(2,1)S(1)}, bf16[64,1024]{1,0:T(8,128)(2,1)}, u32[]{:S(2)}) copy-start(bf16[64,1024]{1,0:T(8,128)(2,1)} %copy-done.13) | copy-start | bytes 393220
  54.2 0.9 %copy-start.16 = (bf16[64,1024]{1,0:T(8,128)(2,1)S(1)}, bf16[64,1024]{1,0:T(8,128)(2,1)}, u32[]{:S(2)}) copy-start(bf16[64,1024]{1,0:T(8,128)(2,1)} %copy-done.15) | copy-start | bytes 393220
  55.1 0.9 %copy-start.18 = (bf16[64,1024]{1,0:T(8,128)(2,1)S(1)}, bf16[64,1024]{1,0:T(8,128)(2,1)}, u32[]{:S(2)}) copy-start(bf16[64,1024]{1,0:T(8,128)(2,1)} %copy-done.17) | copy-start | bytes 393220
  56.0 0.9 %copy-start.20 = (bf16[64,1024]{1,0:T(8,128)(2,1)S(1)}, bf16[64,1024]{1,0:T(8,128)(2,1)}, u32[]{:S(2)}) copy-start(bf16[64,1024]{1,0:T(8,128)(2,1)} %copy-done.19) | copy-start | bytes 393220
  56.9 0.9 %copy-start.22 = (bf16[64,1024]{1,0:T(8,128)(2,1)S(1)}, bf16[64,1024]{1,0:T(8,128)(2,1)}, u32[]{:S(2)}) copy-start(bf16[64,1024]{1,0:T(8,128)(2,1)} %copy-done.21) | copy-start | bytes 393220
  57.8 0.9 %copy-start.24 = (bf16[64,1024]{1,0:T(8,128)(2,1)S(1)}, bf16[64,1024]{1,0:T(8,128)(2,1)}, u32[]{:S(2)}) copy-start(bf16[64,1024]{1,0:T(8,128)(2,1)} %copy-done.23) | copy-start | bytes 393220
  65.9 2.0 %collective-permute-start.17 = (bf16[256,1024]{1,0:T(8,128)(2,1)S(1)}, bf16[256,1024]{1,0:T(8,128)(2,1)S(1)}, u32[]{:S(2)}, u32[]{:S(2)}) collective-permute-start(bf16[256,1024]{1,0:T(8,128)(2,1)S(1)} %pad_maximum_fusion), channel_id=1, source_target_pairs={{0,4},{4,0},{8,12},{12,8},{16,20},{20,16},{24,28},{28,24},{32,36},... | collective-permute-start | bytes 1572872 | tf_op jit(solution)/shard_map/ppermute | solution.py:213

commit v3 on v2

--- a/solution.py
+++ b/solution.py
@@ -77,24 +77,25 @@
     return jnp.concatenate(marks, axis=0)
 
 
-def flash_kernel(blocks, places, first, last, *refs):
-    n_kv = 1 + max(max(k[0], v[0]) for k, v in blocks)
+def flash_kernel(n, places, kind, *refs):
     here_ref, docs_ref, q_ref = refs[:3]
-    kv, refs = refs[3 : 3 + n_kv], refs[3 + n_kv :]
-    if not first:
-        m_in, l_in, acc_in = refs[:3]
-        refs = refs[3:]
-    if last:
-        out_ref, staged, sems = refs
+    if kind == "end":
+        kv, refs = refs[3:8], refs[8:]
+        m_in, l_in, acc_in, *lent, out_ref, staged, sems = refs
     else:
-        m_out, l_out, acc_out = refs
+        kv, refs = refs[3 : 3 + 2 * n], refs[3 + 2 * n :]
 
     here = here_ref[0]
     q_marks = jnp.concatenate([query_marks(here, docs_ref)] * GROUP, axis=0)
     k_marks = key_marks(here, docs_ref, places)
 
     def shards(which, h):
-        parts = [kv[pair[which][0]][pair[which][1] : pair[which][1] + ROWS, h * DH : (h + 1) * DH] for pair in blocks]
+        cols = slice(h * DH, (h + 1) * DH)
+        if kind == "end":
+            parts = [kv[which][:, cols], kv[2 + which][:, cols]]
+            parts += [kv[4][(2 * s + which) * ROWS : (2 * s + which + 1) * ROWS, cols] for s in range(2)]
+        else:
+            parts = [kv[2 * s + which][:, cols] for s in range(n)]
         return jnp.concatenate(parts, axis=0)
 
     scores = []
@@ -108,103 +109,117 @@
                 preferred_element_type=jnp.float32,
             )
         )
+    if kind == "end":
+        m_lent, l_lent = lent_stats(lent)
+        known = jnp.maximum(m_in[...], m_lent)
     tops, totals, weights = [], [], []
     for h in range(HK):
         top = jnp.max(scores[h], axis=0, keepdims=True)
-        if not first:
-            top = jnp.maximum(top, m_in[h : h + 1, :])
+        if kind == "end":
+            top = jnp.maximum(top, known[h : h + 1, :])
         weight = jnp.exp2(scores[h] * RATE - top * RATE)
         tops.append(top)
         totals.append(jnp.sum(weight, axis=0, keepdims=True))
         weights.append(weight.astype(jnp.bfloat16))
+    if kind == "lend":
+        lent = refs
+        for i in range(HALVES):
+            half = slice(i * HALF, (i + 1) * HALF)
+            pieces = in_three(jnp.concatenate(tops[half], axis=0)) + in_three(jnp.concatenate(totals[half], axis=0))
+            pieces += [jnp.zeros((STATS - 6 * HALF, COLS), jnp.float32)]
+            lent[i][HALF * DH :, :] = jnp.concatenate(pieces, axis=0).astype(jnp.bfloat16)
+    if kind == "own":
+        m_out, l_out, acc_out = refs
+        m_out[...] = jnp.concatenate(tops, axis=0)
+        l_out[...] = jnp.concatenate(totals, axis=0)
     copies = []
     for h in range(HK):
-        wide = slice(h * WIDE, (h + 1) * WIDE)
-        total = totals[h]
         part = lax.dot_general(
             shards(1, h), weights[h], (((0,), (0,)), ((), ())), preferred_element_type=jnp.float32
         )
-        if not first:
-            factor = jnp.exp2((m_in[h : h + 1, :] - tops[h]) * RATE)
-            total = total + l_in[h : h + 1, :] * factor
-            part = part + acc_in[h] * factor
-        if last:
-            result = (part / total).T.astype(jnp.bfloat16)
+        if kind == "own":
+            acc_out[h] = part
+        if kind == "lend":
+            lent[h // HALF][h % HALF * DH : (h % HALF + 1) * DH, :] = (part * (1.0 / totals[h])).astype(jnp.bfloat16)
+        if kind == "end":
+            wide = slice(h * WIDE, (h + 1) * WIDE)
+            held = jnp.exp2((m_in[h : h + 1, :] - tops[h]) * RATE)
+            got = l_lent[h : h + 1, :] * jnp.exp2((m_lent[h : h + 1, :] - tops[h]) * RATE)
+            share = 1.0 / (totals[h] + l_in[h : h + 1, :] * held + got)
+            part = part * share + acc_in[h] * (held * share)
+            part = part + lent[h // HALF][h % HALF * DH : (h % HALF + 1) * DH, :].astype(jnp.float32) * (got * share)
+            result = part.T.astype(jnp.bfloat16)
             for g in range(GROUP):
                 staged[:, h * WIDE + g * DH : h * WIDE + (g + 1) * DH] = result[g * ROWS : (g + 1) * ROWS, :]
             copies.append(pltpu.make_async_copy(staged.at[:, wide], out_ref.at[:, wide], sems.at[h]))
             copies[-1].start()
-        else:
-            m_out[h : h + 1, :] = tops[h]
-            l_out[h : h + 1, :] = total
-            acc_out[h] = part
     for copy in copies:
         copy.wait()
+
+
+HALVES = 2
+HALF = HK // HALVES
+STATS = 32
+
+
+def in_three(x):
+    pieces = []
+    for _ in range(3):
+        pieces.append(x.astype(jnp.bfloat16).astype(jnp.float32))
+        x = x - pieces[-1]
+    return pieces
+
+
+def lent_stats(lent):
+    tops, totals = [], []
+    for half in lent:
+        stats = half[HALF * DH :, :].astype(jnp.float32)
+        pieces = [stats[i * HALF : (i + 1) * HALF, :] for i in range(6)]
+        tops.append(pieces[0] + pieces[1] + pieces[2])
+        totals.append(pieces[3] + pieces[4] + pieces[5])
+    return jnp.concatenate(tops, axis=0), jnp.concatenate(totals, axis=0)
 
 
 VMEM = pl.BlockSpec(memory_space=pltpu.VMEM)
 SMEM = pl.BlockSpec(memory_space=pltpu.SMEM)
 HBM = pl.BlockSpec(memory_space=pl.ANY)
-PARAMS = pltpu.CompilerParams(vmem_limit_bytes=16 * 1024 * 1024)
-
-
-def flash(here, docs, q, arrays, blocks, places, state, last):
+
+
+def flash(kind, here, docs, q, arrays, places):
     n = len(places)
-    first = state is None
-    operands = [here, docs, q] + list(arrays) + ([] if first else list(state))
-    if last:
+    operands = [here, docs, q] + list(arrays)
+    scratch = []
+    out_specs = VMEM
+    if kind == "end":
         out_shape = jax.ShapeDtypeStruct((ROWS, HQ * DH), jnp.bfloat16)
         out_specs = HBM
         scratch = [pltpu.VMEM((ROWS, HQ * DH), jnp.bfloat16), pltpu.SemaphoreType.DMA((HK,))]
+    elif kind == "lend":
+        out_specs = (VMEM,) * HALVES
+        out_shape = (jax.ShapeDtypeStruct((HALF * DH + STATS, COLS), jnp.bfloat16),) * HALVES
     else:
+        out_specs = (VMEM, VMEM, VMEM)
         out_shape = (
             jax.ShapeDtypeStruct((HK, COLS), jnp.float32),
             jax.ShapeDtypeStruct((HK, COLS), jnp.float32),
             jax.ShapeDtypeStruct((HK, DH, COLS), jnp.float32),
         )
-        out_specs = (VMEM, VMEM, VMEM)
-        scratch = []
     return pl.pallas_call(
-        functools.partial(flash_kernel, tuple(blocks), tuple(places), first, last),
+        functools.partial(flash_kernel, n, tuple(places), kind),
         out_shape=out_shape,
         in_specs=[SMEM, SMEM] + [VMEM] * (len(operands) - 2),
         out_specs=out_specs,
         scratch_shapes=scratch,
-        compiler_params=PARAMS,
+        compiler_params=pltpu.CompilerParams(vmem_limit_bytes=16 * 1024 * 1024),
         cost_estimate=pl.CostEstimate(
             flops=4 * n * ROWS * HQ * ROWS * DH, bytes_accessed=1 << 16, transcendentals=n * ROWS * HQ * ROWS
         ),
     )(*operands)
 
 
-def pack_kernel(n, *refs):
-    out_ref = refs[-1]
-    for i in range(n):
-        out_ref[i * ROWS : (i + 1) * ROWS, :] = refs[i][...]
-
-
-def pack(blocks, after):
-    n = len(blocks)
-    return pl.pallas_call(
-        functools.partial(pack_kernel, n),
-        out_shape=jax.ShapeDtypeStruct((n * ROWS, HK * DH), jnp.bfloat16),
-        in_specs=[VMEM] * n + [HBM],
-        out_specs=VMEM,
-        compiler_params=PARAMS,
-        cost_estimate=pl.CostEstimate(flops=0, bytes_accessed=1 << 16, transcendentals=0),
-    )(*blocks, after)
-
-
-def apart(n):
-    return [((2 * s, 0), (2 * s + 1, 0)) for s in range(n)]
-
-
-def stacked(n, array=0):
-    return [((array, 2 * s * ROWS), (array, (2 * s + 1) * ROWS)) for s in range(n)]
-
-
 def per_device(queries, key_heads, value_heads, doc_lengths):
     here = lax.axis_index("seq").astype(jnp.int32).reshape(1)
+    there = here + 1 - 2 * lax.rem(here, 2)
 
     def send(block, ahead):
         return lax.ppermute(block, "seq", chip_route(ahead))
@@ -225,25 +240,13 @@
     end = near + far
     end_chips = [NEAR, FAR - NEAR + 1]
 
-    def at(chips, sibling):
-        return [(c, sibling) for c in chips]
-
-    n = len(chips)
-    other = swap(pack(shards, far[0]))
-    state = flash(here, doc_lengths, queries, shards, apart(n), at(chips, False), None, False)
-    state = flash(here, doc_lengths, queries, [other], stacked(n), at(chips, True), state, False)
-    end, state = lax.optimization_barrier((end, state))
-    other = swap(jnp.concatenate(end, axis=0))
-    return flash(
-        here,
-        doc_lengths,
-        queries,
-        list(end) + [other],
-        apart(2) + stacked(2, 4),
-        at(end_chips, False) + at(end_chips, True),
-        state,
-        True,
-    )
+    lent = flash("lend", there, doc_lengths, swap(queries), shards, [(c, True) for c in chips])
+    got = [swap(x) for x in lent]
+    state = flash("own", here, doc_lengths, queries, shards, [(c, False) for c in chips])
+    end, state, _ = lax.optimization_barrier((end, state, lent))
+    arrays = list(end) + [swap(jnp.concatenate(end, axis=0))] + list(state) + got
+    places = [(c, False) for c in end_chips] + [(c, True) for c in end_chips]
+    return flash("end", here, doc_lengths, queries, arrays, places)
 
 
 def solution(mesh):

time: 71.8 us -> 58.2 us (0.81)
  starting transfers between devices: 39.8 us -> 29.5 us
  local copies, waits for them, and re-layouts: 10.9 us -> 3.7 us
  waiting for transfers between devices: 8.43 us -> 13 us
    ppermute x16, starting transfers between devices: 35 us -> 23.3 us  [send(): return lax.ppermute(block, 'seq', chip_route(ahead))]
    unnamed x52 -> x16, local copies, waits for them, and re-layouts: 10.9 us -> 3.7 us
    ppermute x16, waiting for transfers between devices: 6.81 us -> 10.5 us  [send(): return lax.ppermute(block, 'seq', chip_route(ahead))]
    ppermute x2 -> x4, starting transfers between devices: 4.8 us -> 6.21 us  [swap(): return lax.ppermute(block, 'seq', SIBLING)]
    ppermute x2 -> x4, waiting for transfers between devices: 1.62 us -> 2.48 us  [swap(): return lax.ppermute(block, 'seq', SIBLING)]
    pallas_call x4 -> x3, Pallas kernels: 11.9 us -> 11.5 us  [flash(): pl.pallas_call(functools.partial(flash_kernel, n, tuple(places), kind), o...]
  transfers between devices with their start and end apart: 18 -> 20, of which waited for: 3 -> 5; matrix products, arithmetic and copies ran while one was open for 0% -> 0% of each run, Pallas kernels for 10% -> 13%
where the time goes in v3:
time: 58.2 us; the launch traced here: 58 us
  starting transfers between devices  29.5 us (51%)
  waiting for transfers between devices  13 us (22%)
  Pallas kernels  11.5 us (20%)
  local copies, waits for them, and re-layouts  3.7 us (6%)
    ppermute x16, starting transfers between devices, send(): return lax.ppermute(block, 'seq', chip_route(ahead))  23.3 us
    pallas_call x3, Pallas kernels, flash(): pl.pallas_call(functools.partial(flash_kernel, n, tuple(places), kind), o...  11.5 us
    ppermute x16, waiting for transfers between devices, send(): return lax.ppermute(block, 'seq', chip_route(ahead))  10.5 us
    ppermute x4, starting transfers between devices, swap(): return lax.ppermute(block, 'seq', SIBLING)  6.21 us
    unnamed x16, local copies, waits for them, and re-layouts  3.7 us
    ppermute x4, waiting for transfers between devices, swap(): return lax.ppermute(block, 'seq', SIBLING)  2.48 us
  transfers between devices with their start and end apart: 20, of which 5 were waited for; matrix products, arithmetic and copies ran while one was open for 0% of the time, Pallas kernels for 13%

profile of v3, /device:TPU:1, one launch (start us, length us, event | category | flops | bytes accessed | tf_op | source)
XLA Modules:
  0.0 58.0 jit_solution(16959861169907575064)
XLA Ops:
  0.0 0.0 copy-start.3
  0.0 3.2 %collective-permute-start.16 = (bf16[64,8192]{1,0:T(8,128)(2,1)}, bf16[64,8192]{1,0:T(8,128)(2,1)S(1)}, u32[]{:S(2)}, u32[]{:S(2)}) collective-permute-start(bf16[64,8192]{1,0:T(8,128)(2,1)} %refs_2_.3), channel_id=1, source_target_pairs={{0,4},{4,0},{8,12},{12,8},{16,20},{20,16},{24,28},{28,24},{32,36},... | collective-permute-start | bytes 3145736 | tf_op jit(solution)/shard_map/ppermute | solution.py:228
  3.2 0.0 collective-permute-start.8
  3.2 0.9 %collective-permute-start.12 = (bf16[64,1024]{1,0:T(8,128)(2,1)}, bf16[64,1024]{1,0:T(8,128)(2,1)S(1)}, u32[]{:S(2)}, u32[]{:S(2)}) collective-permute-start(bf16[64,1024]{1,0:T(8,128)(2,1)} %refs_4_.3), channel_id=1, source_target_pairs={{0,64},{4,68},{8,72},{12,76},{16,80},{20,84},{24,88},{28,92},{32,9... | collective-permute-start | bytes 393224 | tf_op jit(solution)/shard_map/ppermute | solution.py:225
  4.1 1.6 %collective-permute-start = (bf16[64,1024]{1,0:T(8,128)(2,1)}, bf16[64,1024]{1,0:T(8,128)(2,1)S(1)}, u32[]{:S(2)}, u32[]{:S(2)}) collective-permute-start(bf16[64,1024]{1,0:T(8,128)(2,1)} %refs_3_.3), channel_id=1, source_target_pairs={{0,8},{4,12},{8,16},{12,20},{16,24},{20,28},{24,32},{28,36},{32,40... | collective-permute-start | bytes 393224 | tf_op jit(solution)/shard_map/ppermute | solution.py:225
  5.7 1.6 %collective-permute-start.4 = (bf16[64,1024]{1,0:T(8,128)(2,1)}, bf16[64,1024]{1,0:T(8,128)(2,1)S(1)}, u32[]{:S(2)}, u32[]{:S(2)}) collective-permute-start(bf16[64,1024]{1,0:T(8,128)(2,1)} %refs_4_.3), channel_id=1, source_target_pairs={{0,8},{4,12},{8,16},{12,20},{16,24},{20,28},{24,32},{28,36},{32,40... | collective-permute-start | bytes 393224 | tf_op jit(solution)/shard_map/ppermute | solution.py:225
  7.4 2.4 %collective-permute-done.8.refs_7_ = bf16[64,1024]{1,0:T(8,128)(2,1)S(1)} collective-permute-done((bf16[64,1024]{1,0:T(8,128)(2,1)}, bf16[64,1024]{1,0:T(8,128)(2,1)S(1)}, u32[]{:S(2)}, u32[]{:S(2)}) %collective-permute-start.8) | collective-permute-done | bytes 131104 | tf_op jit(solution)/shard_map/ppermute | solution.py:225
  9.8 5.0 %collective-permute-start.9 = (bf16[64,1024]{1,0:T(8,128)(2,1)S(1)}, bf16[64,1024]{1,0:T(8,128)(2,1)S(1)}, u32[]{:S(2)}, u32[]{:S(2)}) collective-permute-start(bf16[64,1024]{1,0:T(8,128)(2,1)S(1)} %collective-permute-done.8.refs_7_), channel_id=1, source_target_pairs={{0,248},{4,252},{8,0},{12,4},{16,8},{20,12},{24,16},{28,20},{32,24... | collective-permute-start | bytes 393224 | tf_op jit(solution)/shard_map/ppermute | solution.py:225
  14.8 3.5 %collective-permute-done.12.refs_8_ = bf16[64,1024]{1,0:T(8,128)(2,1)S(1)} collective-permute-done((bf16[64,1024]{1,0:T(8,128)(2,1)}, bf16[64,1024]{1,0:T(8,128)(2,1)S(1)}, u32[]{:S(2)}, u32[]{:S(2)}) %collective-permute-start.12) | collective-permute-done | bytes 131104 | tf_op jit(solution)/shard_map/ppermute | solution.py:225
  18.3 0.0 collective-permute-start.13
  18.3 0.0 collective-permute-done.refs_5_
  18.3 1.5 %collective-permute-start.1 = (bf16[64,1024]{1,0:T(8,128)(2,1)S(1)}, bf16[64,1024]{1,0:T(8,128)(2,1)S(1)}, u32[]{:S(2)}, u32[]{:S(2)}) collective-permute-start(bf16[64,1024]{1,0:T(8,128)(2,1)S(1)} %collective-permute-done.refs_5_), channel_id=1, source_target_pairs={{0,8},{4,12},{8,16},{12,20},{16,24},{20,28},{24,32},{28,36},{32,40... | collective-permute-start | bytes 393224 | tf_op jit(solution)/shard_map/ppermute | solution.py:225
  19.7 0.0 collective-permute-done.4.refs_6_
  19.7 0.1 collective-permute-start.5
  19.8 0.0 collective-permute-done.9.refs_11_
  19.8 4.7 %collective-permute-start.10 = (bf16[64,1024]{1,0:T(8,128)(2,1)S(1)}, bf16[64,1024]{1,0:T(8,128)(2,1)S(1)}, u32[]{:S(2)}, u32[]{:S(2)}) collective-permute-start(bf16[64,1024]{1,0:T(8,128)(2,1)S(1)} %collective-permute-done.9.refs_11_), channel_id=1, source_target_pairs={{0,248},{4,252},{8,0},{12,4},{16,8},{20,12},{24,16},{28,20},{32,24... | collective-permute-start | bytes 393224 | tf_op jit(solution)/shard_map/ppermute | solution.py:225
  24.5 0.0 collective-permute-done.13.refs_12_
  24.5 1.6 %collective-permute-start.14 = (bf16[64,1024]{1,0:T(8,128)(2,1)S(1)}, bf16[64,1024]{1,0:T(8,128)(2,1)S(1)}, u32[]{:S(2)}, u32[]{:S(2)}) collective-permute-start(bf16[64,1024]{1,0:T(8,128)(2,1)S(1)} %collective-permute-done.13.refs_12_), channel_id=1, source_target_pairs={{0,248},{4,252},{8,0},{12,4},{16,8},{20,12},{24,16},{28,20},{32,24... | collective-permute-start | bytes 393224 | tf_op jit(solution)/shard_map/ppermute | solution.py:225
  26.2 0.0 collective-permute-done.1.refs_9_
  26.2 0.0 collective-permute-start.2
  26.2 2.5 %collective-permute-done.5.refs_10_ = bf16[64,1024]{1,0:T(8,128)(2,1)S(1)} collective-permute-done((bf16[64,1024]{1,0:T(8,128)(2,1)S(1)}, bf16[64,1024]{1,0:T(8,128)(2,1)S(1)}, u32[]{:S(2)}, u32[]{:S(2)}) %collective-permute-start.5) | collective-permute-done | bytes 131104 | tf_op jit(solution)/shard_map/ppermute | solution.py:225
  28.6 0.0 collective-permute-start.6
  28.7 0.0 collective-permute-done.10.refs_15_
  28.7 4.8 %collective-permute-start.11 = (bf16[64,1024]{1,0:T(8,128)(2,1)S(1)}, bf16[64,1024]{1,0:T(8,128)(2,1)S(1)}, u32[]{:S(2)}, u32[]{:S(2)}) collective-permute-start(bf16[64,1024]{1,0:T(8,128)(2,1)S(1)} %collective-permute-done.10.refs_15_), channel_id=1, source_target_pairs={{0,248},{4,252},{8,0},{12,4},{16,8},{20,12},{24,16},{28,20},{32,24... | collective-permute-start | bytes 393224 | tf_op jit(solution)/shard_map/ppermute | solution.py:225
  33.5 0.0 collective-permute-done.14.refs_16_
  33.5 1.2 %collective-permute-start.15 = (bf16[64,1024]{1,0:T(8,128)(2,1)S(1)}, bf16[64,1024]{1,0:T(8,128)(2,1)S(1)}, u32[]{:S(2)}, u32[]{:S(2)}) collective-permute-start(bf16[64,1024]{1,0:T(8,128)(2,1)S(1)} %collective-permute-done.14.refs_16_), channel_id=1, source_target_pairs={{0,248},{4,252},{8,0},{12,4},{16,8},{20,12},{24,16},{28,20},{32,24... | collective-permute-start | bytes 393224 | tf_op jit(solution)/shard_map/ppermute | solution.py:225
  34.6 0.0 collective-permute-done.2.refs_13_
  34.6 0.3 collective-permute-start.3
  34.9 2.1 %collective-permute-done.6.refs_14_ = bf16[64,1024]{1,0:T(8,128)(2,1)S(1)} collective-permute-done((bf16[64,1024]{1,0:T(8,128)(2,1)S(1)}, bf16[64,1024]{1,0:T(8,128)(2,1)S(1)}, u32[]{:S(2)}, u32[]{:S(2)}) %collective-permute-start.6) | collective-permute-done | bytes 131104 | tf_op jit(solution)/shard_map/ppermute | solution.py:225
  37.0 0.0 collective-permute-start.7
  37.0 0.0 copy-start
  37.0 1.2 %copy-done = bf16[64,8192]{1,0:T(8,128)(2,1)S(1)} copy-done((bf16[64,8192]{1,0:T(8,128)(2,1)S(1)}, bf16[64,8192]{1,0:T(8,128)(2,1)}, u32[]{:S(2)}) %copy-start) | copy-done | bytes 1048600
  38.3 0.0 copy-start.2
  38.3 0.7 %copy-done.2 = s32[8]{0:T(128)S(1)} copy-done((s32[8]{0:T(128)S(1)}, s32[8]{0:T(128)}, u32[]{:S(2)}) %copy-start.2) | copy-done | bytes 56
  38.9 0.0 copy-start.4
  38.9 0.9 %copy-done.4 = bf16[64,1024]{1,0:T(8,128)(2,1)S(1)} copy-done((bf16[64,1024]{1,0:T(8,128)(2,1)S(1)}, bf16[64,1024]{1,0:T(8,128)(2,1)}, u32[]{:S(2)}) %copy-start.4) | copy-done | bytes 131096
  39.8 0.0 copy-start.6
  39.8 0.9 %copy-done.6 = bf16[64,1024]{1,0:T(8,128)(2,1)S(1)} copy-done((bf16[64,1024]{1,0:T(8,128)(2,1)S(1)}, bf16[64,1024]{1,0:T(8,128)(2,1)}, u32[]{:S(2)}) %copy-start.6) | copy-done | bytes 131096
  40.7 0.0 copy-start.5
  40.7 0.0 copy-start.7
  40.7 3.9 %shard_map.46 = (f32[8,512]{1,0:T(8,128)S(1)}, f32[8,512]{1,0:T(8,128)S(1)}, f32[8,128,512]{2,1,0:T(8,128)S(1)}) custom-call(s32[1]{0:T(128)} %bitcast.refs_0_, s32[8]{0:T(128)S(1)} %copy-done.2, bf16[64,8192]{1,0:T(8,128)(2,1)S(1)} %copy-done, bf16[64,1024]{1,0:T(8,128)(2,1)S(1)} %copy-done.4, bf16[64,1024]{1,0:T(8,128)(2,1)S(1)} %copy-done.6, ...), custom_call_target="tpu_custom_call" | custom-call | flops 939524096 | bytes 65536 | tf_op jit(solution)/shard_map/pallas_call | solution.py:207
  44.6 0.0 copy-start.1
  44.6 0.0 collective-permute-done.16.refs_2_
  44.6 0.0 copy-done.3
  44.7 0.0 copy-done.5
  44.7 0.0 copy-done.7
  44.7 3.9 %shard_map.47 = (bf16[544,512]{1,0:T(8,128)(2,1)S(1)}, bf16[544,512]{1,0:T(8,128)(2,1)S(1)}) custom-call(s32[1]{0:T(128)S(6)} %sub.3.refs_0_, s32[8]{0:T(128)S(1)} %copy-done.3, bf16[64,8192]{1,0:T(8,128)(2,1)S(1)} %collective-permute-done.16.refs_2_, bf16[64,1024]{1,0:T(8,128)(2,1)S(1)} %copy-done.5, bf16[64,1024]{1,0:T(8,128)(2,1)S(1)} %copy-done.7, ...), custom_call_target="tpu_custom_call" | custom-call | flops 939524096 | bytes 65536 | tf_op jit(solution)/shard_map/pallas_call | solution.py:207
  48.5 2.4 %collective-permute-start.18 = (bf16[544,512]{1,0:T(8,128)(2,1)S(1)}, bf16[544,512]{1,0:T(8,128)(2,1)S(1)}, u32[]{:S(2)}, u32[]{:S(2)}) collective-permute-start(bf16[544,512]{1,0:T(8,128)(2,1)S(1)} %get-tuple-element.20), channel_id=1, source_target_pairs={{0,4},{4,0},{8,12},{12,8},{16,20},{20,16},{24,28},{28,24},{32,36},... | collective-permute-start | bytes 1671176 | tf_op jit(solution)/shard_map/ppermute | solution.py:228
  50.9 0.0 collective-permute-done.11.refs_5_
  50.9 0.1 collective-permute-start.19
  51.0 0.0 collective-permute-done.15.refs_6_
  51.0 0.0 collective-permute-done.3.refs_3_
  51.0 0.0 collective-permute-done.7.refs_4_
  51.1 0.5 collective-permute-start.17
  51.6 2.5 %collective-permute-done.17.refs_7_ = bf16[256,1024]{1,0:T(8,128)(2,1)S(1)} collective-permute-done((bf16[256,1024]{1,0:T(8,128)(2,1)S(1)}, bf16[256,1024]{1,0:T(8,128)(2,1)S(1)}, u32[]{:S(2)}, u32[]{:S(2)}) %collective-permute-start.17) | collective-permute-done | bytes 524320 | tf_op jit(solution)/shard_map/ppermute | solution.py:228
  54.0 0.0 collective-permute-done.18.refs_11_
  54.0 0.0 collective-permute-done.19.refs_12_
  54.1 0.0 copy-done.1
  54.1 3.8 %shard_map.48 = bf16[64,8192]{1,0:T(8,128)(2,1)} custom-call(s32[1]{0:T(128)} %bitcast.refs_0_, s32[8]{0:T(128)S(1)} %copy-done.3, bf16[64,8192]{1,0:T(8,128)(2,1)S(1)} %copy-done.1, bf16[64,1024]{1,0:T(8,128)(2,1)S(1)} %collective-permute-done.3.refs_3_, bf16[64,1024]{1,0:T(8,128)(2,1)S(1)} %collective-permute-done.7.refs_4_, ...), custom_call_target="tpu_custom_call" | custom-call | flops 536870912 | bytes 65536 | tf_op jit(solution)/shard_map/pallas_call | solution.py:207
  (1 shorter events, 0.0 us)
Async XLA Ops:
  0.0 44.6 %copy-start.3 = (s32[8]{0:T(128)S(1)}, s32[8]{0:T(128)}, u32[]{:S(2)}) copy-start(s32[8]{0:T(128)} %refs_1_.5) | copy-start | bytes 100
  0.0 44.6 %collective-permute-start.16 = (bf16[64,8192]{1,0:T(8,128)(2,1)}, bf16[64,8192]{1,0:T(8,128)(2,1)S(1)}, u32[]{:S(2)}, u32[]{:S(2)}) collective-permute-start(bf16[64,8192]{1,0:T(8,128)(2,1)} %refs_2_.3), channel_id=1, source_target_pairs={{0,4},{4,0},{8,12},{12,8},{16,20},{20,16},{24,28},{28,24},{32,36},... | collective-permute-start | bytes 3145736 | tf_op jit(solution)/shard_map/ppermute | solution.py:228
  3.2 6.6 %collective-permute-start.8 = (bf16[64,1024]{1,0:T(8,128)(2,1)}, bf16[64,1024]{1,0:T(8,128)(2,1)S(1)}, u32[]{:S(2)}, u32[]{:S(2)}) collective-permute-start(bf16[64,1024]{1,0:T(8,128)(2,1)} %refs_3_.3), channel_id=1, source_target_pairs={{0,64},{4,68},{8,72},{12,76},{16,80},{20,84},{24,88},{28,92},{32,9... | collective-permute-start | bytes 393224 | tf_op jit(solution)/shard_map/ppermute | solution.py:225
  3.2 15.0 %collective-permute-start.12 = (bf16[64,1024]{1,0:T(8,128)(2,1)}, bf16[64,1024]{1,0:T(8,128)(2,1)S(1)}, u32[]{:S(2)}, u32[]{:S(2)}) collective-permute-start(bf16[64,1024]{1,0:T(8,128)(2,1)} %refs_4_.3), channel_id=1, source_target_pairs={{0,64},{4,68},{8,72},{12,76},{16,80},{20,84},{24,88},{28,92},{32,9... | collective-permute-start | bytes 393224 | tf_op jit(solution)/shard_map/ppermute | solution.py:225
  4.1 14.2 %collective-permute-start = (bf16[64,1024]{1,0:T(8,128)(2,1)}, bf16[64,1024]{1,0:T(8,128)(2,1)S(1)}, u32[]{:S(2)}, u32[]{:S(2)}) collective-permute-start(bf16[64,1024]{1,0:T(8,128)(2,1)} %refs_3_.3), channel_id=1, source_target_pairs={{0,8},{4,12},{8,16},{12,20},{16,24},{20,28},{24,32},{28,36},{32,40... | collective-permute-start | bytes 393224 | tf_op jit(solution)/shard_map/ppermute | solution.py:225
  5.7 14.0 %collective-permute-start.4 = (bf16[64,1024]{1,0:T(8,128)(2,1)}, bf16[64,1024]{1,0:T(8,128)(2,1)S(1)}, u32[]{:S(2)}, u32[]{:S(2)}) collective-permute-start(bf16[64,1024]{1,0:T(8,128)(2,1)} %refs_4_.3), channel_id=1, source_target_pairs={{0,8},{4,12},{8,16},{12,20},{16,24},{20,28},{24,32},{28,36},{32,40... | collective-permute-start | bytes 393224 | tf_op jit(solution)/shard_map/ppermute | solution.py:225
  9.8 10.0 %collective-permute-start.9 = (bf16[64,1024]{1,0:T(8,128)(2,1)S(1)}, bf16[64,1024]{1,0:T(8,128)(2,1)S(1)}, u32[]{:S(2)}, u32[]{:S(2)}) collective-permute-start(bf16[64,1024]{1,0:T(8,128)(2,1)S(1)} %collective-permute-done.8.refs_7_), channel_id=1, source_target_pairs={{0,248},{4,252},{8,0},{12,4},{16,8},{20,12},{24,16},{28,20},{32,24... | collective-permute-start | bytes 393224 | tf_op jit(solution)/shard_map/ppermute | solution.py:225
  18.3 6.3 %collective-permute-start.13 = (bf16[64,1024]{1,0:T(8,128)(2,1)S(1)}, bf16[64,1024]{1,0:T(8,128)(2,1)S(1)}, u32[]{:S(2)}, u32[]{:S(2)}) collective-permute-start(bf16[64,1024]{1,0:T(8,128)(2,1)S(1)} %collective-permute-done.12.refs_8_), channel_id=1, source_target_pairs={{0,248},{4,252},{8,0},{12,4},{16,8},{20,12},{24,16},{28,20},{32,24... | collective-permute-start | bytes 393224 | tf_op jit(solution)/shard_map/ppermute | solution.py:225
  18.3 7.9 %collective-permute-start.1 = (bf16[64,1024]{1,0:T(8,128)(2,1)S(1)}, bf16[64,1024]{1,0:T(8,128)(2,1)S(1)}, u32[]{:S(2)}, u32[]{:S(2)}) collective-permute-start(bf16[64,1024]{1,0:T(8,128)(2,1)S(1)} %collective-permute-done.refs_5_), channel_id=1, source_target_pairs={{0,8},{4,12},{8,16},{12,20},{16,24},{20,28},{24,32},{28,36},{32,40... | collective-permute-start | bytes 393224 | tf_op jit(solution)/shard_map/ppermute | solution.py:225
  19.7 8.9 %collective-permute-start.5 = (bf16[64,1024]{1,0:T(8,128)(2,1)S(1)}, bf16[64,1024]{1,0:T(8,128)(2,1)S(1)}, u32[]{:S(2)}, u32[]{:S(2)}) collective-permute-start(bf16[64,1024]{1,0:T(8,128)(2,1)S(1)} %collective-permute-done.4.refs_6_), channel_id=1, source_target_pairs={{0,8},{4,12},{8,16},{12,20},{16,24},{20,28},{24,32},{28,36},{32,40... | collective-permute-start | bytes 393224 | tf_op jit(solution)/shard_map/ppermute | solution.py:225
  19.8 8.8 %collective-permute-start.10 = (bf16[64,1024]{1,0:T(8,128)(2,1)S(1)}, bf16[64,1024]{1,0:T(8,128)(2,1)S(1)}, u32[]{:S(2)}, u32[]{:S(2)}) collective-permute-start(bf16[64,1024]{1,0:T(8,128)(2,1)S(1)} %collective-permute-done.9.refs_11_), channel_id=1, source_target_pairs={{0,248},{4,252},{8,0},{12,4},{16,8},{20,12},{24,16},{28,20},{32,24... | collective-permute-start | bytes 393224 | tf_op jit(solution)/shard_map/ppermute | solution.py:225
  24.5 8.9 %collective-permute-start.14 = (bf16[64,1024]{1,0:T(8,128)(2,1)S(1)}, bf16[64,1024]{1,0:T(8,128)(2,1)S(1)}, u32[]{:S(2)}, u32[]{:S(2)}) collective-permute-start(bf16[64,1024]{1,0:T(8,128)(2,1)S(1)} %collective-permute-done.13.refs_12_), channel_id=1, source_target_pairs={{0,248},{4,252},{8,0},{12,4},{16,8},{20,12},{24,16},{28,20},{32,24... | collective-permute-start | bytes 393224 | tf_op jit(solution)/shard_map/ppermute | solution.py:225
  26.2 8.5 %collective-permute-start.2 = (bf16[64,1024]{1,0:T(8,128)(2,1)S(1)}, bf16[64,1024]{1,0:T(8,128)(2,1)S(1)}, u32[]{:S(2)}, u32[]{:S(2)}) collective-permute-start(bf16[64,1024]{1,0:T(8,128)(2,1)S(1)} %collective-permute-done.1.refs_9_), channel_id=1, source_target_pairs={{0,8},{4,12},{8,16},{12,20},{16,24},{20,28},{24,32},{28,36},{32,40... | collective-permute-start | bytes 393224 | tf_op jit(solution)/shard_map/ppermute | solution.py:225
  28.6 8.4 %collective-permute-start.6 = (bf16[64,1024]{1,0:T(8,128)(2,1)S(1)}, bf16[64,1024]{1,0:T(8,128)(2,1)S(1)}, u32[]{:S(2)}, u32[]{:S(2)}) collective-permute-start(bf16[64,1024]{1,0:T(8,128)(2,1)S(1)} %collective-permute-done.5.refs_10_), channel_id=1, source_target_pairs={{0,8},{4,12},{8,16},{12,20},{16,24},{20,28},{24,32},{28,36},{32,40... | collective-permute-start | bytes 393224 | tf_op jit(solution)/shard_map/ppermute | solution.py:225
  28.7 22.3 %collective-permute-start.11 = (bf16[64,1024]{1,0:T(8,128)(2,1)S(1)}, bf16[64,1024]{1,0:T(8,128)(2,1)S(1)}, u32[]{:S(2)}, u32[]{:S(2)}) collective-permute-start(bf16[64,1024]{1,0:T(8,128)(2,1)S(1)} %collective-permute-done.10.refs_15_), channel_id=1, source_target_pairs={{0,248},{4,252},{8,0},{12,4},{16,8},{20,12},{24,16},{28,20},{32,24... | collective-permute-start | bytes 393224 | tf_op jit(solution)/shard_map/ppermute | solution.py:225
  33.5 17.6 %collective-permute-start.15 = (bf16[64,1024]{1,0:T(8,128)(2,1)S(1)}, bf16[64,1024]{1,0:T(8,128)(2,1)S(1)}, u32[]{:S(2)}, u32[]{:S(2)}) collective-permute-start(bf16[64,1024]{1,0:T(8,128)(2,1)S(1)} %collective-permute-done.14.refs_16_), channel_id=1, source_target_pairs={{0,248},{4,252},{8,0},{12,4},{16,8},{20,12},{24,16},{28,20},{32,24... | collective-permute-start | bytes 393224 | tf_op jit(solution)/shard_map/ppermute | solution.py:225
  34.6 16.4 %collective-permute-start.3 = (bf16[64,1024]{1,0:T(8,128)(2,1)S(1)}, bf16[64,1024]{1,0:T(8,128)(2,1)S(1)}, u32[]{:S(2)}, u32[]{:S(2)}) collective-permute-start(bf16[64,1024]{1,0:T(8,128)(2,1)S(1)} %collective-permute-done.2.refs_13_), channel_id=1, source_target_pairs={{0,8},{4,12},{8,16},{12,20},{16,24},{20,28},{24,32},{28,36},{32,40... | collective-permute-start | bytes 393224 | tf_op jit(solution)/shard_map/ppermute | solution.py:225
  37.0 14.0 %collective-permute-start.7 = (bf16[64,1024]{1,0:T(8,128)(2,1)S(1)}, bf16[64,1024]{1,0:T(8,128)(2,1)S(1)}, u32[]{:S(2)}, u32[]{:S(2)}) collective-permute-start(bf16[64,1024]{1,0:T(8,128)(2,1)S(1)} %collective-permute-done.6.refs_14_), channel_id=1, source_target_pairs={{0,8},{4,12},{8,16},{12,20},{16,24},{20,28},{24,32},{28,36},{32,40... | collective-permute-start | bytes 393224 | tf_op jit(solution)/shard_map/ppermute | solution.py:225
  37.0 1.2 %copy-start = (bf16[64,8192]{1,0:T(8,128)(2,1)S(1)}, bf16[64,8192]{1,0:T(8,128)(2,1)}, u32[]{:S(2)}) copy-start(bf16[64,8192]{1,0:T(8,128)(2,1)} %refs_2_.3) | copy-start | bytes 3145732
  38.3 0.7 %copy-start.2 = (s32[8]{0:T(128)S(1)}, s32[8]{0:T(128)}, u32[]{:S(2)}) copy-start(s32[8]{0:T(128)} %refs_1_.5) | copy-start | bytes 100
  38.9 0.9 %copy-start.4 = (bf16[64,1024]{1,0:T(8,128)(2,1)S(1)}, bf16[64,1024]{1,0:T(8,128)(2,1)}, u32[]{:S(2)}) copy-start(bf16[64,1024]{1,0:T(8,128)(2,1)} %refs_3_.3) | copy-start | bytes 393220
  39.8 0.9 %copy-start.6 = (bf16[64,1024]{1,0:T(8,128)(2,1)S(1)}, bf16[64,1024]{1,0:T(8,128)(2,1)}, u32[]{:S(2)}) copy-start(bf16[64,1024]{1,0:T(8,128)(2,1)} %refs_4_.3) | copy-start | bytes 393220
  40.7 3.9 %copy-start.5 = (bf16[64,1024]{1,0:T(8,128)(2,1)S(1)}, bf16[64,1024]{1,0:T(8,128)(2,1)}, u32[]{:S(2)}) copy-start(bf16[64,1024]{1,0:T(8,128)(2,1)} %refs_3_.3) | copy-start | bytes 393220
  40.7 3.9 %copy-start.7 = (bf16[64,1024]{1,0:T(8,128)(2,1)S(1)}, bf16[64,1024]{1,0:T(8,128)(2,1)}, u32[]{:S(2)}) copy-start(bf16[64,1024]{1,0:T(8,128)(2,1)} %refs_4_.3) | copy-start | bytes 393220
  44.6 9.4 %copy-start.1 = (bf16[64,8192]{1,0:T(8,128)(2,1)S(1)}, bf16[64,8192]{1,0:T(8,128)(2,1)}, u32[]{:S(2)}) copy-start(bf16[64,8192]{1,0:T(8,128)(2,1)} %refs_2_.3) | copy-start | bytes 3145732
  48.5 5.5 %collective-permute-start.18 = (bf16[544,512]{1,0:T(8,128)(2,1)S(1)}, bf16[544,512]{1,0:T(8,128)(2,1)S(1)}, u32[]{:S(2)}, u32[]{:S(2)}) collective-permute-start(bf16[544,512]{1,0:T(8,128)(2,1)S(1)} %get-tuple-element.20), channel_id=1, source_target_pairs={{0,4},{4,0},{8,12},{12,8},{16,20},{20,16},{24,28},{28,24},{32,36},... | collective-permute-start | bytes 1671176 | tf_op jit(solution)/shard_map/ppermute | solution.py:228
  50.9 3.1 %collective-permute-start.19 = (bf16[544,512]{1,0:T(8,128)(2,1)S(1)}, bf16[544,512]{1,0:T(8,128)(2,1)S(1)}, u32[]{:S(2)}, u32[]{:S(2)}) collective-permute-start(bf16[544,512]{1,0:T(8,128)(2,1)S(1)} %get-tuple-element.21), channel_id=1, source_target_pairs={{0,4},{4,0},{8,12},{12,8},{16,20},{20,16},{24,28},{28,24},{32,36},... | collective-permute-start | bytes 1671176 | tf_op jit(solution)/shard_map/ppermute | solution.py:228
  51.1 3.0 %collective-permute-start.17 = (bf16[256,1024]{1,0:T(8,128)(2,1)S(1)}, bf16[256,1024]{1,0:T(8,128)(2,1)S(1)}, u32[]{:S(2)}, u32[]{:S(2)}) collective-permute-start(bf16[256,1024]{1,0:T(8,128)(2,1)S(1)} %pad_maximum_fusion), channel_id=1, source_target_pairs={{0,4},{4,0},{8,12},{12,8},{16,20},{20,16},{24,28},{28,24},{32,36},... | collective-permute-start | bytes 1572872 | tf_op jit(solution)/shard_map/ppermute | solution.py:228

commit v4 on v3

--- a/solution.py
+++ b/solution.py
@@ -30,26 +30,26 @@
 SIBLING = [(i, i ^ 1) for i in range(2 * CHIPS)]
 
 
-def bands(docs_ref):
+def bands(info_ref):
     lane = lax.broadcasted_iota(jnp.int32, (ROWS, DH), 1)
     low = jnp.where(lane == ROWS + DOCS, -(1 << 30), 1 << 30)
     high = jnp.where(lane == ROWS + DOCS, 0, 1 << 30)
     end = jnp.int32(0)
     for d in range(DOCS):
-        begin, end = end, end + docs_ref[d]
+        begin, end = end, end + info_ref[1 + d]
         low = jnp.where(lane == ROWS + d, begin, low)
         high = jnp.where(lane == ROWS + d, end, high)
     return lane, low, high
 
 
-def query_marks(here, docs_ref):
-    lane, low, high = bands(docs_ref)
+def query_marks(here, info_ref):
+    lane, low, high = bands(info_ref)
     row = lax.broadcasted_iota(jnp.int32, (ROWS, DH), 0)
     pos = here * ROWS + row
     start = jnp.zeros_like(pos)
     end = jnp.int32(0)
     for d in range(DOCS):
-        end = end + docs_ref[d]
+        end = end + info_ref[1 + d]
         start = jnp.where(pos >= end, end, start)
     own = (lane <= row) & (here * ROWS + lane >= start)
     other = ((pos >= low) & (pos < high)) | (lane > ROWS + DOCS)
@@ -57,8 +57,8 @@
     return marks.astype(jnp.bfloat16)
 
 
-def key_marks(here, docs_ref, places):
-    lane, low, high = bands(docs_ref)
+def key_marks(here, info_ref, places):
+    lane, low, high = bands(info_ref)
     row = lax.broadcasted_iota(jnp.int32, (ROWS, DH), 0)
     core = lax.rem(here, 2)
     marks = []
@@ -78,16 +78,18 @@
 
 
 def flash_kernel(n, places, kind, *refs):
-    here_ref, docs_ref, q_ref = refs[:3]
+    info_ref, q_ref = refs[:2]
     if kind == "end":
-        kv, refs = refs[3:8], refs[8:]
+        kv, refs = refs[2:7], refs[7:]
         m_in, l_in, acc_in, *lent, out_ref, staged, sems = refs
     else:
-        kv, refs = refs[3 : 3 + 2 * n], refs[3 + 2 * n :]
-
-    here = here_ref[0]
-    q_marks = jnp.concatenate([query_marks(here, docs_ref)] * GROUP, axis=0)
-    k_marks = key_marks(here, docs_ref, places)
+        kv, refs = refs[2 : 1 + 2 * n], refs[1 + 2 * n :]
+
+    here = info_ref[0]
+    if kind == "lend":
+        lent = refs
+    q_marks = jnp.concatenate([query_marks(here, info_ref)] * GROUP, axis=0)
+    k_marks = key_marks(here, info_ref, places)
 
     def shards(which, h):
         cols = slice(h * DH, (h + 1) * DH)
@@ -95,7 +97,8 @@
             parts = [kv[which][:, cols], kv[2 + which][:, cols]]
             parts += [kv[4][(2 * s + which) * ROWS : (2 * s + which + 1) * ROWS, cols] for s in range(2)]
         else:
-            parts = [kv[2 * s + which][:, cols] for s in range(n)]
+            parts = [kv[0][which * ROWS : (which + 1) * ROWS, cols]]
+            parts += [kv[2 * s - 1 + which][:, cols] for s in range(1, n)]
         return jnp.concatenate(parts, axis=0)
 
     scores = []
@@ -122,12 +125,13 @@
         totals.append(jnp.sum(weight, axis=0, keepdims=True))
         weights.append(weight.astype(jnp.bfloat16))
     if kind == "lend":
-        lent = refs
-        for i in range(HALVES):
-            half = slice(i * HALF, (i + 1) * HALF)
-            pieces = in_three(jnp.concatenate(tops[half], axis=0)) + in_three(jnp.concatenate(totals[half], axis=0))
-            pieces += [jnp.zeros((STATS - 6 * HALF, COLS), jnp.float32)]
-            lent[i][HALF * DH :, :] = jnp.concatenate(pieces, axis=0).astype(jnp.bfloat16)
+        for i, (low, high) in enumerate(LOTS):
+            pieces = in_three(jnp.concatenate(tops[low:high], axis=0)) + in_three(
+                jnp.concatenate(totals[low:high], axis=0)
+            )
+            if STATS > 6 * (high - low):
+                pieces += [jnp.zeros((STATS - 6 * (high - low), COLS), jnp.float32)]
+            lent[i][(high - low) * DH : (high - low) * DH + STATS, :] = jnp.concatenate(pieces, axis=0).astype(jnp.bfloat16)
     if kind == "own":
         m_out, l_out, acc_out = refs
         m_out[...] = jnp.concatenate(tops, axis=0)
@@ -140,14 +144,16 @@
         if kind == "own":
             acc_out[h] = part
         if kind == "lend":
-            lent[h // HALF][h % HALF * DH : (h % HALF + 1) * DH, :] = (part * (1.0 / totals[h])).astype(jnp.bfloat16)
+            i, j = lot_of(h)
+            lent[i][j * DH : (j + 1) * DH, :] = (part * (1.0 / totals[h])).astype(jnp.bfloat16)
         if kind == "end":
             wide = slice(h * WIDE, (h + 1) * WIDE)
             held = jnp.exp2((m_in[h : h + 1, :] - tops[h]) * RATE)
             got = l_lent[h : h + 1, :] * jnp.exp2((m_lent[h : h + 1, :] - tops[h]) * RATE)
             share = 1.0 / (totals[h] + l_in[h : h + 1, :] * held + got)
             part = part * share + acc_in[h] * (held * share)
-            part = part + lent[h // HALF][h % HALF * DH : (h % HALF + 1) * DH, :].astype(jnp.float32) * (got * share)
+            i, j = lot_of(h)
+            part = part + lent[i][j * DH : (j + 1) * DH, :].astype(jnp.float32) * (got * share)
             result = part.T.astype(jnp.bfloat16)
             for g in range(GROUP):
                 staged[:, h * WIDE + g * DH : h * WIDE + (g + 1) * DH] = result[g * ROWS : (g + 1) * ROWS, :]
@@ -157,9 +163,15 @@
         copy.wait()
 
 
-HALVES = 2
-HALF = HK // HALVES
+LOTS = ((0, 4), (4, 8))
 STATS = 32
+LENT = 640
+
+
+def lot_of(h):
+    for i, (low, high) in enumerate(LOTS):
+        if low <= h < high:
+            return i, h - low
 
 
 def in_three(x):
@@ -172,9 +184,10 @@
 
 def lent_stats(lent):
     tops, totals = [], []
-    for half in lent:
-        stats = half[HALF * DH :, :].astype(jnp.float32)
-        pieces = [stats[i * HALF : (i + 1) * HALF, :] for i in range(6)]
+    for lot, (low, high) in zip(lent, LOTS):
+        n = high - low
+        stats = lot[n * DH : n * DH + STATS, :].astype(jnp.float32)
+        pieces = [stats[i * n : (i + 1) * n, :] for i in range(6)]
         tops.append(pieces[0] + pieces[1] + pieces[2])
         totals.append(pieces[3] + pieces[4] + pieces[5])
     return jnp.concatenate(tops, axis=0), jnp.concatenate(totals, axis=0)
@@ -185,9 +198,10 @@
 HBM = pl.BlockSpec(memory_space=pl.ANY)
 
 
-def flash(kind, here, docs, q, arrays, places):
+def flash(kind, info, q, arrays, places):
     n = len(places)
-    operands = [here, docs, q] + list(arrays)
+    operands = [info, q] + list(arrays)
+    in_specs = [SMEM] + [VMEM] * (len(operands) - 1)
     scratch = []
     out_specs = VMEM
     if kind == "end":
@@ -195,8 +209,10 @@
         out_specs = HBM
         scratch = [pltpu.VMEM((ROWS, HQ * DH), jnp.bfloat16), pltpu.SemaphoreType.DMA((HK,))]
     elif kind == "lend":
-        out_specs = (VMEM,) * HALVES
-        out_shape = (jax.ShapeDtypeStruct((HALF * DH + STATS, COLS), jnp.bfloat16),) * HALVES
+        out_specs = (VMEM,) * len(LOTS)
+        out_shape = tuple(
+            jax.ShapeDtypeStruct((LENT, COLS), jnp.bfloat16) for low, high in LOTS
+        )
     else:
         out_specs = (VMEM, VMEM, VMEM)
         out_shape = (
@@ -207,7 +223,7 @@
     return pl.pallas_call(
         functools.partial(flash_kernel, n, tuple(places), kind),
         out_shape=out_shape,
-        in_specs=[SMEM, SMEM] + [VMEM] * (len(operands) - 2),
+        in_specs=in_specs,
         out_specs=out_specs,
         scratch_shapes=scratch,
         compiler_params=pltpu.CompilerParams(vmem_limit_bytes=16 * 1024 * 1024),
@@ -220,6 +236,7 @@
 def per_device(queries, key_heads, value_heads, doc_lengths):
     here = lax.axis_index("seq").astype(jnp.int32).reshape(1)
     there = here + 1 - 2 * lax.rem(here, 2)
+    info, info_there = (jnp.concatenate([place, doc_lengths]) for place in (here, there))
 
     def send(block, ahead):
         return lax.ppermute(block, "seq", chip_route(ahead))
@@ -229,24 +246,28 @@
 
     own = (key_heads, value_heads)
     near, far = own, own
-    shards = list(own)
+    shards = [jnp.concatenate(own, axis=0)]
     chips = [0]
     for step in range(NEAR):
         near = tuple(send(x, 1) for x in near)
         far = tuple(send(x, FAR if step == 0 else -1) for x in far)
+        if step == 0:
+            first, shards[0] = lax.optimization_barrier((far[0], shards[0]))
+            far = (first, far[1])
         if step < NEAR - 1:
             shards += list(near + far)
             chips += [step + 1, FAR - step]
     end = near + far
     end_chips = [NEAR, FAR - NEAR + 1]
 
-    lent = flash("lend", there, doc_lengths, swap(queries), shards, [(c, True) for c in chips])
+    lent = flash("lend", info_there, swap(queries), shards, [(c, True) for c in chips])
     got = [swap(x) for x in lent]
-    state = flash("own", here, doc_lengths, queries, shards, [(c, False) for c in chips])
-    end, state, _ = lax.optimization_barrier((end, state, lent))
+    q, _ = lax.optimization_barrier((queries, lent))
+    state = flash("own", info, q, shards, [(c, False) for c in chips])
+    end, state = lax.optimization_barrier((end, state))
     arrays = list(end) + [swap(jnp.concatenate(end, axis=0))] + list(state) + got
     places = [(c, False) for c in end_chips] + [(c, True) for c in end_chips]
-    return flash("end", here, doc_lengths, queries, arrays, places)
+    return flash("end", info, queries, arrays, places)
 
 
 def solution(mesh):

time: 58.2 us -> 54.2 us (0.931)
  local copies, waits for them, and re-layouts: 3.7 us -> 0.01 us
  waiting for transfers between devices: 13 us -> 10.3 us
  other arithmetic: 0.04 us -> 1.75 us
  Pallas kernels: 11.5 us -> 12.2 us
    unnamed x16 -> x2, local copies, waits for them, and re-layouts: 3.7 us -> 0.01 us
    ppermute x16, waiting for transfers between devices: 10.5 us -> 8.75 us  [send(): return lax.ppermute(block, 'seq', chip_route(ahead))]
    concatenate x0 -> x2, other arithmetic: none -> 1.71 us  [the longest x1 0.99 us: per_device(): shards = [jnp.concatenate(own, axis=0)]]
    ppermute x4, waiting for transfers between devices: 2.48 us -> 1.54 us  [swap(): return lax.ppermute(block, 'seq', SIBLING)]
    pallas_call x3, Pallas kernels: 11.5 us -> 12.2 us  [flash(): pl.pallas_call(functools.partial(flash_kernel, n, tuple(places), kind), o...]
  transfers between devices with their start and end apart: 20 -> 20, of which waited for: 5 -> 5; matrix products, arithmetic and copies ran while one was open for 0% -> 3% of each run, Pallas kernels for 13% -> 16%
where the time goes in v4:
time: 54.2 us; the launch traced here: 54.1 us
  starting transfers between devices  29.6 us (55%)
  Pallas kernels  12.2 us (23%)
  waiting for transfers between devices  10.3 us (19%)
  other arithmetic  1.75 us (3%)
    ppermute x16, starting transfers between devices, send(): return lax.ppermute(block, 'seq', chip_route(ahead))  23.3 us
    pallas_call x3, Pallas kernels, flash(): pl.pallas_call(functools.partial(flash_kernel, n, tuple(places), kind), o...  12.2 us
    ppermute x16, waiting for transfers between devices, send(): return lax.ppermute(block, 'seq', chip_route(ahead))  8.75 us
    ppermute x4, starting transfers between devices, swap(): return lax.ppermute(block, 'seq', SIBLING)  6.31 us
    ppermute x4, waiting for transfers between devices, swap(): return lax.ppermute(block, 'seq', SIBLING)  1.54 us
  transfers between devices with their start and end apart: 20, of which 5 were waited for; matrix products, arithmetic and copies ran while one was open for 3% of the time, Pallas kernels for 16%

profile of v4, /device:TPU:1, one launch (start us, length us, event | category | flops | bytes accessed | tf_op | source)
XLA Modules:
  0.0 54.1 jit_solution(10624673055799589130)
XLA Ops:
  0.0 0.0 copy-start
  0.0 3.2 %collective-permute-start.16 = (bf16[64,8192]{1,0:T(8,128)(2,1)}, bf16[64,8192]{1,0:T(8,128)(2,1)S(1)}, u32[]{:S(2)}, u32[]{:S(2)}) collective-permute-start(bf16[64,8192]{1,0:T(8,128)(2,1)} %refs_1_.2), channel_id=1, source_target_pairs={{0,4},{4,0},{8,12},{12,8},{16,20},{20,16},{24,28},{28,24},{32,36},... | collective-permute-start | bytes 3145736 | tf_op jit(solution)/shard_map/ppermute | solution.py:245
  3.2 0.0 collective-permute-start.8
  3.2 1.2 %collective-permute-start = (bf16[64,1024]{1,0:T(8,128)(2,1)}, bf16[64,1024]{1,0:T(8,128)(2,1)S(1)}, u32[]{:S(2)}, u32[]{:S(2)}) collective-permute-start(bf16[64,1024]{1,0:T(8,128)(2,1)} %param.5), channel_id=1, source_target_pairs={{0,8},{4,12},{8,16},{12,20},{16,24},{20,28},{24,32},{28,36},{32,40... | collective-permute-start | bytes 393224 | tf_op jit(solution)/shard_map/ppermute | solution.py:242
  4.4 1.3 %collective-permute-start.12 = (bf16[64,1024]{1,0:T(8,128)(2,1)}, bf16[64,1024]{1,0:T(8,128)(2,1)S(1)}, u32[]{:S(2)}, u32[]{:S(2)}) collective-permute-start(bf16[64,1024]{1,0:T(8,128)(2,1)} %param.6), channel_id=1, source_target_pairs={{0,64},{4,68},{8,72},{12,76},{16,80},{20,84},{24,88},{28,92},{32,9... | collective-permute-start | bytes 393224 | tf_op jit(solution)/shard_map/ppermute | solution.py:242
  5.7 1.6 %collective-permute-start.4 = (bf16[64,1024]{1,0:T(8,128)(2,1)}, bf16[64,1024]{1,0:T(8,128)(2,1)S(1)}, u32[]{:S(2)}, u32[]{:S(2)}) collective-permute-start(bf16[64,1024]{1,0:T(8,128)(2,1)} %param.6), channel_id=1, source_target_pairs={{0,8},{4,12},{8,16},{12,20},{16,24},{20,28},{24,32},{28,36},{32,40... | collective-permute-start | bytes 393224 | tf_op jit(solution)/shard_map/ppermute | solution.py:242
  7.4 1.0 %pad_maximum_fusion.1.refs_2_ = bf16[128,1024]{1,0:T(8,128)(2,1)S(1)} fusion(bf16[64,1024]{1,0:T(8,128)(2,1)} %param.6, bf16[64,1024]{1,0:T(8,128)(2,1)} %param.5), kind=kLoop, calls=%fused_computation.1 | loop fusion | flops 524288 | bytes 524288 | tf_op jit(solution)/shard_map/concatenate | solution.py:249
  8.4 1.4 %collective-permute-done.8.refs_5_ = bf16[64,1024]{1,0:T(8,128)(2,1)S(1)} collective-permute-done((bf16[64,1024]{1,0:T(8,128)(2,1)}, bf16[64,1024]{1,0:T(8,128)(2,1)S(1)}, u32[]{:S(2)}, u32[]{:S(2)}) %collective-permute-start.8) | collective-permute-done | bytes 131104 | tf_op jit(solution)/shard_map/ppermute | solution.py:242
  9.8 5.0 %collective-permute-start.9 = (bf16[64,1024]{1,0:T(8,128)(2,1)S(1)}, bf16[64,1024]{1,0:T(8,128)(2,1)S(1)}, u32[]{:S(2)}, u32[]{:S(2)}) collective-permute-start(bf16[64,1024]{1,0:T(8,128)(2,1)S(1)} %collective-permute-done.8.refs_5_), channel_id=1, source_target_pairs={{0,248},{4,252},{8,0},{12,4},{16,8},{20,12},{24,16},{28,20},{32,24... | collective-permute-start | bytes 393224 | tf_op jit(solution)/shard_map/ppermute | solution.py:242
  14.8 3.4 %collective-permute-done.12.refs_6_ = bf16[64,1024]{1,0:T(8,128)(2,1)S(1)} collective-permute-done((bf16[64,1024]{1,0:T(8,128)(2,1)}, bf16[64,1024]{1,0:T(8,128)(2,1)S(1)}, u32[]{:S(2)}, u32[]{:S(2)}) %collective-permute-start.12) | collective-permute-done | bytes 131104 | tf_op jit(solution)/shard_map/ppermute | solution.py:242
  18.2 0.0 collective-permute-start.13
  18.2 0.0 collective-permute-done.refs_3_
  18.2 1.5 %collective-permute-start.1 = (bf16[64,1024]{1,0:T(8,128)(2,1)S(1)}, bf16[64,1024]{1,0:T(8,128)(2,1)S(1)}, u32[]{:S(2)}, u32[]{:S(2)}) collective-permute-start(bf16[64,1024]{1,0:T(8,128)(2,1)S(1)} %collective-permute-done.refs_3_), channel_id=1, source_target_pairs={{0,8},{4,12},{8,16},{12,20},{16,24},{20,28},{24,32},{28,36},{32,40... | collective-permute-start | bytes 393224 | tf_op jit(solution)/shard_map/ppermute | solution.py:242
  19.7 0.0 collective-permute-done.4.refs_4_
  19.7 0.1 collective-permute-start.5
  19.8 0.0 collective-permute-done.9.refs_9_
  19.8 4.7 %collective-permute-start.10 = (bf16[64,1024]{1,0:T(8,128)(2,1)S(1)}, bf16[64,1024]{1,0:T(8,128)(2,1)S(1)}, u32[]{:S(2)}, u32[]{:S(2)}) collective-permute-start(bf16[64,1024]{1,0:T(8,128)(2,1)S(1)} %collective-permute-done.9.refs_9_), channel_id=1, source_target_pairs={{0,248},{4,252},{8,0},{12,4},{16,8},{20,12},{24,16},{28,20},{32,24... | collective-permute-start | bytes 393224 | tf_op jit(solution)/shard_map/ppermute | solution.py:242
  24.5 0.0 collective-permute-done.13.refs_10_
  24.5 1.6 %collective-permute-start.14 = (bf16[64,1024]{1,0:T(8,128)(2,1)S(1)}, bf16[64,1024]{1,0:T(8,128)(2,1)}, u32[]{:S(2)}, u32[]{:S(2)}) collective-permute-start(bf16[64,1024]{1,0:T(8,128)(2,1)S(1)} %collective-permute-done.13.refs_10_), channel_id=1, source_target_pairs={{0,248},{4,252},{8,0},{12,4},{16,8},{20,12},{24,16},{28,20},{32,24... | collective-permute-start | bytes 393224 | tf_op jit(solution)/shard_map/ppermute | solution.py:242
  26.1 0.0 collective-permute-done.1.refs_7_
  26.1 0.0 collective-permute-start.2
  26.1 2.5 %collective-permute-done.5.refs_8_ = bf16[64,1024]{1,0:T(8,128)(2,1)S(1)} collective-permute-done((bf16[64,1024]{1,0:T(8,128)(2,1)S(1)}, bf16[64,1024]{1,0:T(8,128)(2,1)S(1)}, u32[]{:S(2)}, u32[]{:S(2)}) %collective-permute-start.5) | collective-permute-done | bytes 131104 | tf_op jit(solution)/shard_map/ppermute | solution.py:242
  28.6 0.0 collective-permute-start.6
  28.6 0.0 collective-permute-done.10.refs_13_
  28.6 4.8 %collective-permute-start.11 = (bf16[64,1024]{1,0:T(8,128)(2,1)S(1)}, bf16[64,1024]{1,0:T(8,128)(2,1)S(1)}, u32[]{:S(2)}, u32[]{:S(2)}) collective-permute-start(bf16[64,1024]{1,0:T(8,128)(2,1)S(1)} %collective-permute-done.10.refs_13_), channel_id=1, source_target_pairs={{0,248},{4,252},{8,0},{12,4},{16,8},{20,12},{24,16},{28,20},{32,24... | collective-permute-start | bytes 393224 | tf_op jit(solution)/shard_map/ppermute | solution.py:242
  33.4 0.7 %pad_add_fusion.1 = (s32[9]{0:T(128)S(1)}, s32[9]{0:T(128)S(1)}) fusion(s32[1]{0:T(128)S(6)} %sub.3, s32[8]{0:T(128)} %param.7, s32[1]{0:T(128)} %bitcast), kind=kLoop, calls=%fused_computation.3 | loop fusion | flops 18 | bytes 112 | tf_op jit(solution)/shard_map/concatenate | solution.py:239
  34.1 0.0 collective-permute-done.14.refs_14_
  34.1 0.4 collective-permute-start.15
  34.5 0.0 collective-permute-done.2.refs_11_
  34.5 1.1 %collective-permute-start.3 = (bf16[64,1024]{1,0:T(8,128)(2,1)}, bf16[64,1024]{1,0:T(8,128)(2,1)S(1)}, u32[]{:S(2)}, u32[]{:S(2)}) collective-permute-start(bf16[64,1024]{1,0:T(8,128)(2,1)} %collective-permute-done.2.refs_11_), channel_id=1, source_target_pairs={{0,8},{4,12},{8,16},{12,20},{16,24},{20,28},{24,32},{28,36},{32,40... | collective-permute-start | bytes 393224 | tf_op jit(solution)/shard_map/ppermute | solution.py:242
  35.6 1.4 %collective-permute-done.6.refs_12_ = bf16[64,1024]{1,0:T(8,128)(2,1)} collective-permute-done((bf16[64,1024]{1,0:T(8,128)(2,1)S(1)}, bf16[64,1024]{1,0:T(8,128)(2,1)}, u32[]{:S(2)}, u32[]{:S(2)}) %collective-permute-start.6) | collective-permute-done | bytes 131104 | tf_op jit(solution)/shard_map/ppermute | solution.py:242
  37.0 0.0 collective-permute-start.7
  37.0 0.0 collective-permute-done.16.refs_1_
  37.0 4.2 %shard_map.46 = (bf16[640,512]{1,0:T(8,128)(2,1)S(1)}, bf16[640,512]{1,0:T(8,128)(2,1)S(1)}) custom-call(s32[9]{0:T(128)S(1)} %get-tuple-element.35.refs_0_, bf16[64,8192]{1,0:T(8,128)(2,1)S(1)} %collective-permute-done.16.refs_1_, bf16[128,1024]{1,0:T(8,128)(2,1)S(1)} %pad_maximum_fusion.1.refs_2_, bf16[64,1024]{1,0:T(8,128)(2,1)S(1)} %collective-permute-done.refs_3_, ...), custom_call_target="tpu_custom_call" | custom-call | flops 939524096 | bytes 65536 | tf_op jit(solution)/shard_map/pallas_call | solution.py:223
  41.2 2.5 %collective-permute-start.18 = (bf16[640,512]{1,0:T(8,128)(2,1)S(1)}, bf16[640,512]{1,0:T(8,128)(2,1)S(1)}, u32[]{:S(2)}, u32[]{:S(2)}) collective-permute-start(bf16[640,512]{1,0:T(8,128)(2,1)S(1)} %get-tuple-element.22), channel_id=1, source_target_pairs={{0,4},{4,0},{8,12},{12,8},{16,20},{20,16},{24,28},{28,24},{32,36},... | collective-permute-start | bytes 1966088 | tf_op jit(solution)/shard_map/ppermute | solution.py:245
  43.6 0.0 collective-permute-done.11.refs_4_
  43.6 0.1 collective-permute-start.19
  43.8 0.0 copy-done
  43.8 4.2 %shard_map.47 = (f32[8,512]{1,0:T(8,128)S(1)}, f32[8,512]{1,0:T(8,128)S(1)}, f32[8,128,512]{2,1,0:T(8,128)S(1)}) custom-call(s32[9]{0:T(128)S(1)} %get-tuple-element.36.refs_0_, bf16[64,8192]{1,0:T(8,128)(2,1)S(1)} %copy-done, bf16[128,1024]{1,0:T(8,128)(2,1)S(1)} %pad_maximum_fusion.1.refs_2_, bf16[64,1024]{1,0:T(8,128)(2,1)S(1)} %collective-permute-done.refs_3_, ...), custom_call_target="tpu_custom_call" | custom-call | flops 939524096 | bytes 65536 | tf_op jit(solution)/shard_map/pallas_call | solution.py:223
  48.0 0.0 collective-permute-done.15.refs_5_
  48.0 0.0 collective-permute-done.3.refs_2_
  48.0 0.0 collective-permute-done.7.refs_3_
  48.0 0.5 collective-permute-start.17
  48.6 1.5 %collective-permute-done.17.refs_6_ = bf16[256,1024]{1,0:T(8,128)(2,1)S(1)} collective-permute-done((bf16[256,1024]{1,0:T(8,128)(2,1)S(1)}, bf16[256,1024]{1,0:T(8,128)(2,1)S(1)}, u32[]{:S(2)}, u32[]{:S(2)}) %collective-permute-start.17) | collective-permute-done | bytes 524320 | tf_op jit(solution)/shard_map/ppermute | solution.py:245
  50.1 0.0 collective-permute-done.18.refs_10_
  50.1 0.0 collective-permute-done.19.refs_11_
  50.1 3.8 %shard_map.48 = bf16[64,8192]{1,0:T(8,128)(2,1)} custom-call(s32[9]{0:T(128)S(1)} %get-tuple-element.36.refs_0_, bf16[64,8192]{1,0:T(8,128)(2,1)S(1)} %copy-done, bf16[64,1024]{1,0:T(8,128)(2,1)S(1)} %collective-permute-done.3.refs_2_, bf16[64,1024]{1,0:T(8,128)(2,1)S(1)} %collective-permute-done.7.refs_3_, ...), custom_call_target="tpu_custom_call" | custom-call | flops 536870912 | bytes 65536 | tf_op jit(solution)/shard_map/pallas_call | solution.py:223
  (1 shorter events, 0.0 us)
Async XLA Ops:
  0.0 43.8 %copy-start = (bf16[64,8192]{1,0:T(8,128)(2,1)S(1)}, bf16[64,8192]{1,0:T(8,128)(2,1)}, u32[]{:S(2)}) copy-start(bf16[64,8192]{1,0:T(8,128)(2,1)} %refs_1_.2) | copy-start | bytes 3145732
  0.0 37.0 %collective-permute-start.16 = (bf16[64,8192]{1,0:T(8,128)(2,1)}, bf16[64,8192]{1,0:T(8,128)(2,1)S(1)}, u32[]{:S(2)}, u32[]{:S(2)}) collective-permute-start(bf16[64,8192]{1,0:T(8,128)(2,1)} %refs_1_.2), channel_id=1, source_target_pairs={{0,4},{4,0},{8,12},{12,8},{16,20},{20,16},{24,28},{28,24},{32,36},... | collective-permute-start | bytes 3145736 | tf_op jit(solution)/shard_map/ppermute | solution.py:245
  3.2 6.5 %collective-permute-start.8 = (bf16[64,1024]{1,0:T(8,128)(2,1)}, bf16[64,1024]{1,0:T(8,128)(2,1)S(1)}, u32[]{:S(2)}, u32[]{:S(2)}) collective-permute-start(bf16[64,1024]{1,0:T(8,128)(2,1)} %param.5), channel_id=1, source_target_pairs={{0,64},{4,68},{8,72},{12,76},{16,80},{20,84},{24,88},{28,92},{32,9... | collective-permute-start | bytes 393224 | tf_op jit(solution)/shard_map/ppermute | solution.py:242
  3.2 15.0 %collective-permute-start = (bf16[64,1024]{1,0:T(8,128)(2,1)}, bf16[64,1024]{1,0:T(8,128)(2,1)S(1)}, u32[]{:S(2)}, u32[]{:S(2)}) collective-permute-start(bf16[64,1024]{1,0:T(8,128)(2,1)} %param.5), channel_id=1, source_target_pairs={{0,8},{4,12},{8,16},{12,20},{16,24},{20,28},{24,32},{28,36},{32,40... | collective-permute-start | bytes 393224 | tf_op jit(solution)/shard_map/ppermute | solution.py:242
  4.4 13.8 %collective-permute-start.12 = (bf16[64,1024]{1,0:T(8,128)(2,1)}, bf16[64,1024]{1,0:T(8,128)(2,1)S(1)}, u32[]{:S(2)}, u32[]{:S(2)}) collective-permute-start(bf16[64,1024]{1,0:T(8,128)(2,1)} %param.6), channel_id=1, source_target_pairs={{0,64},{4,68},{8,72},{12,76},{16,80},{20,84},{24,88},{28,92},{32,9... | collective-permute-start | bytes 393224 | tf_op jit(solution)/shard_map/ppermute | solution.py:242
  5.7 14.0 %collective-permute-start.4 = (bf16[64,1024]{1,0:T(8,128)(2,1)}, bf16[64,1024]{1,0:T(8,128)(2,1)S(1)}, u32[]{:S(2)}, u32[]{:S(2)}) collective-permute-start(bf16[64,1024]{1,0:T(8,128)(2,1)} %param.6), channel_id=1, source_target_pairs={{0,8},{4,12},{8,16},{12,20},{16,24},{20,28},{24,32},{28,36},{32,40... | collective-permute-start | bytes 393224 | tf_op jit(solution)/shard_map/ppermute | solution.py:242
  9.8 10.0 %collective-permute-start.9 = (bf16[64,1024]{1,0:T(8,128)(2,1)S(1)}, bf16[64,1024]{1,0:T(8,128)(2,1)S(1)}, u32[]{:S(2)}, u32[]{:S(2)}) collective-permute-start(bf16[64,1024]{1,0:T(8,128)(2,1)S(1)} %collective-permute-done.8.refs_5_), channel_id=1, source_target_pairs={{0,248},{4,252},{8,0},{12,4},{16,8},{20,12},{24,16},{28,20},{32,24... | collective-permute-start | bytes 393224 | tf_op jit(solution)/shard_map/ppermute | solution.py:242
  18.2 6.3 %collective-permute-start.13 = (bf16[64,1024]{1,0:T(8,128)(2,1)S(1)}, bf16[64,1024]{1,0:T(8,128)(2,1)S(1)}, u32[]{:S(2)}, u32[]{:S(2)}) collective-permute-start(bf16[64,1024]{1,0:T(8,128)(2,1)S(1)} %collective-permute-done.12.refs_6_), channel_id=1, source_target_pairs={{0,248},{4,252},{8,0},{12,4},{16,8},{20,12},{24,16},{28,20},{32,24... | collective-permute-start | bytes 393224 | tf_op jit(solution)/shard_map/ppermute | solution.py:242
  18.2 7.9 %collective-permute-start.1 = (bf16[64,1024]{1,0:T(8,128)(2,1)S(1)}, bf16[64,1024]{1,0:T(8,128)(2,1)S(1)}, u32[]{:S(2)}, u32[]{:S(2)}) collective-permute-start(bf16[64,1024]{1,0:T(8,128)(2,1)S(1)} %collective-permute-done.refs_3_), channel_id=1, source_target_pairs={{0,8},{4,12},{8,16},{12,20},{16,24},{20,28},{24,32},{28,36},{32,40... | collective-permute-start | bytes 393224 | tf_op jit(solution)/shard_map/ppermute | solution.py:242
  19.7 8.9 %collective-permute-start.5 = (bf16[64,1024]{1,0:T(8,128)(2,1)S(1)}, bf16[64,1024]{1,0:T(8,128)(2,1)S(1)}, u32[]{:S(2)}, u32[]{:S(2)}) collective-permute-start(bf16[64,1024]{1,0:T(8,128)(2,1)S(1)} %collective-permute-done.4.refs_4_), channel_id=1, source_target_pairs={{0,8},{4,12},{8,16},{12,20},{16,24},{20,28},{24,32},{28,36},{32,40... | collective-permute-start | bytes 393224 | tf_op jit(solution)/shard_map/ppermute | solution.py:242
  19.8 8.8 %collective-permute-start.10 = (bf16[64,1024]{1,0:T(8,128)(2,1)S(1)}, bf16[64,1024]{1,0:T(8,128)(2,1)S(1)}, u32[]{:S(2)}, u32[]{:S(2)}) collective-permute-start(bf16[64,1024]{1,0:T(8,128)(2,1)S(1)} %collective-permute-done.9.refs_9_), channel_id=1, source_target_pairs={{0,248},{4,252},{8,0},{12,4},{16,8},{20,12},{24,16},{28,20},{32,24... | collective-permute-start | bytes 393224 | tf_op jit(solution)/shard_map/ppermute | solution.py:242
  24.5 9.6 %collective-permute-start.14 = (bf16[64,1024]{1,0:T(8,128)(2,1)S(1)}, bf16[64,1024]{1,0:T(8,128)(2,1)}, u32[]{:S(2)}, u32[]{:S(2)}) collective-permute-start(bf16[64,1024]{1,0:T(8,128)(2,1)S(1)} %collective-permute-done.13.refs_10_), channel_id=1, source_target_pairs={{0,248},{4,252},{8,0},{12,4},{16,8},{20,12},{24,16},{28,20},{32,24... | collective-permute-start | bytes 393224 | tf_op jit(solution)/shard_map/ppermute | solution.py:242
  26.1 8.4 %collective-permute-start.2 = (bf16[64,1024]{1,0:T(8,128)(2,1)S(1)}, bf16[64,1024]{1,0:T(8,128)(2,1)}, u32[]{:S(2)}, u32[]{:S(2)}) collective-permute-start(bf16[64,1024]{1,0:T(8,128)(2,1)S(1)} %collective-permute-done.1.refs_7_), channel_id=1, source_target_pairs={{0,8},{4,12},{8,16},{12,20},{16,24},{20,28},{24,32},{28,36},{32,40... | collective-permute-start | bytes 393224 | tf_op jit(solution)/shard_map/ppermute | solution.py:242
  28.6 8.4 %collective-permute-start.6 = (bf16[64,1024]{1,0:T(8,128)(2,1)S(1)}, bf16[64,1024]{1,0:T(8,128)(2,1)}, u32[]{:S(2)}, u32[]{:S(2)}) collective-permute-start(bf16[64,1024]{1,0:T(8,128)(2,1)S(1)} %collective-permute-done.5.refs_8_), channel_id=1, source_target_pairs={{0,8},{4,12},{8,16},{12,20},{16,24},{20,28},{24,32},{28,36},{32,40... | collective-permute-start | bytes 393224 | tf_op jit(solution)/shard_map/ppermute | solution.py:242
  28.6 15.0 %collective-permute-start.11 = (bf16[64,1024]{1,0:T(8,128)(2,1)S(1)}, bf16[64,1024]{1,0:T(8,128)(2,1)S(1)}, u32[]{:S(2)}, u32[]{:S(2)}) collective-permute-start(bf16[64,1024]{1,0:T(8,128)(2,1)S(1)} %collective-permute-done.10.refs_13_), channel_id=1, source_target_pairs={{0,248},{4,252},{8,0},{12,4},{16,8},{20,12},{24,16},{28,20},{32,24... | collective-permute-start | bytes 393224 | tf_op jit(solution)/shard_map/ppermute | solution.py:242
  34.1 13.9 %collective-permute-start.15 = (bf16[64,1024]{1,0:T(8,128)(2,1)}, bf16[64,1024]{1,0:T(8,128)(2,1)S(1)}, u32[]{:S(2)}, u32[]{:S(2)}) collective-permute-start(bf16[64,1024]{1,0:T(8,128)(2,1)} %collective-permute-done.14.refs_14_), channel_id=1, source_target_pairs={{0,248},{4,252},{8,0},{12,4},{16,8},{20,12},{24,16},{28,20},{32,24... | collective-permute-start | bytes 393224 | tf_op jit(solution)/shard_map/ppermute | solution.py:242
  34.5 13.4 %collective-permute-start.3 = (bf16[64,1024]{1,0:T(8,128)(2,1)}, bf16[64,1024]{1,0:T(8,128)(2,1)S(1)}, u32[]{:S(2)}, u32[]{:S(2)}) collective-permute-start(bf16[64,1024]{1,0:T(8,128)(2,1)} %collective-permute-done.2.refs_11_), channel_id=1, source_target_pairs={{0,8},{4,12},{8,16},{12,20},{16,24},{20,28},{24,32},{28,36},{32,40... | collective-permute-start | bytes 393224 | tf_op jit(solution)/shard_map/ppermute | solution.py:242
  37.0 11.0 %collective-permute-start.7 = (bf16[64,1024]{1,0:T(8,128)(2,1)}, bf16[64,1024]{1,0:T(8,128)(2,1)S(1)}, u32[]{:S(2)}, u32[]{:S(2)}) collective-permute-start(bf16[64,1024]{1,0:T(8,128)(2,1)} %collective-permute-done.6.refs_12_), channel_id=1, source_target_pairs={{0,8},{4,12},{8,16},{12,20},{16,24},{20,28},{24,32},{28,36},{32,40... | collective-permute-start | bytes 393224 | tf_op jit(solution)/shard_map/ppermute | solution.py:242
  41.2 8.9 %collective-permute-start.18 = (bf16[640,512]{1,0:T(8,128)(2,1)S(1)}, bf16[640,512]{1,0:T(8,128)(2,1)S(1)}, u32[]{:S(2)}, u32[]{:S(2)}) collective-permute-start(bf16[640,512]{1,0:T(8,128)(2,1)S(1)} %get-tuple-element.22), channel_id=1, source_target_pairs={{0,4},{4,0},{8,12},{12,8},{16,20},{20,16},{24,28},{28,24},{32,36},... | collective-permute-start | bytes 1966088 | tf_op jit(solution)/shard_map/ppermute | solution.py:245
  43.6 6.5 %collective-permute-start.19 = (bf16[640,512]{1,0:T(8,128)(2,1)S(1)}, bf16[640,512]{1,0:T(8,128)(2,1)S(1)}, u32[]{:S(2)}, u32[]{:S(2)}) collective-permute-start(bf16[640,512]{1,0:T(8,128)(2,1)S(1)} %get-tuple-element.23), channel_id=1, source_target_pairs={{0,4},{4,0},{8,12},{12,8},{16,20},{20,16},{24,28},{28,24},{32,36},... | collective-permute-start | bytes 1966088 | tf_op jit(solution)/shard_map/ppermute | solution.py:245
  48.0 2.0 %collective-permute-start.17 = (bf16[256,1024]{1,0:T(8,128)(2,1)S(1)}, bf16[256,1024]{1,0:T(8,128)(2,1)S(1)}, u32[]{:S(2)}, u32[]{:S(2)}) collective-permute-start(bf16[256,1024]{1,0:T(8,128)(2,1)S(1)} %pad_maximum_fusion), channel_id=1, source_target_pairs={{0,4},{4,0},{8,12},{12,8},{16,20},{20,16},{24,28},{28,24},{32,36},... | collective-permute-start | bytes 1572872 | tf_op jit(solution)/shard_map/ppermute | solution.py:245

commit v5 on v4

--- a/solution.py
+++ b/solution.py
@@ -77,46 +77,79 @@
     return jnp.concatenate(marks, axis=0)
 
 
-def flash_kernel(n, places, kind, *refs):
+def flash_kernel(places, kind, *refs):
+    n = len(places)
     info_ref, q_ref = refs[:2]
-    if kind == "end":
-        kv, refs = refs[2:7], refs[7:]
-        m_in, l_in, acc_in, *lent, out_ref, staged, sems = refs
-    else:
-        kv, refs = refs[2 : 1 + 2 * n], refs[1 + 2 * n :]
-
+    n_kv = 5 if kind == "end" else 2 * n - 1
+    kv, refs = refs[2 : 2 + n_kv], refs[2 + n_kv :]
+
+    here = info_ref[0]
+    start = jnp.int32(0)
+    end = jnp.int32(0)
+    for d in range(DOCS):
+        end = end + info_ref[1 + d]
+        start = jnp.where(here * ROWS >= end, end, start)
+
+    def reach(some):
+        nearest = here - 2 * min(places[s][0] for s in some) + 1
+        return nearest * ROWS + ROWS - 1 >= start
+
+    base = [s for s in range(n) if places[s][0] == 0]
+    near = [s for s in range(n) if 0 < places[s][0] <= NEAR]
+    far = [s for s in range(n) if places[s][0] > NEAR]
+    all_reach, near_reach = reach(far), reach(near)
+
+    def attend(some):
+        attend_some(some, places, kind, info_ref, q_ref, kv, refs)
+
+    pl.when(all_reach)(lambda: attend(base + near + far))
+    pl.when(near_reach & jnp.logical_not(all_reach))(lambda: attend(base + near))
+    pl.when(jnp.logical_not(near_reach))(lambda: attend(base))
+
+
+def attend_some(some, places, kind, info_ref, q_ref, kv, refs):
     here = info_ref[0]
     if kind == "lend":
         lent = refs
-    q_marks = jnp.concatenate([query_marks(here, info_ref)] * GROUP, axis=0)
-    k_marks = key_marks(here, info_ref, places)
+    if kind == "end":
+        m_in, l_in, acc_in, *lent, out_ref, staged, sems = refs
 
     def shards(which, h):
         cols = slice(h * DH, (h + 1) * DH)
-        if kind == "end":
-            parts = [kv[which][:, cols], kv[2 + which][:, cols]]
-            parts += [kv[4][(2 * s + which) * ROWS : (2 * s + which + 1) * ROWS, cols] for s in range(2)]
-        else:
-            parts = [kv[0][which * ROWS : (which + 1) * ROWS, cols]]
-            parts += [kv[2 * s - 1 + which][:, cols] for s in range(1, n)]
+        parts = []
+        for s in some:
+            if kind == "end" and s >= 2:
+                parts.append(kv[4][(2 * (s - 2) + which) * ROWS : (2 * (s - 2) + which + 1) * ROWS, cols])
+            elif kind == "end":
+                parts.append(kv[2 * s + which][:, cols])
+            elif s == 0:
+                parts.append(kv[0][which * ROWS : (which + 1) * ROWS, cols])
+            else:
+                parts.append(kv[2 * s - 1 + which][:, cols])
         return jnp.concatenate(parts, axis=0)
 
     scores = []
-    for h in range(HK):
-        q = jnp.concatenate([q_ref[:, h * WIDE + g * DH : h * WIDE + (g + 1) * DH] for g in range(GROUP)], axis=0)
-        scores.append(
-            lax.dot_general(
-                jnp.concatenate([shards(0, h), k_marks], axis=1),
-                jnp.concatenate([q, q_marks], axis=1),
-                (((1,), (1,)), ((), ())),
-                preferred_element_type=jnp.float32,
+    if some:
+        q_marks = jnp.concatenate([query_marks(here, info_ref)] * GROUP, axis=0)
+        k_marks = key_marks(here, info_ref, [places[s] for s in some])
+        for h in range(HK):
+            q = jnp.concatenate([q_ref[:, h * WIDE + g * DH : h * WIDE + (g + 1) * DH] for g in range(GROUP)], axis=0)
+            scores.append(
+                lax.dot_general(
+                    jnp.concatenate([shards(0, h), k_marks], axis=1),
+                    jnp.concatenate([q, q_marks], axis=1),
+                    (((1,), (1,)), ((), ())),
+                    preferred_element_type=jnp.float32,
+                )
             )
-        )
     if kind == "end":
         m_lent, l_lent = lent_stats(lent)
         known = jnp.maximum(m_in[...], m_lent)
     tops, totals, weights = [], [], []
     for h in range(HK):
+        if not some:
+            tops.append(known[h : h + 1, :])
+            continue
         top = jnp.max(scores[h], axis=0, keepdims=True)
         if kind == "end":
             top = jnp.maximum(top, known[h : h + 1, :])
@@ -131,30 +164,37 @@
             )
             if STATS > 6 * (high - low):
                 pieces += [jnp.zeros((STATS - 6 * (high - low), COLS), jnp.float32)]
-            lent[i][(high - low) * DH : (high - low) * DH + STATS, :] = jnp.concatenate(pieces, axis=0).astype(jnp.bfloat16)
+            stats = jnp.concatenate(pieces, axis=0).astype(jnp.bfloat16)
+            lent[i][(high - low) * DH : (high - low) * DH + STATS, :] = stats
     if kind == "own":
         m_out, l_out, acc_out = refs
         m_out[...] = jnp.concatenate(tops, axis=0)
         l_out[...] = jnp.concatenate(totals, axis=0)
     copies = []
     for h in range(HK):
-        part = lax.dot_general(
-            shards(1, h), weights[h], (((0,), (0,)), ((), ())), preferred_element_type=jnp.float32
-        )
+        if some:
+            part = lax.dot_general(
+                shards(1, h), weights[h], (((0,), (0,)), ((), ())), preferred_element_type=jnp.float32
+            )
         if kind == "own":
             acc_out[h] = part
         if kind == "lend":
             i, j = lot_of(h)
             lent[i][j * DH : (j + 1) * DH, :] = (part * (1.0 / totals[h])).astype(jnp.bfloat16)
         if kind == "end":
+            i, j = lot_of(h)
             wide = slice(h * WIDE, (h + 1) * WIDE)
             held = jnp.exp2((m_in[h : h + 1, :] - tops[h]) * RATE)
             got = l_lent[h : h + 1, :] * jnp.exp2((m_lent[h : h + 1, :] - tops[h]) * RATE)
-            share = 1.0 / (totals[h] + l_in[h : h + 1, :] * held + got)
-            part = part * share + acc_in[h] * (held * share)
-            i, j = lot_of(h)
-            part = part + lent[i][j * DH : (j + 1) * DH, :].astype(jnp.float32) * (got * share)
-            result = part.T.astype(jnp.bfloat16)
+            total = l_in[h : h + 1, :] * held + got
+            if some:
+                total = total + totals[h]
+            share = 1.0 / total
+            result = acc_in[h] * (held * share)
+            result = result + lent[i][j * DH : (j + 1) * DH, :].astype(jnp.float32) * (got * share)
+            if some:
+                result = result + part * share
+            result = result.T.astype(jnp.bfloat16)
             for g in range(GROUP):
                 staged[:, h * WIDE + g * DH : h * WIDE + (g + 1) * DH] = result[g * ROWS : (g + 1) * ROWS, :]
             copies.append(pltpu.make_async_copy(staged.at[:, wide], out_ref.at[:, wide], sems.at[h]))
@@ -210,9 +250,7 @@
         scratch = [pltpu.VMEM((ROWS, HQ * DH), jnp.bfloat16), pltpu.SemaphoreType.DMA((HK,))]
     elif kind == "lend":
         out_specs = (VMEM,) * len(LOTS)
-        out_shape = tuple(
-            jax.ShapeDtypeStruct((LENT, COLS), jnp.bfloat16) for low, high in LOTS
-        )
+        out_shape = (jax.ShapeDtypeStruct((LENT, COLS), jnp.bfloat16),) * len(LOTS)
     else:
         out_specs = (VMEM, VMEM, VMEM)
         out_shape = (
@@ -221,7 +259,7 @@
             jax.ShapeDtypeStruct((HK, DH, COLS), jnp.float32),
         )
     return pl.pallas_call(
-        functools.partial(flash_kernel, n, tuple(places), kind),
+        functools.partial(flash_kernel, tuple(places), kind),
         out_shape=out_shape,
         in_specs=in_specs,
         out_specs=out_specs,
@@ -252,7 +290,7 @@
         near = tuple(send(x, 1) for x in near)
         far = tuple(send(x, FAR if step == 0 else -1) for x in far)
         if step == 0:
-            first, shards[0] = lax.optimization_barrier((far[0], shards[0]))
+            first, shards[0], info, info_there = lax.optimization_barrier((far[0], shards[0], info, info_there))
             far = (first, far[1])
         if step < NEAR - 1:
             shards += list(near + far)

time: 54.2 us -> 51.4 us (0.948)
  Pallas kernels: 12.2 us -> 6.23 us
  starting transfers between devices: 29.6 us -> 32.8 us
    pallas_call x3, Pallas kernels: 12.2 us -> 6.23 us  [flash(): pl.pallas_call(functools.partial(flash_kernel, tuple(places), kind), out_...]
    ppermute x4, starting transfers between devices: 6.31 us -> 9.57 us  [swap(): return lax.ppermute(block, 'seq', SIBLING)]
  transfers between devices with their start and end apart: 20 -> 20, of which waited for: 5 -> 5; matrix products, arithmetic and copies ran while one was open for 3% -> 3% of each run, Pallas kernels for 16% -> 8%
where the time goes in v5:
time: 51.4 us; the launch traced here: 51.3 us
  starting transfers between devices  32.8 us (64%)
  waiting for transfers between devices  10.2 us (20%)
  Pallas kernels  6.23 us (12%)
  other arithmetic  1.75 us (3%)
    ppermute x16, starting transfers between devices, send(): return lax.ppermute(block, 'seq', chip_route(ahead))  23.3 us
    ppermute x4, starting transfers between devices, swap(): return lax.ppermute(block, 'seq', SIBLING)  9.57 us
    ppermute x16, waiting for transfers between devices, send(): return lax.ppermute(block, 'seq', chip_route(ahead))  8.65 us
    pallas_call x3, Pallas kernels, flash(): pl.pallas_call(functools.partial(flash_kernel, tuple(places), kind), out_...  6.23 us
    ppermute x4, waiting for transfers between devices, swap(): return lax.ppermute(block, 'seq', SIBLING)  1.54 us
  transfers between devices with their start and end apart: 20, of which 5 were waited for; matrix products, arithmetic and copies ran while one was open for 3% of the time, Pallas kernels for 8%

profile of v5, /device:TPU:1, one launch (start us, length us, event | category | flops | bytes accessed | tf_op | source)
XLA Modules:
  0.0 51.3 jit_solution(13952584556145899562)
XLA Ops:
  0.0 0.0 copy-start
  0.0 3.2 %collective-permute-start.16 = (bf16[64,8192]{1,0:T(8,128)(2,1)}, bf16[64,8192]{1,0:T(8,128)(2,1)S(1)}, u32[]{:S(2)}, u32[]{:S(2)}) collective-permute-start(bf16[64,8192]{1,0:T(8,128)(2,1)} %refs_1_.2), channel_id=1, source_target_pairs={{0,4},{4,0},{8,12},{12,8},{16,20},{20,16},{24,28},{28,24},{32,36},... | collective-permute-start | bytes 3145736 | tf_op jit(solution)/shard_map/ppermute | solution.py:283
  3.2 0.0 collective-permute-start
  3.2 1.2 %collective-permute-start.1 = (bf16[64,1024]{1,0:T(8,128)(2,1)}, bf16[64,1024]{1,0:T(8,128)(2,1)S(1)}, u32[]{:S(2)}, u32[]{:S(2)}) collective-permute-start(bf16[64,1024]{1,0:T(8,128)(2,1)} %param.5), channel_id=1, source_target_pairs={{0,8},{4,12},{8,16},{12,20},{16,24},{20,28},{24,32},{28,36},{32,40... | collective-permute-start | bytes 393224 | tf_op jit(solution)/shard_map/ppermute | solution.py:280
  4.4 1.3 %collective-permute-start.12 = (bf16[64,1024]{1,0:T(8,128)(2,1)}, bf16[64,1024]{1,0:T(8,128)(2,1)S(1)}, u32[]{:S(2)}, u32[]{:S(2)}) collective-permute-start(bf16[64,1024]{1,0:T(8,128)(2,1)} %param.6), channel_id=1, source_target_pairs={{0,64},{4,68},{8,72},{12,76},{16,80},{20,84},{24,88},{28,92},{32,9... | collective-permute-start | bytes 393224 | tf_op jit(solution)/shard_map/ppermute | solution.py:280
  5.7 1.6 %collective-permute-start.5 = (bf16[64,1024]{1,0:T(8,128)(2,1)}, bf16[64,1024]{1,0:T(8,128)(2,1)S(1)}, u32[]{:S(2)}, u32[]{:S(2)}) collective-permute-start(bf16[64,1024]{1,0:T(8,128)(2,1)} %param.6), channel_id=1, source_target_pairs={{0,8},{4,12},{8,16},{12,20},{16,24},{20,28},{24,32},{28,36},{32,40... | collective-permute-start | bytes 393224 | tf_op jit(solution)/shard_map/ppermute | solution.py:280
  7.4 1.0 %pad_maximum_fusion.1.refs_2_ = bf16[128,1024]{1,0:T(8,128)(2,1)S(1)} fusion(bf16[64,1024]{1,0:T(8,128)(2,1)} %param.6, bf16[64,1024]{1,0:T(8,128)(2,1)} %param.5), kind=kLoop, calls=%fused_computation.1 | loop fusion | flops 524288 | bytes 524288 | tf_op jit(solution)/shard_map/concatenate | solution.py:287
  8.4 0.7 %pad_add_fusion.1 = (s32[9]{0:T(128)S(1)}, s32[9]{0:T(128)S(1)}) fusion(s32[1]{0:T(128)S(6)} %sub.3, s32[8]{0:T(128)} %param.7, s32[1]{0:T(128)} %bitcast), kind=kLoop, calls=%fused_computation.3 | loop fusion | flops 18 | bytes 112 | tf_op jit(solution)/shard_map/concatenate | solution.py:277
  9.1 0.7 %collective-permute-done.refs_5_ = bf16[64,1024]{1,0:T(8,128)(2,1)S(1)} collective-permute-done((bf16[64,1024]{1,0:T(8,128)(2,1)}, bf16[64,1024]{1,0:T(8,128)(2,1)S(1)}, u32[]{:S(2)}, u32[]{:S(2)}) %collective-permute-start) | collective-permute-done | bytes 131104 | tf_op jit(solution)/shard_map/ppermute | solution.py:280
  9.8 5.0 %collective-permute-start.9 = (bf16[64,1024]{1,0:T(8,128)(2,1)S(1)}, bf16[64,1024]{1,0:T(8,128)(2,1)S(1)}, u32[]{:S(2)}, u32[]{:S(2)}) collective-permute-start(bf16[64,1024]{1,0:T(8,128)(2,1)S(1)} %collective-permute-done.refs_5_), channel_id=1, source_target_pairs={{0,248},{4,252},{8,0},{12,4},{16,8},{20,12},{24,16},{28,20},{32,24... | collective-permute-start | bytes 393224 | tf_op jit(solution)/shard_map/ppermute | solution.py:280
  14.8 3.4 %collective-permute-done.12.refs_6_ = bf16[64,1024]{1,0:T(8,128)(2,1)S(1)} collective-permute-done((bf16[64,1024]{1,0:T(8,128)(2,1)}, bf16[64,1024]{1,0:T(8,128)(2,1)S(1)}, u32[]{:S(2)}, u32[]{:S(2)}) %collective-permute-start.12) | collective-permute-done | bytes 131104 | tf_op jit(solution)/shard_map/ppermute | solution.py:280
  18.2 0.0 collective-permute-start.13
  18.2 0.0 collective-permute-done.1.refs_3_
  18.2 1.5 %collective-permute-start.2 = (bf16[64,1024]{1,0:T(8,128)(2,1)S(1)}, bf16[64,1024]{1,0:T(8,128)(2,1)S(1)}, u32[]{:S(2)}, u32[]{:S(2)}) collective-permute-start(bf16[64,1024]{1,0:T(8,128)(2,1)S(1)} %collective-permute-done.1.refs_3_), channel_id=1, source_target_pairs={{0,8},{4,12},{8,16},{12,20},{16,24},{20,28},{24,32},{28,36},{32,40... | collective-permute-start | bytes 393224 | tf_op jit(solution)/shard_map/ppermute | solution.py:280
  19.7 0.0 collective-permute-done.5.refs_4_
  19.7 0.1 collective-permute-start.6
  19.8 0.0 collective-permute-done.9.refs_9_
  19.8 4.7 %collective-permute-start.10 = (bf16[64,1024]{1,0:T(8,128)(2,1)S(1)}, bf16[64,1024]{1,0:T(8,128)(2,1)S(1)}, u32[]{:S(2)}, u32[]{:S(2)}) collective-permute-start(bf16[64,1024]{1,0:T(8,128)(2,1)S(1)} %collective-permute-done.9.refs_9_), channel_id=1, source_target_pairs={{0,248},{4,252},{8,0},{12,4},{16,8},{20,12},{24,16},{28,20},{32,24... | collective-permute-start | bytes 393224 | tf_op jit(solution)/shard_map/ppermute | solution.py:280
  24.5 0.0 collective-permute-done.13.refs_10_
  24.5 1.6 %collective-permute-start.14 = (bf16[64,1024]{1,0:T(8,128)(2,1)S(1)}, bf16[64,1024]{1,0:T(8,128)(2,1)S(1)}, u32[]{:S(2)}, u32[]{:S(2)}) collective-permute-start(bf16[64,1024]{1,0:T(8,128)(2,1)S(1)} %collective-permute-done.13.refs_10_), channel_id=1, source_target_pairs={{0,248},{4,252},{8,0},{12,4},{16,8},{20,12},{24,16},{28,20},{32,24... | collective-permute-start | bytes 393224 | tf_op jit(solution)/shard_map/ppermute | solution.py:280
  26.1 0.0 collective-permute-done.2.refs_7_
  26.1 0.0 collective-permute-start.3
  26.1 2.5 %collective-permute-done.6.refs_8_ = bf16[64,1024]{1,0:T(8,128)(2,1)S(1)} collective-permute-done((bf16[64,1024]{1,0:T(8,128)(2,1)S(1)}, bf16[64,1024]{1,0:T(8,128)(2,1)S(1)}, u32[]{:S(2)}, u32[]{:S(2)}) %collective-permute-start.6) | collective-permute-done | bytes 131104 | tf_op jit(solution)/shard_map/ppermute | solution.py:280
  28.6 0.0 collective-permute-start.7
  28.6 0.0 collective-permute-done.10.refs_13_
  28.6 4.8 %collective-permute-start.11 = (bf16[64,1024]{1,0:T(8,128)(2,1)S(1)}, bf16[64,1024]{1,0:T(8,128)(2,1)S(1)}, u32[]{:S(2)}, u32[]{:S(2)}) collective-permute-start(bf16[64,1024]{1,0:T(8,128)(2,1)S(1)} %collective-permute-done.10.refs_13_), channel_id=1, source_target_pairs={{0,248},{4,252},{8,0},{12,4},{16,8},{20,12},{24,16},{28,20},{32,24... | collective-permute-start | bytes 393224 | tf_op jit(solution)/shard_map/ppermute | solution.py:280
  33.4 0.0 collective-permute-done.14.refs_14_
  33.4 1.2 %collective-permute-start.15 = (bf16[64,1024]{1,0:T(8,128)(2,1)S(1)}, bf16[64,1024]{1,0:T(8,128)(2,1)S(1)}, u32[]{:S(2)}, u32[]{:S(2)}) collective-permute-start(bf16[64,1024]{1,0:T(8,128)(2,1)S(1)} %collective-permute-done.14.refs_14_), channel_id=1, source_target_pairs={{0,248},{4,252},{8,0},{12,4},{16,8},{20,12},{24,16},{28,20},{32,24... | collective-permute-start | bytes 393224 | tf_op jit(solution)/shard_map/ppermute | solution.py:280
  34.5 0.0 collective-permute-done.3.refs_11_
  34.5 0.3 collective-permute-start.4
  34.9 2.0 %collective-permute-done.7.refs_12_ = bf16[64,1024]{1,0:T(8,128)(2,1)S(1)} collective-permute-done((bf16[64,1024]{1,0:T(8,128)(2,1)S(1)}, bf16[64,1024]{1,0:T(8,128)(2,1)S(1)}, u32[]{:S(2)}, u32[]{:S(2)}) %collective-permute-start.7) | collective-permute-done | bytes 131104 | tf_op jit(solution)/shard_map/ppermute | solution.py:280
  36.9 0.0 collective-permute-start.8
  36.9 0.0 collective-permute-done.16.refs_1_
  36.9 1.7 %shard_map.46 = (bf16[640,512]{1,0:T(8,128)(2,1)S(1)}, bf16[640,512]{1,0:T(8,128)(2,1)S(1)}) custom-call(s32[9]{0:T(128)S(1)} %get-tuple-element.24.refs_0_, bf16[64,8192]{1,0:T(8,128)(2,1)S(1)} %collective-permute-done.16.refs_1_, bf16[128,1024]{1,0:T(8,128)(2,1)S(1)} %pad_maximum_fusion.1.refs_2_, bf16[64,1024]{1,0:T(8,128)(2,1)S(1)} %collective-permute-done.1.refs_3_, ...), custom_call_target="tpu_custom_call" | custom-call | flops 939524096 | bytes 65536 | tf_op jit(solution)/shard_map/pallas_call | solution.py:261
  38.5 3.4 %collective-permute-start.18 = (bf16[640,512]{1,0:T(8,128)(2,1)S(1)}, bf16[640,512]{1,0:T(8,128)(2,1)S(1)}, u32[]{:S(2)}, u32[]{:S(2)}) collective-permute-start(bf16[640,512]{1,0:T(8,128)(2,1)S(1)} %get-tuple-element.26), channel_id=1, source_target_pairs={{0,4},{4,0},{8,12},{12,8},{16,20},{20,16},{24,28},{28,24},{32,36},... | collective-permute-start | bytes 1966088 | tf_op jit(solution)/shard_map/ppermute | solution.py:283
  41.9 0.0 collective-permute-done.11.refs_4_
  41.9 0.1 collective-permute-start.19
  42.0 0.0 copy-done
  42.0 2.7 %shard_map.47 = (f32[8,512]{1,0:T(8,128)S(1)}, f32[8,512]{1,0:T(8,128)S(1)}, f32[8,128,512]{2,1,0:T(8,128)S(1)}) custom-call(s32[9]{0:T(128)S(1)} %get-tuple-element.22.refs_0_, bf16[64,8192]{1,0:T(8,128)(2,1)S(1)} %copy-done, bf16[128,1024]{1,0:T(8,128)(2,1)S(1)} %pad_maximum_fusion.1.refs_2_, bf16[64,1024]{1,0:T(8,128)(2,1)S(1)} %collective-permute-done.1.refs_3_, ...), custom_call_target="tpu_custom_call" | custom-call | flops 939524096 | bytes 65536 | tf_op jit(solution)/shard_map/pallas_call | solution.py:261
  44.7 0.0 collective-permute-done.15.refs_5_
  44.7 0.0 collective-permute-done.4.refs_2_
  44.7 0.0 collective-permute-done.8.refs_3_
  44.8 2.9 %collective-permute-start.17 = (bf16[256,1024]{1,0:T(8,128)(2,1)S(1)}, bf16[256,1024]{1,0:T(8,128)(2,1)S(1)}, u32[]{:S(2)}, u32[]{:S(2)}) collective-permute-start(bf16[256,1024]{1,0:T(8,128)(2,1)S(1)} %pad_maximum_fusion), channel_id=1, source_target_pairs={{0,4},{4,0},{8,12},{12,8},{16,20},{20,16},{24,28},{28,24},{32,36},... | collective-permute-start | bytes 1572872 | tf_op jit(solution)/shard_map/ppermute | solution.py:283
  47.6 1.5 %collective-permute-done.17.refs_6_ = bf16[256,1024]{1,0:T(8,128)(2,1)S(1)} collective-permute-done((bf16[256,1024]{1,0:T(8,128)(2,1)S(1)}, bf16[256,1024]{1,0:T(8,128)(2,1)S(1)}, u32[]{:S(2)}, u32[]{:S(2)}) %collective-permute-start.17) | collective-permute-done | bytes 524320 | tf_op jit(solution)/shard_map/ppermute | solution.py:283
  49.2 0.0 collective-permute-done.18.refs_10_
  49.2 0.0 collective-permute-done.19.refs_11_
  49.2 1.9 %shard_map.48 = bf16[64,8192]{1,0:T(8,128)(2,1)} custom-call(s32[9]{0:T(128)S(1)} %get-tuple-element.22.refs_0_, bf16[64,8192]{1,0:T(8,128)(2,1)S(1)} %copy-done, bf16[64,1024]{1,0:T(8,128)(2,1)S(1)} %collective-permute-done.4.refs_2_, bf16[64,1024]{1,0:T(8,128)(2,1)S(1)} %collective-permute-done.8.refs_3_, ...), custom_call_target="tpu_custom_call" | custom-call | flops 536870912 | bytes 65536 | tf_op jit(solution)/shard_map/pallas_call | solution.py:261
  (1 shorter events, 0.0 us)
Async XLA Ops:
  0.0 42.0 %copy-start = (bf16[64,8192]{1,0:T(8,128)(2,1)S(1)}, bf16[64,8192]{1,0:T(8,128)(2,1)}, u32[]{:S(2)}) copy-start(bf16[64,8192]{1,0:T(8,128)(2,1)} %refs_1_.2) | copy-start | bytes 3145732
  0.0 36.9 %collective-permute-start.16 = (bf16[64,8192]{1,0:T(8,128)(2,1)}, bf16[64,8192]{1,0:T(8,128)(2,1)S(1)}, u32[]{:S(2)}, u32[]{:S(2)}) collective-permute-start(bf16[64,8192]{1,0:T(8,128)(2,1)} %refs_1_.2), channel_id=1, source_target_pairs={{0,4},{4,0},{8,12},{12,8},{16,20},{20,16},{24,28},{28,24},{32,36},... | collective-permute-start | bytes 3145736 | tf_op jit(solution)/shard_map/ppermute | solution.py:283
  3.2 6.5 %collective-permute-start = (bf16[64,1024]{1,0:T(8,128)(2,1)}, bf16[64,1024]{1,0:T(8,128)(2,1)S(1)}, u32[]{:S(2)}, u32[]{:S(2)}) collective-permute-start(bf16[64,1024]{1,0:T(8,128)(2,1)} %param.5), channel_id=1, source_target_pairs={{0,64},{4,68},{8,72},{12,76},{16,80},{20,84},{24,88},{28,92},{32,9... | collective-permute-start | bytes 393224 | tf_op jit(solution)/shard_map/ppermute | solution.py:280
  3.2 15.0 %collective-permute-start.1 = (bf16[64,1024]{1,0:T(8,128)(2,1)}, bf16[64,1024]{1,0:T(8,128)(2,1)S(1)}, u32[]{:S(2)}, u32[]{:S(2)}) collective-permute-start(bf16[64,1024]{1,0:T(8,128)(2,1)} %param.5), channel_id=1, source_target_pairs={{0,8},{4,12},{8,16},{12,20},{16,24},{20,28},{24,32},{28,36},{32,40... | collective-permute-start | bytes 393224 | tf_op jit(solution)/shard_map/ppermute | solution.py:280
  4.4 13.8 %collective-permute-start.12 = (bf16[64,1024]{1,0:T(8,128)(2,1)}, bf16[64,1024]{1,0:T(8,128)(2,1)S(1)}, u32[]{:S(2)}, u32[]{:S(2)}) collective-permute-start(bf16[64,1024]{1,0:T(8,128)(2,1)} %param.6), channel_id=1, source_target_pairs={{0,64},{4,68},{8,72},{12,76},{16,80},{20,84},{24,88},{28,92},{32,9... | collective-permute-start | bytes 393224 | tf_op jit(solution)/shard_map/ppermute | solution.py:280
  5.7 14.0 %collective-permute-start.5 = (bf16[64,1024]{1,0:T(8,128)(2,1)}, bf16[64,1024]{1,0:T(8,128)(2,1)S(1)}, u32[]{:S(2)}, u32[]{:S(2)}) collective-permute-start(bf16[64,1024]{1,0:T(8,128)(2,1)} %param.6), channel_id=1, source_target_pairs={{0,8},{4,12},{8,16},{12,20},{16,24},{20,28},{24,32},{28,36},{32,40... | collective-permute-start | bytes 393224 | tf_op jit(solution)/shard_map/ppermute | solution.py:280
  9.8 10.0 %collective-permute-start.9 = (bf16[64,1024]{1,0:T(8,128)(2,1)S(1)}, bf16[64,1024]{1,0:T(8,128)(2,1)S(1)}, u32[]{:S(2)}, u32[]{:S(2)}) collective-permute-start(bf16[64,1024]{1,0:T(8,128)(2,1)S(1)} %collective-permute-done.refs_5_), channel_id=1, source_target_pairs={{0,248},{4,252},{8,0},{12,4},{16,8},{20,12},{24,16},{28,20},{32,24... | collective-permute-start | bytes 393224 | tf_op jit(solution)/shard_map/ppermute | solution.py:280
  18.2 6.3 %collective-permute-start.13 = (bf16[64,1024]{1,0:T(8,128)(2,1)S(1)}, bf16[64,1024]{1,0:T(8,128)(2,1)S(1)}, u32[]{:S(2)}, u32[]{:S(2)}) collective-permute-start(bf16[64,1024]{1,0:T(8,128)(2,1)S(1)} %collective-permute-done.12.refs_6_), channel_id=1, source_target_pairs={{0,248},{4,252},{8,0},{12,4},{16,8},{20,12},{24,16},{28,20},{32,24... | collective-permute-start | bytes 393224 | tf_op jit(solution)/shard_map/ppermute | solution.py:280
  18.2 7.9 %collective-permute-start.2 = (bf16[64,1024]{1,0:T(8,128)(2,1)S(1)}, bf16[64,1024]{1,0:T(8,128)(2,1)S(1)}, u32[]{:S(2)}, u32[]{:S(2)}) collective-permute-start(bf16[64,1024]{1,0:T(8,128)(2,1)S(1)} %collective-permute-done.1.refs_3_), channel_id=1, source_target_pairs={{0,8},{4,12},{8,16},{12,20},{16,24},{20,28},{24,32},{28,36},{32,40... | collective-permute-start | bytes 393224 | tf_op jit(solution)/shard_map/ppermute | solution.py:280
  19.7 8.9 %collective-permute-start.6 = (bf16[64,1024]{1,0:T(8,128)(2,1)S(1)}, bf16[64,1024]{1,0:T(8,128)(2,1)S(1)}, u32[]{:S(2)}, u32[]{:S(2)}) collective-permute-start(bf16[64,1024]{1,0:T(8,128)(2,1)S(1)} %collective-permute-done.5.refs_4_), channel_id=1, source_target_pairs={{0,8},{4,12},{8,16},{12,20},{16,24},{20,28},{24,32},{28,36},{32,40... | collective-permute-start | bytes 393224 | tf_op jit(solution)/shard_map/ppermute | solution.py:280
  19.8 8.8 %collective-permute-start.10 = (bf16[64,1024]{1,0:T(8,128)(2,1)S(1)}, bf16[64,1024]{1,0:T(8,128)(2,1)S(1)}, u32[]{:S(2)}, u32[]{:S(2)}) collective-permute-start(bf16[64,1024]{1,0:T(8,128)(2,1)S(1)} %collective-permute-done.9.refs_9_), channel_id=1, source_target_pairs={{0,248},{4,252},{8,0},{12,4},{16,8},{20,12},{24,16},{28,20},{32,24... | collective-permute-start | bytes 393224 | tf_op jit(solution)/shard_map/ppermute | solution.py:280
  24.5 8.9 %collective-permute-start.14 = (bf16[64,1024]{1,0:T(8,128)(2,1)S(1)}, bf16[64,1024]{1,0:T(8,128)(2,1)S(1)}, u32[]{:S(2)}, u32[]{:S(2)}) collective-permute-start(bf16[64,1024]{1,0:T(8,128)(2,1)S(1)} %collective-permute-done.13.refs_10_), channel_id=1, source_target_pairs={{0,248},{4,252},{8,0},{12,4},{16,8},{20,12},{24,16},{28,20},{32,24... | collective-permute-start | bytes 393224 | tf_op jit(solution)/shard_map/ppermute | solution.py:280
  26.1 8.4 %collective-permute-start.3 = (bf16[64,1024]{1,0:T(8,128)(2,1)S(1)}, bf16[64,1024]{1,0:T(8,128)(2,1)S(1)}, u32[]{:S(2)}, u32[]{:S(2)}) collective-permute-start(bf16[64,1024]{1,0:T(8,128)(2,1)S(1)} %collective-permute-done.2.refs_7_), channel_id=1, source_target_pairs={{0,8},{4,12},{8,16},{12,20},{16,24},{20,28},{24,32},{28,36},{32,40... | collective-permute-start | bytes 393224 | tf_op jit(solution)/shard_map/ppermute | solution.py:280
  28.6 8.3 %collective-permute-start.7 = (bf16[64,1024]{1,0:T(8,128)(2,1)S(1)}, bf16[64,1024]{1,0:T(8,128)(2,1)S(1)}, u32[]{:S(2)}, u32[]{:S(2)}) collective-permute-start(bf16[64,1024]{1,0:T(8,128)(2,1)S(1)} %collective-permute-done.6.refs_8_), channel_id=1, source_target_pairs={{0,8},{4,12},{8,16},{12,20},{16,24},{20,28},{24,32},{28,36},{32,40... | collective-permute-start | bytes 393224 | tf_op jit(solution)/shard_map/ppermute | solution.py:280
  28.6 13.3 %collective-permute-start.11 = (bf16[64,1024]{1,0:T(8,128)(2,1)S(1)}, bf16[64,1024]{1,0:T(8,128)(2,1)S(1)}, u32[]{:S(2)}, u32[]{:S(2)}) collective-permute-start(bf16[64,1024]{1,0:T(8,128)(2,1)S(1)} %collective-permute-done.10.refs_13_), channel_id=1, source_target_pairs={{0,248},{4,252},{8,0},{12,4},{16,8},{20,12},{24,16},{28,20},{32,24... | collective-permute-start | bytes 393224 | tf_op jit(solution)/shard_map/ppermute | solution.py:280
  33.4 11.3 %collective-permute-start.15 = (bf16[64,1024]{1,0:T(8,128)(2,1)S(1)}, bf16[64,1024]{1,0:T(8,128)(2,1)S(1)}, u32[]{:S(2)}, u32[]{:S(2)}) collective-permute-start(bf16[64,1024]{1,0:T(8,128)(2,1)S(1)} %collective-permute-done.14.refs_14_), channel_id=1, source_target_pairs={{0,248},{4,252},{8,0},{12,4},{16,8},{20,12},{24,16},{28,20},{32,24... | collective-permute-start | bytes 393224 | tf_op jit(solution)/shard_map/ppermute | solution.py:280
  34.5 10.2 %collective-permute-start.4 = (bf16[64,1024]{1,0:T(8,128)(2,1)S(1)}, bf16[64,1024]{1,0:T(8,128)(2,1)S(1)}, u32[]{:S(2)}, u32[]{:S(2)}) collective-permute-start(bf16[64,1024]{1,0:T(8,128)(2,1)S(1)} %collective-permute-done.3.refs_11_), channel_id=1, source_target_pairs={{0,8},{4,12},{8,16},{12,20},{16,24},{20,28},{24,32},{28,36},{32,40... | collective-permute-start | bytes 393224 | tf_op jit(solution)/shard_map/ppermute | solution.py:280
  36.9 7.9 %collective-permute-start.8 = (bf16[64,1024]{1,0:T(8,128)(2,1)S(1)}, bf16[64,1024]{1,0:T(8,128)(2,1)S(1)}, u32[]{:S(2)}, u32[]{:S(2)}) collective-permute-start(bf16[64,1024]{1,0:T(8,128)(2,1)S(1)} %collective-permute-done.7.refs_12_), channel_id=1, source_target_pairs={{0,8},{4,12},{8,16},{12,20},{16,24},{20,28},{24,32},{28,36},{32,40... | collective-permute-start | bytes 393224 | tf_op jit(solution)/shard_map/ppermute | solution.py:280
  38.5 10.6 %collective-permute-start.18 = (bf16[640,512]{1,0:T(8,128)(2,1)S(1)}, bf16[640,512]{1,0:T(8,128)(2,1)S(1)}, u32[]{:S(2)}, u32[]{:S(2)}) collective-permute-start(bf16[640,512]{1,0:T(8,128)(2,1)S(1)} %get-tuple-element.26), channel_id=1, source_target_pairs={{0,4},{4,0},{8,12},{12,8},{16,20},{20,16},{24,28},{28,24},{32,36},... | collective-permute-start | bytes 1966088 | tf_op jit(solution)/shard_map/ppermute | solution.py:283
  41.9 7.3 %collective-permute-start.19 = (bf16[640,512]{1,0:T(8,128)(2,1)S(1)}, bf16[640,512]{1,0:T(8,128)(2,1)S(1)}, u32[]{:S(2)}, u32[]{:S(2)}) collective-permute-start(bf16[640,512]{1,0:T(8,128)(2,1)S(1)} %get-tuple-element.27), channel_id=1, source_target_pairs={{0,4},{4,0},{8,12},{12,8},{16,20},{20,16},{24,28},{28,24},{32,36},... | collective-permute-start | bytes 1966088 | tf_op jit(solution)/shard_map/ppermute | solution.py:283
  44.8 4.4 %collective-permute-start.17 = (bf16[256,1024]{1,0:T(8,128)(2,1)S(1)}, bf16[256,1024]{1,0:T(8,128)(2,1)S(1)}, u32[]{:S(2)}, u32[]{:S(2)}) collective-permute-start(bf16[256,1024]{1,0:T(8,128)(2,1)S(1)} %pad_maximum_fusion), channel_id=1, source_target_pairs={{0,4},{4,0},{8,12},{12,8},{16,20},{20,16},{24,28},{28,24},{32,36},... | collective-permute-start | bytes 1572872 | tf_op jit(solution)/shard_map/ppermute | solution.py:283

commit v6 on v5

--- a/solution.py
+++ b/solution.py
@@ -20,7 +20,9 @@
 
 CHIPS = 32
 NEAR = 4
-FAR = 8
+HOPS = ((2, 0), (7, 0), (1, 0), (8, 0), (6, 7), (4, 2), (5, 7), (3, 2))
+EARLY = (0, 1, 2, 8, 7, 6)
+LATE = (4, 5, 3)
 
 
 def chip_route(ahead):
@@ -77,10 +79,10 @@
     return jnp.concatenate(marks, axis=0)
 
 
-def flash_kernel(places, kind, *refs):
+def flash_kernel(blocks, places, kind, *refs):
     n = len(places)
     info_ref, q_ref = refs[:2]
-    n_kv = 5 if kind == "end" else 2 * n - 1
+    n_kv = 1 + max(array for array, _ in blocks)
     kv, refs = refs[2 : 2 + n_kv], refs[2 + n_kv :]
 
     here = info_ref[0]
@@ -100,14 +102,14 @@
     all_reach, near_reach = reach(far), reach(near)
 
     def attend(some):
-        attend_some(some, places, kind, info_ref, q_ref, kv, refs)
+        attend_some(some, blocks, places, kind, info_ref, q_ref, kv, refs)
 
     pl.when(all_reach)(lambda: attend(base + near + far))
     pl.when(near_reach & jnp.logical_not(all_reach))(lambda: attend(base + near))
     pl.when(jnp.logical_not(near_reach))(lambda: attend(base))
 
 
-def attend_some(some, places, kind, info_ref, q_ref, kv, refs):
+def attend_some(some, blocks, places, kind, info_ref, q_ref, kv, refs):
     here = info_ref[0]
     if kind == "lend":
         lent = refs
@@ -118,14 +120,8 @@
         cols = slice(h * DH, (h + 1) * DH)
         parts = []
         for s in some:
-            if kind == "end" and s >= 2:
-                parts.append(kv[4][(2 * (s - 2) + which) * ROWS : (2 * (s - 2) + which + 1) * ROWS, cols])
-            elif kind == "end":
-                parts.append(kv[2 * s + which][:, cols])
-            elif s == 0:
-                parts.append(kv[0][which * ROWS : (which + 1) * ROWS, cols])
-            else:
-                parts.append(kv[2 * s - 1 + which][:, cols])
+            array, row = blocks[s]
+            parts.append(kv[array][row + which * ROWS : row + (which + 1) * ROWS, cols])
         return jnp.concatenate(parts, axis=0)
 
     scores = []
@@ -238,7 +234,7 @@
 HBM = pl.BlockSpec(memory_space=pl.ANY)
 
 
-def flash(kind, info, q, arrays, places):
+def flash(kind, info, q, arrays, blocks, places):
     n = len(places)
     operands = [info, q] + list(arrays)
     in_specs = [SMEM] + [VMEM] * (len(operands) - 1)
@@ -259,7 +255,7 @@
             jax.ShapeDtypeStruct((HK, DH, COLS), jnp.float32),
         )
     return pl.pallas_call(
-        functools.partial(flash_kernel, tuple(places), kind),
+        functools.partial(flash_kernel, tuple(blocks), tuple(places), kind),
         out_shape=out_shape,
         in_specs=in_specs,
         out_specs=out_specs,
@@ -276,36 +272,28 @@
     there = here + 1 - 2 * lax.rem(here, 2)
     info, info_there = (jnp.concatenate([place, doc_lengths]) for place in (here, there))
 
-    def send(block, ahead):
-        return lax.ppermute(block, "seq", chip_route(ahead))
-
     def swap(block):
         return lax.ppermute(block, "seq", SIBLING)
 
-    own = (key_heads, value_heads)
-    near, far = own, own
-    shards = [jnp.concatenate(own, axis=0)]
-    chips = [0]
-    for step in range(NEAR):
-        near = tuple(send(x, 1) for x in near)
-        far = tuple(send(x, FAR if step == 0 else -1) for x in far)
-        if step == 0:
-            first, shards[0], info, info_there = lax.optimization_barrier((far[0], shards[0], info, info_there))
-            far = (first, far[1])
-        if step < NEAR - 1:
-            shards += list(near + far)
-            chips += [step + 1, FAR - step]
-    end = near + far
-    end_chips = [NEAR, FAR - NEAR + 1]
-
-    lent = flash("lend", info_there, swap(queries), shards, [(c, True) for c in chips])
-    got = [swap(x) for x in lent]
+    got = {0: jnp.concatenate([key_heads, value_heads], axis=0)}
+    for chips, source in HOPS:
+        got[chips] = lax.ppermute(got[source], "seq", chip_route(chips - source))
+        if chips == HOPS[0][0]:
+            got[chips], info, info_there = lax.optimization_barrier((got[chips], info, info_there))
+
+    arrays = [got[c] for c in EARLY]
+    blocks = [(i, 0) for i in range(len(EARLY))]
+    lent = flash("lend", info_there, swap(queries), arrays, blocks, [(c, True) for c in EARLY])
+    lent_here = [swap(x) for x in lent]
     q, _ = lax.optimization_barrier((queries, lent))
-    state = flash("own", info, q, shards, [(c, False) for c in chips])
-    end, state = lax.optimization_barrier((end, state))
-    arrays = list(end) + [swap(jnp.concatenate(end, axis=0))] + list(state) + got
-    places = [(c, False) for c in end_chips] + [(c, True) for c in end_chips]
-    return flash("end", info, queries, arrays, places)
+    state = flash("own", info, q, arrays, blocks, [(c, False) for c in EARLY])
+
+    *mid, end = (got[c] for c in LATE)
+    *mid, end, state = lax.optimization_barrier((*mid, end, state))
+    arrays = mid + [end, swap(jnp.concatenate(mid, axis=0)), swap(end)]
+    blocks = [(0, 0), (1, 0), (2, 0), (3, 0), (3, 2 * ROWS), (4, 0)]
+    places = [(c, False) for c in LATE] + [(c, True) for c in LATE]
+    return flash("end", info, queries, arrays + list(state) + lent_here, blocks, places)
 
 
 def solution(mesh):

time: 51.4 us -> 56.1 us (1.091)
  waiting for transfers between devices: 10.2 us -> 27.1 us
  starting transfers between devices: 32.8 us -> 19.6 us
  local copies, waits for them, and re-layouts: 0.01 us -> 1.83 us
  other arithmetic: 1.75 us -> 0.76 us
    ppermute x16 -> x8, waiting for transfers between devices: 8.65 us -> 25.3 us  [per_device(): got[chips] = lax.ppermute(got[source], 'seq', chip_route(chips - source))]
    ppermute x16 -> x8, starting transfers between devices: 23.3 us -> 12.9 us  [per_device(): got[chips] = lax.ppermute(got[source], 'seq', chip_route(chips - source))]
    ppermute x4 -> x5, starting transfers between devices: 9.57 us -> 6.62 us  [swap(): return lax.ppermute(block, 'seq', SIBLING)]
    concatenate x2 -> x1, other arithmetic: 1.02 us -> 0.03 us  [per_device(): arrays = mid + [end, swap(jnp.concatenate(mid, axis=0)), swap(end)]]
    concatenate x0 -> x1, local copies, waits for them, and re-layouts: none -> 0.92 us  [per_device(): got = {0: jnp.concatenate([key_heads, value_heads], axis=0)}]
    unnamed x2 -> x3, local copies, waits for them, and re-layouts: 0.01 us -> 0.92 us
    ppermute x4 -> x5, waiting for transfers between devices: 1.54 us -> 1.82 us  [swap(): return lax.ppermute(block, 'seq', SIBLING)]
  transfers between devices with their start and end apart: 20 -> 13, of which waited for: 5 -> 5; matrix products, arithmetic and copies ran while one was open for 3% -> 5% of each run, Pallas kernels for 8% -> 8%
where the time goes in v6:
time: 56.1 us; the launch traced here: 55.9 us
  waiting for transfers between devices  27.1 us (48%)
  starting transfers between devices  19.6 us (35%)
  Pallas kernels  6.41 us (11%)
  local copies, waits for them, and re-layouts  1.83 us (3%)
  other arithmetic  0.76 us (1%)
    ppermute x8, waiting for transfers between devices, per_device(): got[chips] = lax.ppermute(got[source], 'seq', chip_route(chips - source))  25.3 us
    ppermute x8, starting transfers between devices, per_device(): got[chips] = lax.ppermute(got[source], 'seq', chip_route(chips - source))  12.9 us
    ppermute x5, starting transfers between devices, swap(): return lax.ppermute(block, 'seq', SIBLING)  6.62 us
    pallas_call x3, Pallas kernels, flash(): pl.pallas_call(functools.partial(flash_kernel, tuple(blocks), tuple(place...  6.41 us
    ppermute x5, waiting for transfers between devices, swap(): return lax.ppermute(block, 'seq', SIBLING)  1.82 us
  transfers between devices with their start and end apart: 13, of which 5 were waited for; matrix products, arithmetic and copies ran while one was open for 5% of the time, Pallas kernels for 8%

profile of v6, /device:TPU:1, one launch (start us, length us, event | category | flops | bytes accessed | tf_op | source)
XLA Modules:
  0.0 55.9 jit_solution(480478738557020034)
XLA Ops:
  0.0 0.0 copy-start
  0.0 3.2 %collective-permute-start.5 = (bf16[64,8192]{1,0:T(8,128)(2,1)}, bf16[64,8192]{1,0:T(8,128)(2,1)S(1)}, u32[]{:S(2)}, u32[]{:S(2)}) collective-permute-start(bf16[64,8192]{1,0:T(8,128)(2,1)} %refs_1_.2), channel_id=1, source_target_pairs={{0,4},{4,0},{8,12},{12,8},{16,20},{20,16},{24,28},{28,24},{32,36},... | collective-permute-start | bytes 3145736 | tf_op jit(solution)/shard_map/ppermute | solution.py:276
  3.2 0.9 %constant_dynamic-update-slice_fusion.1 = bf16[128,1024]{1,0:T(8,128)(2,1)S(1)} fusion(bf16[64,1024]{1,0:T(8,128)(2,1)} %param.5), kind=kLoop, calls=%fused_computation.2 | loop fusion | bytes 262144
  4.2 0.9 %constant_dynamic-update-slice_fusion.refs_2_ = bf16[128,1024]{1,0:T(8,128)(2,1)S(1)} fusion(bf16[128,1024]{1,0:T(8,128)(2,1)S(1)} %constant_dynamic-update-slice_fusion.1, bf16[64,1024]{1,0:T(8,128)(2,1)} %param.6), kind=kLoop, calls=%fused_computation.1 | loop fusion | bytes 262144 | tf_op jit(solution)/shard_map/concatenate | solution.py:278
  5.1 3.9 %collective-permute-start.2 = (bf16[128,1024]{1,0:T(8,128)(2,1)S(1)}, bf16[128,1024]{1,0:T(8,128)(2,1)S(1)}, u32[]{:S(2)}, u32[]{:S(2)}) collective-permute-start(bf16[128,1024]{1,0:T(8,128)(2,1)S(1)} %constant_dynamic-update-slice_fusion.refs_2_), channel_id=1, source_target_pairs={{0,56},{4,60},{8,64},{12,68},{16,72},{20,76},{24,80},{28,84},{32,8... | collective-permute-start | bytes 786440 | tf_op jit(solution)/shard_map/ppermute | solution.py:280
  9.0 0.0 collective-permute-start
  9.0 1.3 %collective-permute-start.7 = (bf16[128,1024]{1,0:T(8,128)(2,1)S(1)}, bf16[128,1024]{1,0:T(8,128)(2,1)S(1)}, u32[]{:S(2)}, u32[]{:S(2)}) collective-permute-start(bf16[128,1024]{1,0:T(8,128)(2,1)S(1)} %constant_dynamic-update-slice_fusion.refs_2_), channel_id=1, source_target_pairs={{0,64},{4,68},{8,72},{12,76},{16,80},{20,84},{24,88},{28,92},{32,9... | collective-permute-start | bytes 786440 | tf_op jit(solution)/shard_map/ppermute | solution.py:280
  10.3 0.0 collective-permute-start.6
  10.3 4.9 %collective-permute-done.2.refs_6_ = bf16[128,1024]{1,0:T(8,128)(2,1)S(1)} collective-permute-done((bf16[128,1024]{1,0:T(8,128)(2,1)S(1)}, bf16[128,1024]{1,0:T(8,128)(2,1)S(1)}, u32[]{:S(2)}, u32[]{:S(2)}) %collective-permute-start.2) | collective-permute-done | bytes 262176 | tf_op jit(solution)/shard_map/ppermute | solution.py:280
  15.2 5.3 %collective-permute-start.8 = (bf16[128,1024]{1,0:T(8,128)(2,1)S(1)}, bf16[128,1024]{1,0:T(8,128)(2,1)}, u32[]{:S(2)}, u32[]{:S(2)}) collective-permute-start(bf16[128,1024]{1,0:T(8,128)(2,1)S(1)} %collective-permute-done.2.refs_6_), channel_id=1, source_target_pairs={{0,248},{4,252},{8,0},{12,4},{16,8},{20,12},{24,16},{28,20},{32,24... | collective-permute-start | bytes 786440 | tf_op jit(solution)/shard_map/ppermute | solution.py:280
  20.5 0.7 %pad_add_fusion.1 = (s32[9]{0:T(128)S(1)}, s32[9]{0:T(128)S(1)}) fusion(s32[1]{0:T(128)S(6)} %sub.3, s32[8]{0:T(128)} %param.7, s32[1]{0:T(128)} %bitcast), kind=kLoop, calls=%fused_computation.4 | loop fusion | flops 18 | bytes 112 | tf_op jit(solution)/shard_map/concatenate | solution.py:273
  21.3 3.9 %collective-permute-done.refs_4_ = bf16[128,1024]{1,0:T(8,128)(2,1)S(1)} collective-permute-done((bf16[128,1024]{1,0:T(8,128)(2,1)S(1)}, bf16[128,1024]{1,0:T(8,128)(2,1)S(1)}, u32[]{:S(2)}, u32[]{:S(2)}) %collective-permute-start) | collective-permute-done | bytes 262176 | tf_op jit(solution)/shard_map/ppermute | solution.py:280
  25.1 0.0 collective-permute-start.4
  25.1 12.9 %collective-permute-done.7.refs_5_ = bf16[128,1024]{1,0:T(8,128)(2,1)S(1)} collective-permute-done((bf16[128,1024]{1,0:T(8,128)(2,1)S(1)}, bf16[128,1024]{1,0:T(8,128)(2,1)S(1)}, u32[]{:S(2)}, u32[]{:S(2)}) %collective-permute-start.7) | collective-permute-done | bytes 262176 | tf_op jit(solution)/shard_map/ppermute | solution.py:280
  38.0 0.0 collective-permute-start.3
  38.0 0.0 collective-permute-done.6.refs_3_
  38.0 2.4 %collective-permute-start.1 = (bf16[128,1024]{1,0:T(8,128)(2,1)S(1)}, bf16[128,1024]{1,0:T(8,128)(2,1)S(1)}, u32[]{:S(2)}, u32[]{:S(2)}) collective-permute-start(bf16[128,1024]{1,0:T(8,128)(2,1)S(1)} %collective-permute-done.refs_4_), channel_id=1, source_target_pairs={{0,16},{4,20},{8,24},{12,28},{16,32},{20,36},{24,40},{28,44},{32,4... | collective-permute-start | bytes 786440 | tf_op jit(solution)/shard_map/ppermute | solution.py:280
  40.4 0.0 collective-permute-done.8.refs_7_
  40.4 0.0 collective-permute-done.5.refs_1_
  40.4 2.1 %shard_map.46 = (bf16[640,512]{1,0:T(8,128)(2,1)S(1)}, bf16[640,512]{1,0:T(8,128)(2,1)S(1)}) custom-call(s32[9]{0:T(128)S(1)} %get-tuple-element.22.refs_0_, bf16[64,8192]{1,0:T(8,128)(2,1)S(1)} %collective-permute-done.5.refs_1_, bf16[128,1024]{1,0:T(8,128)(2,1)S(1)} %constant_dynamic-update-slice_fusion.refs_2_, ...), custom_call_target="tpu_custom_call" | custom-call | flops 805306368 | bytes 65536 | tf_op jit(solution)/shard_map/pallas_call | solution.py:257
  42.5 1.6 %collective-permute-start.11 = (bf16[640,512]{1,0:T(8,128)(2,1)S(1)}, bf16[640,512]{1,0:T(8,128)(2,1)S(1)}, u32[]{:S(2)}, u32[]{:S(2)}) collective-permute-start(bf16[640,512]{1,0:T(8,128)(2,1)S(1)} %get-tuple-element.23), channel_id=1, source_target_pairs={{0,4},{4,0},{8,12},{12,8},{16,20},{20,16},{24,28},{28,24},{32,36},... | collective-permute-start | bytes 1966088 | tf_op jit(solution)/shard_map/ppermute | solution.py:276
  44.1 0.3 collective-permute-start.12
  44.3 0.0 copy-done
  44.4 2.4 %shard_map.47 = (f32[8,512]{1,0:T(8,128)S(1)}, f32[8,512]{1,0:T(8,128)S(1)}, f32[8,128,512]{2,1,0:T(8,128)S(1)}) custom-call(s32[9]{0:T(128)S(1)} %get-tuple-element.20.refs_0_, bf16[64,8192]{1,0:T(8,128)(2,1)S(1)} %copy-done, bf16[128,1024]{1,0:T(8,128)(2,1)S(1)} %constant_dynamic-update-slice_fusion.refs_2_, ...), custom_call_target="tpu_custom_call" | custom-call | flops 805306368 | bytes 65536 | tf_op jit(solution)/shard_map/pallas_call | solution.py:257
  46.8 0.0 collective-permute-done.3.refs_3_
  46.8 0.0 collective-permute-done.4.refs_4_
  46.8 3.7 %collective-permute-done.1.refs_2_ = bf16[128,1024]{1,0:T(8,128)(2,1)S(1)} collective-permute-done((bf16[128,1024]{1,0:T(8,128)(2,1)S(1)}, bf16[128,1024]{1,0:T(8,128)(2,1)S(1)}, u32[]{:S(2)}, u32[]{:S(2)}) %collective-permute-start.1) | collective-permute-done | bytes 262176 | tf_op jit(solution)/shard_map/ppermute | solution.py:280
  50.6 1.4 %collective-permute-start.9 = (bf16[256,1024]{1,0:T(8,128)(2,1)S(1)}, bf16[256,1024]{1,0:T(8,128)(2,1)S(1)}, u32[]{:S(2)}, u32[]{:S(2)}) collective-permute-start(bf16[256,1024]{1,0:T(8,128)(2,1)S(1)} %pad_maximum_fusion), channel_id=1, source_target_pairs={{0,4},{4,0},{8,12},{12,8},{16,20},{20,16},{24,28},{28,24},{32,36},... | collective-permute-start | bytes 1572872 | tf_op jit(solution)/shard_map/ppermute | solution.py:276
  52.0 0.1 collective-permute-start.10
  52.1 1.8 %collective-permute-done.10.refs_6_ = bf16[128,1024]{1,0:T(8,128)(2,1)S(1)} collective-permute-done((bf16[128,1024]{1,0:T(8,128)(2,1)S(1)}, bf16[128,1024]{1,0:T(8,128)(2,1)S(1)}, u32[]{:S(2)}, u32[]{:S(2)}) %collective-permute-start.10) | collective-permute-done | bytes 262176 | tf_op jit(solution)/shard_map/ppermute | solution.py:276
  53.9 0.0 collective-permute-done.9.refs_5_
  53.9 0.0 collective-permute-done.11.refs_10_
  53.9 0.0 collective-permute-done.12.refs_11_
  53.9 1.9 %shard_map.48 = bf16[64,8192]{1,0:T(8,128)(2,1)} custom-call(s32[9]{0:T(128)S(1)} %get-tuple-element.20.refs_0_, bf16[64,8192]{1,0:T(8,128)(2,1)S(1)} %copy-done, bf16[128,1024]{1,0:T(8,128)(2,1)S(1)} %collective-permute-done.1.refs_2_, bf16[128,1024]{1,0:T(8,128)(2,1)S(1)} %collective-permute-done.3.refs_3_, ...), custom_call_target="tpu_custom_call" | custom-call | flops 805306368 | bytes 65536 | tf_op jit(solution)/shard_map/pallas_call | solution.py:257
  (1 shorter events, 0.0 us)
Async XLA Ops:
  0.0 44.4 %copy-start = (bf16[64,8192]{1,0:T(8,128)(2,1)S(1)}, bf16[64,8192]{1,0:T(8,128)(2,1)}, u32[]{:S(2)}) copy-start(bf16[64,8192]{1,0:T(8,128)(2,1)} %refs_1_.2) | copy-start | bytes 3145732
  0.0 40.4 %collective-permute-start.5 = (bf16[64,8192]{1,0:T(8,128)(2,1)}, bf16[64,8192]{1,0:T(8,128)(2,1)S(1)}, u32[]{:S(2)}, u32[]{:S(2)}) collective-permute-start(bf16[64,8192]{1,0:T(8,128)(2,1)} %refs_1_.2), channel_id=1, source_target_pairs={{0,4},{4,0},{8,12},{12,8},{16,20},{20,16},{24,28},{28,24},{32,36},... | collective-permute-start | bytes 3145736 | tf_op jit(solution)/shard_map/ppermute | solution.py:276
  5.1 10.1 %collective-permute-start.2 = (bf16[128,1024]{1,0:T(8,128)(2,1)S(1)}, bf16[128,1024]{1,0:T(8,128)(2,1)S(1)}, u32[]{:S(2)}, u32[]{:S(2)}) collective-permute-start(bf16[128,1024]{1,0:T(8,128)(2,1)S(1)} %constant_dynamic-update-slice_fusion.refs_2_), channel_id=1, source_target_pairs={{0,56},{4,60},{8,64},{12,68},{16,72},{20,76},{24,80},{28,84},{32,8... | collective-permute-start | bytes 786440 | tf_op jit(solution)/shard_map/ppermute | solution.py:280
  9.0 16.1 %collective-permute-start = (bf16[128,1024]{1,0:T(8,128)(2,1)S(1)}, bf16[128,1024]{1,0:T(8,128)(2,1)S(1)}, u32[]{:S(2)}, u32[]{:S(2)}) collective-permute-start(bf16[128,1024]{1,0:T(8,128)(2,1)S(1)} %constant_dynamic-update-slice_fusion.refs_2_), channel_id=1, source_target_pairs={{0,16},{4,20},{8,24},{12,28},{16,32},{20,36},{24,40},{28,44},{32,4... | collective-permute-start | bytes 786440 | tf_op jit(solution)/shard_map/ppermute | solution.py:280
  9.0 29.0 %collective-permute-start.7 = (bf16[128,1024]{1,0:T(8,128)(2,1)S(1)}, bf16[128,1024]{1,0:T(8,128)(2,1)S(1)}, u32[]{:S(2)}, u32[]{:S(2)}) collective-permute-start(bf16[128,1024]{1,0:T(8,128)(2,1)S(1)} %constant_dynamic-update-slice_fusion.refs_2_), channel_id=1, source_target_pairs={{0,64},{4,68},{8,72},{12,76},{16,80},{20,84},{24,88},{28,92},{32,9... | collective-permute-start | bytes 786440 | tf_op jit(solution)/shard_map/ppermute | solution.py:280
  10.3 27.7 %collective-permute-start.6 = (bf16[128,1024]{1,0:T(8,128)(2,1)S(1)}, bf16[128,1024]{1,0:T(8,128)(2,1)S(1)}, u32[]{:S(2)}, u32[]{:S(2)}) collective-permute-start(bf16[128,1024]{1,0:T(8,128)(2,1)S(1)} %constant_dynamic-update-slice_fusion.refs_2_), channel_id=1, source_target_pairs={{0,8},{4,12},{8,16},{12,20},{16,24},{20,28},{24,32},{28,36},{32,40... | collective-permute-start | bytes 786440 | tf_op jit(solution)/shard_map/ppermute | solution.py:280
  15.2 25.2 %collective-permute-start.8 = (bf16[128,1024]{1,0:T(8,128)(2,1)S(1)}, bf16[128,1024]{1,0:T(8,128)(2,1)}, u32[]{:S(2)}, u32[]{:S(2)}) collective-permute-start(bf16[128,1024]{1,0:T(8,128)(2,1)S(1)} %collective-permute-done.2.refs_6_), channel_id=1, source_target_pairs={{0,248},{4,252},{8,0},{12,4},{16,8},{20,12},{24,16},{28,20},{32,24... | collective-permute-start | bytes 786440 | tf_op jit(solution)/shard_map/ppermute | solution.py:280
  25.1 21.7 %collective-permute-start.4 = (bf16[128,1024]{1,0:T(8,128)(2,1)S(1)}, bf16[128,1024]{1,0:T(8,128)(2,1)S(1)}, u32[]{:S(2)}, u32[]{:S(2)}) collective-permute-start(bf16[128,1024]{1,0:T(8,128)(2,1)S(1)} %collective-permute-done.refs_4_), channel_id=1, source_target_pairs={{0,8},{4,12},{8,16},{12,20},{16,24},{20,28},{24,32},{28,36},{32,40... | collective-permute-start | bytes 786440 | tf_op jit(solution)/shard_map/ppermute | solution.py:280
  38.0 8.8 %collective-permute-start.3 = (bf16[128,1024]{1,0:T(8,128)(2,1)S(1)}, bf16[128,1024]{1,0:T(8,128)(2,1)S(1)}, u32[]{:S(2)}, u32[]{:S(2)}) collective-permute-start(bf16[128,1024]{1,0:T(8,128)(2,1)S(1)} %collective-permute-done.2.refs_6_), channel_id=1, source_target_pairs={{0,240},{4,244},{8,248},{12,252},{16,0},{20,4},{24,8},{28,12},{32,... | collective-permute-start | bytes 786440 | tf_op jit(solution)/shard_map/ppermute | solution.py:280
  38.0 12.5 %collective-permute-start.1 = (bf16[128,1024]{1,0:T(8,128)(2,1)S(1)}, bf16[128,1024]{1,0:T(8,128)(2,1)S(1)}, u32[]{:S(2)}, u32[]{:S(2)}) collective-permute-start(bf16[128,1024]{1,0:T(8,128)(2,1)S(1)} %collective-permute-done.refs_4_), channel_id=1, source_target_pairs={{0,16},{4,20},{8,24},{12,28},{16,32},{20,36},{24,40},{28,44},{32,4... | collective-permute-start | bytes 786440 | tf_op jit(solution)/shard_map/ppermute | solution.py:280
  42.5 11.4 %collective-permute-start.11 = (bf16[640,512]{1,0:T(8,128)(2,1)S(1)}, bf16[640,512]{1,0:T(8,128)(2,1)S(1)}, u32[]{:S(2)}, u32[]{:S(2)}) collective-permute-start(bf16[640,512]{1,0:T(8,128)(2,1)S(1)} %get-tuple-element.23), channel_id=1, source_target_pairs={{0,4},{4,0},{8,12},{12,8},{16,20},{20,16},{24,28},{28,24},{32,36},... | collective-permute-start | bytes 1966088 | tf_op jit(solution)/shard_map/ppermute | solution.py:276
  44.1 9.8 %collective-permute-start.12 = (bf16[640,512]{1,0:T(8,128)(2,1)S(1)}, bf16[640,512]{1,0:T(8,128)(2,1)S(1)}, u32[]{:S(2)}, u32[]{:S(2)}) collective-permute-start(bf16[640,512]{1,0:T(8,128)(2,1)S(1)} %get-tuple-element.24), channel_id=1, source_target_pairs={{0,4},{4,0},{8,12},{12,8},{16,20},{20,16},{24,28},{28,24},{32,36},... | collective-permute-start | bytes 1966088 | tf_op jit(solution)/shard_map/ppermute | solution.py:276
  50.6 3.3 %collective-permute-start.9 = (bf16[256,1024]{1,0:T(8,128)(2,1)S(1)}, bf16[256,1024]{1,0:T(8,128)(2,1)S(1)}, u32[]{:S(2)}, u32[]{:S(2)}) collective-permute-start(bf16[256,1024]{1,0:T(8,128)(2,1)S(1)} %pad_maximum_fusion), channel_id=1, source_target_pairs={{0,4},{4,0},{8,12},{12,8},{16,20},{20,16},{24,28},{28,24},{32,36},... | collective-permute-start | bytes 1572872 | tf_op jit(solution)/shard_map/ppermute | solution.py:276
  52.0 1.9 %collective-permute-start.10 = (bf16[128,1024]{1,0:T(8,128)(2,1)S(1)}, bf16[128,1024]{1,0:T(8,128)(2,1)S(1)}, u32[]{:S(2)}, u32[]{:S(2)}) collective-permute-start(bf16[128,1024]{1,0:T(8,128)(2,1)S(1)} %collective-permute-done.4.refs_4_), channel_id=1, source_target_pairs={{0,4},{4,0},{8,12},{12,8},{16,20},{20,16},{24,28},{28,24},{32,36},... | collective-permute-start | bytes 786440 | tf_op jit(solution)/shard_map/ppermute | solution.py:276

commit v7 on v5

--- a/solution.py
+++ b/solution.py
@@ -153,7 +153,7 @@
         top = jnp.max(scores[h], axis=0, keepdims=True)
         if kind == "end":
             top = jnp.maximum(top, known[h : h + 1, :])
-        weight = jnp.exp2(scores[h] * RATE - top * RATE)
+        weight = jnp.exp2((scores[h] - top) * RATE)
         tops.append(top)
         totals.append(jnp.sum(weight, axis=0, keepdims=True))
         weights.append(weight.astype(jnp.bfloat16))

time: 51.4 us -> 51.6 us (level)
  no operation moved by 1% of the time
where the time goes in v7:
time: 51.6 us; the launch traced here: 51.5 us
  starting transfers between devices  33.2 us (64%)
  waiting for transfers between devices  10.2 us (20%)
  Pallas kernels  6.11 us (12%)
  other arithmetic  1.75 us (3%)
    ppermute x16, starting transfers between devices, send(): return lax.ppermute(block, 'seq', chip_route(ahead))  23.3 us
    ppermute x4, starting transfers between devices, swap(): return lax.ppermute(block, 'seq', SIBLING)  9.91 us
    ppermute x16, waiting for transfers between devices, send(): return lax.ppermute(block, 'seq', chip_route(ahead))  8.65 us
    pallas_call x3, Pallas kernels, flash(): pl.pallas_call(functools.partial(flash_kernel, tuple(places), kind), out_...  6.11 us
    ppermute x4, waiting for transfers between devices, swap(): return lax.ppermute(block, 'seq', SIBLING)  1.54 us
  transfers between devices with their start and end apart: 20, of which 5 were waited for; matrix products, arithmetic and copies ran while one was open for 3% of the time, Pallas kernels for 8%

profile of v7, /device:TPU:1, one launch (start us, length us, event | category | flops | bytes accessed | tf_op | source)
XLA Modules:
  0.0 51.5 jit_solution(557049252611767386)
XLA Ops:
  0.0 0.0 copy-start
  0.0 3.2 %collective-permute-start.16 = (bf16[64,8192]{1,0:T(8,128)(2,1)}, bf16[64,8192]{1,0:T(8,128)(2,1)S(1)}, u32[]{:S(2)}, u32[]{:S(2)}) collective-permute-start(bf16[64,8192]{1,0:T(8,128)(2,1)} %refs_1_.2), channel_id=1, source_target_pairs={{0,4},{4,0},{8,12},{12,8},{16,20},{20,16},{24,28},{28,24},{32,36},... | collective-permute-start | bytes 3145736 | tf_op jit(solution)/shard_map/ppermute | solution.py:283
  3.2 0.0 collective-permute-start
  3.2 1.2 %collective-permute-start.1 = (bf16[64,1024]{1,0:T(8,128)(2,1)}, bf16[64,1024]{1,0:T(8,128)(2,1)S(1)}, u32[]{:S(2)}, u32[]{:S(2)}) collective-permute-start(bf16[64,1024]{1,0:T(8,128)(2,1)} %param.5), channel_id=1, source_target_pairs={{0,8},{4,12},{8,16},{12,20},{16,24},{20,28},{24,32},{28,36},{32,40... | collective-permute-start | bytes 393224 | tf_op jit(solution)/shard_map/ppermute | solution.py:280
  4.4 1.3 %collective-permute-start.12 = (bf16[64,1024]{1,0:T(8,128)(2,1)}, bf16[64,1024]{1,0:T(8,128)(2,1)S(1)}, u32[]{:S(2)}, u32[]{:S(2)}) collective-permute-start(bf16[64,1024]{1,0:T(8,128)(2,1)} %param.6), channel_id=1, source_target_pairs={{0,64},{4,68},{8,72},{12,76},{16,80},{20,84},{24,88},{28,92},{32,9... | collective-permute-start | bytes 393224 | tf_op jit(solution)/shard_map/ppermute | solution.py:280
  5.7 1.6 %collective-permute-start.5 = (bf16[64,1024]{1,0:T(8,128)(2,1)}, bf16[64,1024]{1,0:T(8,128)(2,1)S(1)}, u32[]{:S(2)}, u32[]{:S(2)}) collective-permute-start(bf16[64,1024]{1,0:T(8,128)(2,1)} %param.6), channel_id=1, source_target_pairs={{0,8},{4,12},{8,16},{12,20},{16,24},{20,28},{24,32},{28,36},{32,40... | collective-permute-start | bytes 393224 | tf_op jit(solution)/shard_map/ppermute | solution.py:280
  7.4 1.0 %pad_maximum_fusion.1.refs_2_ = bf16[128,1024]{1,0:T(8,128)(2,1)S(1)} fusion(bf16[64,1024]{1,0:T(8,128)(2,1)} %param.6, bf16[64,1024]{1,0:T(8,128)(2,1)} %param.5), kind=kLoop, calls=%fused_computation.1 | loop fusion | flops 524288 | bytes 524288 | tf_op jit(solution)/shard_map/concatenate | solution.py:287
  8.4 0.7 %pad_add_fusion.1 = (s32[9]{0:T(128)S(1)}, s32[9]{0:T(128)S(1)}) fusion(s32[1]{0:T(128)S(6)} %sub.3, s32[8]{0:T(128)} %param.7, s32[1]{0:T(128)} %bitcast), kind=kLoop, calls=%fused_computation.3 | loop fusion | flops 18 | bytes 112 | tf_op jit(solution)/shard_map/concatenate | solution.py:277
  9.1 0.7 %collective-permute-done.refs_5_ = bf16[64,1024]{1,0:T(8,128)(2,1)S(1)} collective-permute-done((bf16[64,1024]{1,0:T(8,128)(2,1)}, bf16[64,1024]{1,0:T(8,128)(2,1)S(1)}, u32[]{:S(2)}, u32[]{:S(2)}) %collective-permute-start) | collective-permute-done | bytes 131104 | tf_op jit(solution)/shard_map/ppermute | solution.py:280
  9.8 5.0 %collective-permute-start.9 = (bf16[64,1024]{1,0:T(8,128)(2,1)S(1)}, bf16[64,1024]{1,0:T(8,128)(2,1)S(1)}, u32[]{:S(2)}, u32[]{:S(2)}) collective-permute-start(bf16[64,1024]{1,0:T(8,128)(2,1)S(1)} %collective-permute-done.refs_5_), channel_id=1, source_target_pairs={{0,248},{4,252},{8,0},{12,4},{16,8},{20,12},{24,16},{28,20},{32,24... | collective-permute-start | bytes 393224 | tf_op jit(solution)/shard_map/ppermute | solution.py:280
  14.8 3.4 %collective-permute-done.12.refs_6_ = bf16[64,1024]{1,0:T(8,128)(2,1)S(1)} collective-permute-done((bf16[64,1024]{1,0:T(8,128)(2,1)}, bf16[64,1024]{1,0:T(8,128)(2,1)S(1)}, u32[]{:S(2)}, u32[]{:S(2)}) %collective-permute-start.12) | collective-permute-done | bytes 131104 | tf_op jit(solution)/shard_map/ppermute | solution.py:280
  18.2 0.0 collective-permute-start.13
  18.2 0.0 collective-permute-done.1.refs_3_
  18.2 1.5 %collective-permute-start.2 = (bf16[64,1024]{1,0:T(8,128)(2,1)S(1)}, bf16[64,1024]{1,0:T(8,128)(2,1)S(1)}, u32[]{:S(2)}, u32[]{:S(2)}) collective-permute-start(bf16[64,1024]{1,0:T(8,128)(2,1)S(1)} %collective-permute-done.1.refs_3_), channel_id=1, source_target_pairs={{0,8},{4,12},{8,16},{12,20},{16,24},{20,28},{24,32},{28,36},{32,40... | collective-permute-start | bytes 393224 | tf_op jit(solution)/shard_map/ppermute | solution.py:280
  19.7 0.0 collective-permute-done.5.refs_4_
  19.7 0.1 collective-permute-start.6
  19.8 0.0 collective-permute-done.9.refs_9_
  19.8 4.7 %collective-permute-start.10 = (bf16[64,1024]{1,0:T(8,128)(2,1)S(1)}, bf16[64,1024]{1,0:T(8,128)(2,1)S(1)}, u32[]{:S(2)}, u32[]{:S(2)}) collective-permute-start(bf16[64,1024]{1,0:T(8,128)(2,1)S(1)} %collective-permute-done.9.refs_9_), channel_id=1, source_target_pairs={{0,248},{4,252},{8,0},{12,4},{16,8},{20,12},{24,16},{28,20},{32,24... | collective-permute-start | bytes 393224 | tf_op jit(solution)/shard_map/ppermute | solution.py:280
  24.5 0.0 collective-permute-done.13.refs_10_
  24.5 1.6 %collective-permute-start.14 = (bf16[64,1024]{1,0:T(8,128)(2,1)S(1)}, bf16[64,1024]{1,0:T(8,128)(2,1)S(1)}, u32[]{:S(2)}, u32[]{:S(2)}) collective-permute-start(bf16[64,1024]{1,0:T(8,128)(2,1)S(1)} %collective-permute-done.13.refs_10_), channel_id=1, source_target_pairs={{0,248},{4,252},{8,0},{12,4},{16,8},{20,12},{24,16},{28,20},{32,24... | collective-permute-start | bytes 393224 | tf_op jit(solution)/shard_map/ppermute | solution.py:280
  26.1 0.0 collective-permute-done.2.refs_7_
  26.1 0.0 collective-permute-start.3
  26.1 2.5 %collective-permute-done.6.refs_8_ = bf16[64,1024]{1,0:T(8,128)(2,1)S(1)} collective-permute-done((bf16[64,1024]{1,0:T(8,128)(2,1)S(1)}, bf16[64,1024]{1,0:T(8,128)(2,1)S(1)}, u32[]{:S(2)}, u32[]{:S(2)}) %collective-permute-start.6) | collective-permute-done | bytes 131104 | tf_op jit(solution)/shard_map/ppermute | solution.py:280
  28.6 0.0 collective-permute-start.7
  28.6 0.0 collective-permute-done.10.refs_13_
  28.6 4.8 %collective-permute-start.11 = (bf16[64,1024]{1,0:T(8,128)(2,1)S(1)}, bf16[64,1024]{1,0:T(8,128)(2,1)S(1)}, u32[]{:S(2)}, u32[]{:S(2)}) collective-permute-start(bf16[64,1024]{1,0:T(8,128)(2,1)S(1)} %collective-permute-done.10.refs_13_), channel_id=1, source_target_pairs={{0,248},{4,252},{8,0},{12,4},{16,8},{20,12},{24,16},{28,20},{32,24... | collective-permute-start | bytes 393224 | tf_op jit(solution)/shard_map/ppermute | solution.py:280
  33.4 0.0 collective-permute-done.14.refs_14_
  33.4 1.2 %collective-permute-start.15 = (bf16[64,1024]{1,0:T(8,128)(2,1)S(1)}, bf16[64,1024]{1,0:T(8,128)(2,1)S(1)}, u32[]{:S(2)}, u32[]{:S(2)}) collective-permute-start(bf16[64,1024]{1,0:T(8,128)(2,1)S(1)} %collective-permute-done.14.refs_14_), channel_id=1, source_target_pairs={{0,248},{4,252},{8,0},{12,4},{16,8},{20,12},{24,16},{28,20},{32,24... | collective-permute-start | bytes 393224 | tf_op jit(solution)/shard_map/ppermute | solution.py:280
  34.5 0.0 collective-permute-done.3.refs_11_
  34.5 0.3 collective-permute-start.4
  34.9 2.0 %collective-permute-done.7.refs_12_ = bf16[64,1024]{1,0:T(8,128)(2,1)S(1)} collective-permute-done((bf16[64,1024]{1,0:T(8,128)(2,1)S(1)}, bf16[64,1024]{1,0:T(8,128)(2,1)S(1)}, u32[]{:S(2)}, u32[]{:S(2)}) %collective-permute-start.7) | collective-permute-done | bytes 131104 | tf_op jit(solution)/shard_map/ppermute | solution.py:280
  36.9 0.0 collective-permute-start.8
  36.9 0.0 collective-permute-done.16.refs_1_
  36.9 1.6 %shard_map.46 = (bf16[640,512]{1,0:T(8,128)(2,1)S(1)}, bf16[640,512]{1,0:T(8,128)(2,1)S(1)}) custom-call(s32[9]{0:T(128)S(1)} %get-tuple-element.24.refs_0_, bf16[64,8192]{1,0:T(8,128)(2,1)S(1)} %collective-permute-done.16.refs_1_, bf16[128,1024]{1,0:T(8,128)(2,1)S(1)} %pad_maximum_fusion.1.refs_2_, bf16[64,1024]{1,0:T(8,128)(2,1)S(1)} %collective-permute-done.1.refs_3_, ...), custom_call_target="tpu_custom_call" | custom-call | flops 939524096 | bytes 65536 | tf_op jit(solution)/shard_map/pallas_call | solution.py:261
  38.5 3.2 %collective-permute-start.18 = (bf16[640,512]{1,0:T(8,128)(2,1)S(1)}, bf16[640,512]{1,0:T(8,128)(2,1)S(1)}, u32[]{:S(2)}, u32[]{:S(2)}) collective-permute-start(bf16[640,512]{1,0:T(8,128)(2,1)S(1)} %get-tuple-element.26), channel_id=1, source_target_pairs={{0,4},{4,0},{8,12},{12,8},{16,20},{20,16},{24,28},{28,24},{32,36},... | collective-permute-start | bytes 1966088 | tf_op jit(solution)/shard_map/ppermute | solution.py:283
  41.7 0.0 collective-permute-done.11.refs_4_
  41.7 0.1 collective-permute-start.19
  41.8 0.0 copy-done
  41.8 2.4 %shard_map.47 = (f32[8,512]{1,0:T(8,128)S(1)}, f32[8,512]{1,0:T(8,128)S(1)}, f32[8,128,512]{2,1,0:T(8,128)S(1)}) custom-call(s32[9]{0:T(128)S(1)} %get-tuple-element.22.refs_0_, bf16[64,8192]{1,0:T(8,128)(2,1)S(1)} %copy-done, bf16[128,1024]{1,0:T(8,128)(2,1)S(1)} %pad_maximum_fusion.1.refs_2_, bf16[64,1024]{1,0:T(8,128)(2,1)S(1)} %collective-permute-done.1.refs_3_, ...), custom_call_target="tpu_custom_call" | custom-call | flops 939524096 | bytes 65536 | tf_op jit(solution)/shard_map/pallas_call | solution.py:261
  44.2 0.0 collective-permute-done.15.refs_5_
  44.2 0.0 collective-permute-done.4.refs_2_
  44.2 0.0 collective-permute-done.8.refs_3_
  44.3 3.4 %collective-permute-start.17 = (bf16[256,1024]{1,0:T(8,128)(2,1)S(1)}, bf16[256,1024]{1,0:T(8,128)(2,1)S(1)}, u32[]{:S(2)}, u32[]{:S(2)}) collective-permute-start(bf16[256,1024]{1,0:T(8,128)(2,1)S(1)} %pad_maximum_fusion), channel_id=1, source_target_pairs={{0,4},{4,0},{8,12},{12,8},{16,20},{20,16},{24,28},{28,24},{32,36},... | collective-permute-start | bytes 1572872 | tf_op jit(solution)/shard_map/ppermute | solution.py:283
  47.6 1.5 %collective-permute-done.17.refs_6_ = bf16[256,1024]{1,0:T(8,128)(2,1)S(1)} collective-permute-done((bf16[256,1024]{1,0:T(8,128)(2,1)S(1)}, bf16[256,1024]{1,0:T(8,128)(2,1)S(1)}, u32[]{:S(2)}, u32[]{:S(2)}) %collective-permute-start.17) | collective-permute-done | bytes 524320 | tf_op jit(solution)/shard_map/ppermute | solution.py:283
  49.2 0.0 collective-permute-done.18.refs_10_
  49.2 0.0 collective-permute-done.19.refs_11_
  49.2 2.1 %shard_map.48 = bf16[64,8192]{1,0:T(8,128)(2,1)} custom-call(s32[9]{0:T(128)S(1)} %get-tuple-element.22.refs_0_, bf16[64,8192]{1,0:T(8,128)(2,1)S(1)} %copy-done, bf16[64,1024]{1,0:T(8,128)(2,1)S(1)} %collective-permute-done.4.refs_2_, bf16[64,1024]{1,0:T(8,128)(2,1)S(1)} %collective-permute-done.8.refs_3_, ...), custom_call_target="tpu_custom_call" | custom-call | flops 536870912 | bytes 65536 | tf_op jit(solution)/shard_map/pallas_call | solution.py:261
  (1 shorter events, 0.0 us)
Async XLA Ops:
  0.0 41.8 %copy-start = (bf16[64,8192]{1,0:T(8,128)(2,1)S(1)}, bf16[64,8192]{1,0:T(8,128)(2,1)}, u32[]{:S(2)}) copy-start(bf16[64,8192]{1,0:T(8,128)(2,1)} %refs_1_.2) | copy-start | bytes 3145732
  0.0 36.9 %collective-permute-start.16 = (bf16[64,8192]{1,0:T(8,128)(2,1)}, bf16[64,8192]{1,0:T(8,128)(2,1)S(1)}, u32[]{:S(2)}, u32[]{:S(2)}) collective-permute-start(bf16[64,8192]{1,0:T(8,128)(2,1)} %refs_1_.2), channel_id=1, source_target_pairs={{0,4},{4,0},{8,12},{12,8},{16,20},{20,16},{24,28},{28,24},{32,36},... | collective-permute-start | bytes 3145736 | tf_op jit(solution)/shard_map/ppermute | solution.py:283
  3.2 6.5 %collective-permute-start = (bf16[64,1024]{1,0:T(8,128)(2,1)}, bf16[64,1024]{1,0:T(8,128)(2,1)S(1)}, u32[]{:S(2)}, u32[]{:S(2)}) collective-permute-start(bf16[64,1024]{1,0:T(8,128)(2,1)} %param.5), channel_id=1, source_target_pairs={{0,64},{4,68},{8,72},{12,76},{16,80},{20,84},{24,88},{28,92},{32,9... | collective-permute-start | bytes 393224 | tf_op jit(solution)/shard_map/ppermute | solution.py:280
  3.2 15.0 %collective-permute-start.1 = (bf16[64,1024]{1,0:T(8,128)(2,1)}, bf16[64,1024]{1,0:T(8,128)(2,1)S(1)}, u32[]{:S(2)}, u32[]{:S(2)}) collective-permute-start(bf16[64,1024]{1,0:T(8,128)(2,1)} %param.5), channel_id=1, source_target_pairs={{0,8},{4,12},{8,16},{12,20},{16,24},{20,28},{24,32},{28,36},{32,40... | collective-permute-start | bytes 393224 | tf_op jit(solution)/shard_map/ppermute | solution.py:280
  4.4 13.8 %collective-permute-start.12 = (bf16[64,1024]{1,0:T(8,128)(2,1)}, bf16[64,1024]{1,0:T(8,128)(2,1)S(1)}, u32[]{:S(2)}, u32[]{:S(2)}) collective-permute-start(bf16[64,1024]{1,0:T(8,128)(2,1)} %param.6), channel_id=1, source_target_pairs={{0,64},{4,68},{8,72},{12,76},{16,80},{20,84},{24,88},{28,92},{32,9... | collective-permute-start | bytes 393224 | tf_op jit(solution)/shard_map/ppermute | solution.py:280
  5.7 14.0 %collective-permute-start.5 = (bf16[64,1024]{1,0:T(8,128)(2,1)}, bf16[64,1024]{1,0:T(8,128)(2,1)S(1)}, u32[]{:S(2)}, u32[]{:S(2)}) collective-permute-start(bf16[64,1024]{1,0:T(8,128)(2,1)} %param.6), channel_id=1, source_target_pairs={{0,8},{4,12},{8,16},{12,20},{16,24},{20,28},{24,32},{28,36},{32,40... | collective-permute-start | bytes 393224 | tf_op jit(solution)/shard_map/ppermute | solution.py:280
  9.8 10.0 %collective-permute-start.9 = (bf16[64,1024]{1,0:T(8,128)(2,1)S(1)}, bf16[64,1024]{1,0:T(8,128)(2,1)S(1)}, u32[]{:S(2)}, u32[]{:S(2)}) collective-permute-start(bf16[64,1024]{1,0:T(8,128)(2,1)S(1)} %collective-permute-done.refs_5_), channel_id=1, source_target_pairs={{0,248},{4,252},{8,0},{12,4},{16,8},{20,12},{24,16},{28,20},{32,24... | collective-permute-start | bytes 393224 | tf_op jit(solution)/shard_map/ppermute | solution.py:280
  18.2 6.3 %collective-permute-start.13 = (bf16[64,1024]{1,0:T(8,128)(2,1)S(1)}, bf16[64,1024]{1,0:T(8,128)(2,1)S(1)}, u32[]{:S(2)}, u32[]{:S(2)}) collective-permute-start(bf16[64,1024]{1,0:T(8,128)(2,1)S(1)} %collective-permute-done.12.refs_6_), channel_id=1, source_target_pairs={{0,248},{4,252},{8,0},{12,4},{16,8},{20,12},{24,16},{28,20},{32,24... | collective-permute-start | bytes 393224 | tf_op jit(solution)/shard_map/ppermute | solution.py:280
  18.2 7.9 %collective-permute-start.2 = (bf16[64,1024]{1,0:T(8,128)(2,1)S(1)}, bf16[64,1024]{1,0:T(8,128)(2,1)S(1)}, u32[]{:S(2)}, u32[]{:S(2)}) collective-permute-start(bf16[64,1024]{1,0:T(8,128)(2,1)S(1)} %collective-permute-done.1.refs_3_), channel_id=1, source_target_pairs={{0,8},{4,12},{8,16},{12,20},{16,24},{20,28},{24,32},{28,36},{32,40... | collective-permute-start | bytes 393224 | tf_op jit(solution)/shard_map/ppermute | solution.py:280
  19.7 8.9 %collective-permute-start.6 = (bf16[64,1024]{1,0:T(8,128)(2,1)S(1)}, bf16[64,1024]{1,0:T(8,128)(2,1)S(1)}, u32[]{:S(2)}, u32[]{:S(2)}) collective-permute-start(bf16[64,1024]{1,0:T(8,128)(2,1)S(1)} %collective-permute-done.5.refs_4_), channel_id=1, source_target_pairs={{0,8},{4,12},{8,16},{12,20},{16,24},{20,28},{24,32},{28,36},{32,40... | collective-permute-start | bytes 393224 | tf_op jit(solution)/shard_map/ppermute | solution.py:280
  19.8 8.8 %collective-permute-start.10 = (bf16[64,1024]{1,0:T(8,128)(2,1)S(1)}, bf16[64,1024]{1,0:T(8,128)(2,1)S(1)}, u32[]{:S(2)}, u32[]{:S(2)}) collective-permute-start(bf16[64,1024]{1,0:T(8,128)(2,1)S(1)} %collective-permute-done.9.refs_9_), channel_id=1, source_target_pairs={{0,248},{4,252},{8,0},{12,4},{16,8},{20,12},{24,16},{28,20},{32,24... | collective-permute-start | bytes 393224 | tf_op jit(solution)/shard_map/ppermute | solution.py:280
  24.5 8.9 %collective-permute-start.14 = (bf16[64,1024]{1,0:T(8,128)(2,1)S(1)}, bf16[64,1024]{1,0:T(8,128)(2,1)S(1)}, u32[]{:S(2)}, u32[]{:S(2)}) collective-permute-start(bf16[64,1024]{1,0:T(8,128)(2,1)S(1)} %collective-permute-done.13.refs_10_), channel_id=1, source_target_pairs={{0,248},{4,252},{8,0},{12,4},{16,8},{20,12},{24,16},{28,20},{32,24... | collective-permute-start | bytes 393224 | tf_op jit(solution)/shard_map/ppermute | solution.py:280
  26.1 8.4 %collective-permute-start.3 = (bf16[64,1024]{1,0:T(8,128)(2,1)S(1)}, bf16[64,1024]{1,0:T(8,128)(2,1)S(1)}, u32[]{:S(2)}, u32[]{:S(2)}) collective-permute-start(bf16[64,1024]{1,0:T(8,128)(2,1)S(1)} %collective-permute-done.2.refs_7_), channel_id=1, source_target_pairs={{0,8},{4,12},{8,16},{12,20},{16,24},{20,28},{24,32},{28,36},{32,40... | collective-permute-start | bytes 393224 | tf_op jit(solution)/shard_map/ppermute | solution.py:280
  28.6 8.3 %collective-permute-start.7 = (bf16[64,1024]{1,0:T(8,128)(2,1)S(1)}, bf16[64,1024]{1,0:T(8,128)(2,1)S(1)}, u32[]{:S(2)}, u32[]{:S(2)}) collective-permute-start(bf16[64,1024]{1,0:T(8,128)(2,1)S(1)} %collective-permute-done.6.refs_8_), channel_id=1, source_target_pairs={{0,8},{4,12},{8,16},{12,20},{16,24},{20,28},{24,32},{28,36},{32,40... | collective-permute-start | bytes 393224 | tf_op jit(solution)/shard_map/ppermute | solution.py:280
  28.6 13.1 %collective-permute-start.11 = (bf16[64,1024]{1,0:T(8,128)(2,1)S(1)}, bf16[64,1024]{1,0:T(8,128)(2,1)S(1)}, u32[]{:S(2)}, u32[]{:S(2)}) collective-permute-start(bf16[64,1024]{1,0:T(8,128)(2,1)S(1)} %collective-permute-done.10.refs_13_), channel_id=1, source_target_pairs={{0,248},{4,252},{8,0},{12,4},{16,8},{20,12},{24,16},{28,20},{32,24... | collective-permute-start | bytes 393224 | tf_op jit(solution)/shard_map/ppermute | solution.py:280
  33.4 10.8 %collective-permute-start.15 = (bf16[64,1024]{1,0:T(8,128)(2,1)S(1)}, bf16[64,1024]{1,0:T(8,128)(2,1)S(1)}, u32[]{:S(2)}, u32[]{:S(2)}) collective-permute-start(bf16[64,1024]{1,0:T(8,128)(2,1)S(1)} %collective-permute-done.14.refs_14_), channel_id=1, source_target_pairs={{0,248},{4,252},{8,0},{12,4},{16,8},{20,12},{24,16},{28,20},{32,24... | collective-permute-start | bytes 393224 | tf_op jit(solution)/shard_map/ppermute | solution.py:280
  34.5 9.7 %collective-permute-start.4 = (bf16[64,1024]{1,0:T(8,128)(2,1)S(1)}, bf16[64,1024]{1,0:T(8,128)(2,1)S(1)}, u32[]{:S(2)}, u32[]{:S(2)}) collective-permute-start(bf16[64,1024]{1,0:T(8,128)(2,1)S(1)} %collective-permute-done.3.refs_11_), channel_id=1, source_target_pairs={{0,8},{4,12},{8,16},{12,20},{16,24},{20,28},{24,32},{28,36},{32,40... | collective-permute-start | bytes 393224 | tf_op jit(solution)/shard_map/ppermute | solution.py:280
  36.9 7.3 %collective-permute-start.8 = (bf16[64,1024]{1,0:T(8,128)(2,1)S(1)}, bf16[64,1024]{1,0:T(8,128)(2,1)S(1)}, u32[]{:S(2)}, u32[]{:S(2)}) collective-permute-start(bf16[64,1024]{1,0:T(8,128)(2,1)S(1)} %collective-permute-done.7.refs_12_), channel_id=1, source_target_pairs={{0,8},{4,12},{8,16},{12,20},{16,24},{20,28},{24,32},{28,36},{32,40... | collective-permute-start | bytes 393224 | tf_op jit(solution)/shard_map/ppermute | solution.py:280
  38.5 10.7 %collective-permute-start.18 = (bf16[640,512]{1,0:T(8,128)(2,1)S(1)}, bf16[640,512]{1,0:T(8,128)(2,1)S(1)}, u32[]{:S(2)}, u32[]{:S(2)}) collective-permute-start(bf16[640,512]{1,0:T(8,128)(2,1)S(1)} %get-tuple-element.26), channel_id=1, source_target_pairs={{0,4},{4,0},{8,12},{12,8},{16,20},{20,16},{24,28},{28,24},{32,36},... | collective-permute-start | bytes 1966088 | tf_op jit(solution)/shard_map/ppermute | solution.py:283
  41.7 7.5 %collective-permute-start.19 = (bf16[640,512]{1,0:T(8,128)(2,1)S(1)}, bf16[640,512]{1,0:T(8,128)(2,1)S(1)}, u32[]{:S(2)}, u32[]{:S(2)}) collective-permute-start(bf16[640,512]{1,0:T(8,128)(2,1)S(1)} %get-tuple-element.27), channel_id=1, source_target_pairs={{0,4},{4,0},{8,12},{12,8},{16,20},{20,16},{24,28},{28,24},{32,36},... | collective-permute-start | bytes 1966088 | tf_op jit(solution)/shard_map/ppermute | solution.py:283
  44.3 4.9 %collective-permute-start.17 = (bf16[256,1024]{1,0:T(8,128)(2,1)S(1)}, bf16[256,1024]{1,0:T(8,128)(2,1)S(1)}, u32[]{:S(2)}, u32[]{:S(2)}) collective-permute-start(bf16[256,1024]{1,0:T(8,128)(2,1)S(1)} %pad_maximum_fusion), channel_id=1, source_target_pairs={{0,4},{4,0},{8,12},{12,8},{16,20},{20,16},{24,28},{28,24},{32,36},... | collective-permute-start | bytes 1572872 | tf_op jit(solution)/shard_map/ppermute | solution.py:283

commit v8 on v7

--- a/solution.py
+++ b/solution.py
@@ -91,7 +91,9 @@
         start = jnp.where(here * ROWS >= end, end, start)
 
     def reach(some):
-        nearest = here - 2 * min(places[s][0] for s in some) + 1
+        core = lax.rem(here, 2)
+        ahead = {"end": 1 - core, "lend": 1 - 2 * core, "own": 0}[kind]
+        nearest = here - 2 * min(places[s][0] for s in some) + ahead
         return nearest * ROWS + ROWS - 1 >= start
 
     base = [s for s in range(n) if places[s][0] == 0]

time: 51.6 us -> 51.6 us (level)
  waiting for transfers between devices: 10.2 us -> 11.4 us
  Pallas kernels: 6.11 us -> 5.39 us
  starting transfers between devices: 33.2 us -> 32.6 us
    ppermute x16, waiting for transfers between devices: 8.65 us -> 9.9 us  [send(): return lax.ppermute(block, 'seq', chip_route(ahead))]
    pallas_call x3, Pallas kernels: 6.11 us -> 5.39 us  [flash(): pl.pallas_call(functools.partial(flash_kernel, tuple(places), kind), out_...]
    ppermute x4, starting transfers between devices: 9.91 us -> 9.38 us  [swap(): return lax.ppermute(block, 'seq', SIBLING)]
  transfers between devices with their start and end apart: 20 -> 20, of which waited for: 5 -> 6; matrix products, arithmetic and copies ran while one was open for 3% -> 3% of each run, Pallas kernels for 8% -> 6%
where the time goes in v8:
time: 51.6 us; the launch traced here: 51.5 us
  starting transfers between devices  32.6 us (63%)
  waiting for transfers between devices  11.4 us (22%)
  Pallas kernels  5.39 us (10%)
  other arithmetic  1.75 us (3%)
    ppermute x16, starting transfers between devices, send(): return lax.ppermute(block, 'seq', chip_route(ahead))  23.3 us
    ppermute x16, waiting for transfers between devices, send(): return lax.ppermute(block, 'seq', chip_route(ahead))  9.9 us
    ppermute x4, starting transfers between devices, swap(): return lax.ppermute(block, 'seq', SIBLING)  9.38 us
    pallas_call x3, Pallas kernels, flash(): pl.pallas_call(functools.partial(flash_kernel, tuple(places), kind), out_...  5.39 us
    ppermute x4, waiting for transfers between devices, swap(): return lax.ppermute(block, 'seq', SIBLING)  1.54 us
  transfers between devices with their start and end apart: 20, of which 6 were waited for; matrix products, arithmetic and copies ran while one was open for 3% of the time, Pallas kernels for 6%

profile of v8, /device:TPU:1, one launch (start us, length us, event | category | flops | bytes accessed | tf_op | source)
XLA Modules:
  0.0 51.5 jit_solution(8078703991833623173)
XLA Ops:
  0.0 0.0 copy-start
  0.0 3.2 %collective-permute-start.16 = (bf16[64,8192]{1,0:T(8,128)(2,1)}, bf16[64,8192]{1,0:T(8,128)(2,1)S(1)}, u32[]{:S(2)}, u32[]{:S(2)}) collective-permute-start(bf16[64,8192]{1,0:T(8,128)(2,1)} %refs_1_.2), channel_id=1, source_target_pairs={{0,4},{4,0},{8,12},{12,8},{16,20},{20,16},{24,28},{28,24},{32,36},... | collective-permute-start | bytes 3145736 | tf_op jit(solution)/shard_map/ppermute | solution.py:285
  3.2 0.0 collective-permute-start
  3.2 1.2 %collective-permute-start.1 = (bf16[64,1024]{1,0:T(8,128)(2,1)}, bf16[64,1024]{1,0:T(8,128)(2,1)S(1)}, u32[]{:S(2)}, u32[]{:S(2)}) collective-permute-start(bf16[64,1024]{1,0:T(8,128)(2,1)} %param.5), channel_id=1, source_target_pairs={{0,8},{4,12},{8,16},{12,20},{16,24},{20,28},{24,32},{28,36},{32,40... | collective-permute-start | bytes 393224 | tf_op jit(solution)/shard_map/ppermute | solution.py:282
  4.4 1.3 %collective-permute-start.12 = (bf16[64,1024]{1,0:T(8,128)(2,1)}, bf16[64,1024]{1,0:T(8,128)(2,1)S(1)}, u32[]{:S(2)}, u32[]{:S(2)}) collective-permute-start(bf16[64,1024]{1,0:T(8,128)(2,1)} %param.6), channel_id=1, source_target_pairs={{0,64},{4,68},{8,72},{12,76},{16,80},{20,84},{24,88},{28,92},{32,9... | collective-permute-start | bytes 393224 | tf_op jit(solution)/shard_map/ppermute | solution.py:282
  5.7 1.6 %collective-permute-start.5 = (bf16[64,1024]{1,0:T(8,128)(2,1)}, bf16[64,1024]{1,0:T(8,128)(2,1)S(1)}, u32[]{:S(2)}, u32[]{:S(2)}) collective-permute-start(bf16[64,1024]{1,0:T(8,128)(2,1)} %param.6), channel_id=1, source_target_pairs={{0,8},{4,12},{8,16},{12,20},{16,24},{20,28},{24,32},{28,36},{32,40... | collective-permute-start | bytes 393224 | tf_op jit(solution)/shard_map/ppermute | solution.py:282
  7.4 1.0 %pad_maximum_fusion.1.refs_2_ = bf16[128,1024]{1,0:T(8,128)(2,1)S(1)} fusion(bf16[64,1024]{1,0:T(8,128)(2,1)} %param.6, bf16[64,1024]{1,0:T(8,128)(2,1)} %param.5), kind=kLoop, calls=%fused_computation.1 | loop fusion | flops 524288 | bytes 524288 | tf_op jit(solution)/shard_map/concatenate | solution.py:289
  8.4 0.7 %pad_add_fusion.1 = (s32[9]{0:T(128)S(1)}, s32[9]{0:T(128)S(1)}) fusion(s32[1]{0:T(128)S(6)} %sub.3, s32[8]{0:T(128)} %param.7, s32[1]{0:T(128)} %bitcast), kind=kLoop, calls=%fused_computation.3 | loop fusion | flops 18 | bytes 112 | tf_op jit(solution)/shard_map/concatenate | solution.py:279
  9.1 0.7 %collective-permute-done.refs_5_ = bf16[64,1024]{1,0:T(8,128)(2,1)S(1)} collective-permute-done((bf16[64,1024]{1,0:T(8,128)(2,1)}, bf16[64,1024]{1,0:T(8,128)(2,1)S(1)}, u32[]{:S(2)}, u32[]{:S(2)}) %collective-permute-start) | collective-permute-done | bytes 131104 | tf_op jit(solution)/shard_map/ppermute | solution.py:282
  9.8 5.0 %collective-permute-start.9 = (bf16[64,1024]{1,0:T(8,128)(2,1)S(1)}, bf16[64,1024]{1,0:T(8,128)(2,1)S(1)}, u32[]{:S(2)}, u32[]{:S(2)}) collective-permute-start(bf16[64,1024]{1,0:T(8,128)(2,1)S(1)} %collective-permute-done.refs_5_), channel_id=1, source_target_pairs={{0,248},{4,252},{8,0},{12,4},{16,8},{20,12},{24,16},{28,20},{32,24... | collective-permute-start | bytes 393224 | tf_op jit(solution)/shard_map/ppermute | solution.py:282
  14.8 3.4 %collective-permute-done.12.refs_6_ = bf16[64,1024]{1,0:T(8,128)(2,1)S(1)} collective-permute-done((bf16[64,1024]{1,0:T(8,128)(2,1)}, bf16[64,1024]{1,0:T(8,128)(2,1)S(1)}, u32[]{:S(2)}, u32[]{:S(2)}) %collective-permute-start.12) | collective-permute-done | bytes 131104 | tf_op jit(solution)/shard_map/ppermute | solution.py:282
  18.2 0.0 collective-permute-start.13
  18.2 0.0 collective-permute-done.1.refs_3_
  18.2 1.5 %collective-permute-start.2 = (bf16[64,1024]{1,0:T(8,128)(2,1)S(1)}, bf16[64,1024]{1,0:T(8,128)(2,1)S(1)}, u32[]{:S(2)}, u32[]{:S(2)}) collective-permute-start(bf16[64,1024]{1,0:T(8,128)(2,1)S(1)} %collective-permute-done.1.refs_3_), channel_id=1, source_target_pairs={{0,8},{4,12},{8,16},{12,20},{16,24},{20,28},{24,32},{28,36},{32,40... | collective-permute-start | bytes 393224 | tf_op jit(solution)/shard_map/ppermute | solution.py:282
  19.7 0.0 collective-permute-done.5.refs_4_
  19.7 0.1 collective-permute-start.6
  19.8 0.0 collective-permute-done.9.refs_9_
  19.8 4.7 %collective-permute-start.10 = (bf16[64,1024]{1,0:T(8,128)(2,1)S(1)}, bf16[64,1024]{1,0:T(8,128)(2,1)S(1)}, u32[]{:S(2)}, u32[]{:S(2)}) collective-permute-start(bf16[64,1024]{1,0:T(8,128)(2,1)S(1)} %collective-permute-done.9.refs_9_), channel_id=1, source_target_pairs={{0,248},{4,252},{8,0},{12,4},{16,8},{20,12},{24,16},{28,20},{32,24... | collective-permute-start | bytes 393224 | tf_op jit(solution)/shard_map/ppermute | solution.py:282
  24.5 0.0 collective-permute-done.13.refs_10_
  24.5 1.6 %collective-permute-start.14 = (bf16[64,1024]{1,0:T(8,128)(2,1)S(1)}, bf16[64,1024]{1,0:T(8,128)(2,1)S(1)}, u32[]{:S(2)}, u32[]{:S(2)}) collective-permute-start(bf16[64,1024]{1,0:T(8,128)(2,1)S(1)} %collective-permute-done.13.refs_10_), channel_id=1, source_target_pairs={{0,248},{4,252},{8,0},{12,4},{16,8},{20,12},{24,16},{28,20},{32,24... | collective-permute-start | bytes 393224 | tf_op jit(solution)/shard_map/ppermute | solution.py:282
  26.1 0.0 collective-permute-done.2.refs_7_
  26.1 0.0 collective-permute-start.3
  26.1 2.5 %collective-permute-done.6.refs_8_ = bf16[64,1024]{1,0:T(8,128)(2,1)S(1)} collective-permute-done((bf16[64,1024]{1,0:T(8,128)(2,1)S(1)}, bf16[64,1024]{1,0:T(8,128)(2,1)S(1)}, u32[]{:S(2)}, u32[]{:S(2)}) %collective-permute-start.6) | collective-permute-done | bytes 131104 | tf_op jit(solution)/shard_map/ppermute | solution.py:282
  28.6 0.0 collective-permute-start.7
  28.6 0.0 collective-permute-done.10.refs_13_
  28.6 4.8 %collective-permute-start.11 = (bf16[64,1024]{1,0:T(8,128)(2,1)S(1)}, bf16[64,1024]{1,0:T(8,128)(2,1)S(1)}, u32[]{:S(2)}, u32[]{:S(2)}) collective-permute-start(bf16[64,1024]{1,0:T(8,128)(2,1)S(1)} %collective-permute-done.10.refs_13_), channel_id=1, source_target_pairs={{0,248},{4,252},{8,0},{12,4},{16,8},{20,12},{24,16},{28,20},{32,24... | collective-permute-start | bytes 393224 | tf_op jit(solution)/shard_map/ppermute | solution.py:282
  33.4 0.0 collective-permute-done.14.refs_14_
  33.4 1.2 %collective-permute-start.15 = (bf16[64,1024]{1,0:T(8,128)(2,1)S(1)}, bf16[64,1024]{1,0:T(8,128)(2,1)S(1)}, u32[]{:S(2)}, u32[]{:S(2)}) collective-permute-start(bf16[64,1024]{1,0:T(8,128)(2,1)S(1)} %collective-permute-done.14.refs_14_), channel_id=1, source_target_pairs={{0,248},{4,252},{8,0},{12,4},{16,8},{20,12},{24,16},{28,20},{32,24... | collective-permute-start | bytes 393224 | tf_op jit(solution)/shard_map/ppermute | solution.py:282
  34.5 0.0 collective-permute-done.3.refs_11_
  34.5 0.3 collective-permute-start.4
  34.9 2.0 %collective-permute-done.7.refs_12_ = bf16[64,1024]{1,0:T(8,128)(2,1)S(1)} collective-permute-done((bf16[64,1024]{1,0:T(8,128)(2,1)S(1)}, bf16[64,1024]{1,0:T(8,128)(2,1)S(1)}, u32[]{:S(2)}, u32[]{:S(2)}) %collective-permute-start.7) | collective-permute-done | bytes 131104 | tf_op jit(solution)/shard_map/ppermute | solution.py:282
  36.9 0.0 collective-permute-start.8
  36.9 0.0 collective-permute-done.16.refs_1_
  36.9 1.6 %shard_map.46 = (bf16[640,512]{1,0:T(8,128)(2,1)S(1)}, bf16[640,512]{1,0:T(8,128)(2,1)S(1)}) custom-call(s32[9]{0:T(128)S(1)} %get-tuple-element.24.refs_0_, bf16[64,8192]{1,0:T(8,128)(2,1)S(1)} %collective-permute-done.16.refs_1_, bf16[128,1024]{1,0:T(8,128)(2,1)S(1)} %pad_maximum_fusion.1.refs_2_, bf16[64,1024]{1,0:T(8,128)(2,1)S(1)} %collective-permute-done.1.refs_3_, ...), custom_call_target="tpu_custom_call" | custom-call | flops 939524096 | bytes 65536 | tf_op jit(solution)/shard_map/pallas_call | solution.py:263
  38.5 2.4 %collective-permute-start.18 = (bf16[640,512]{1,0:T(8,128)(2,1)S(1)}, bf16[640,512]{1,0:T(8,128)(2,1)S(1)}, u32[]{:S(2)}, u32[]{:S(2)}) collective-permute-start(bf16[640,512]{1,0:T(8,128)(2,1)S(1)} %get-tuple-element.26), channel_id=1, source_target_pairs={{0,4},{4,0},{8,12},{12,8},{16,20},{20,16},{24,28},{28,24},{32,36},... | collective-permute-start | bytes 1966088 | tf_op jit(solution)/shard_map/ppermute | solution.py:285
  41.0 0.0 collective-permute-done.11.refs_4_
  41.0 0.1 collective-permute-start.19
  41.1 0.0 copy-done
  41.1 1.6 %shard_map.47 = (f32[8,512]{1,0:T(8,128)S(1)}, f32[8,512]{1,0:T(8,128)S(1)}, f32[8,128,512]{2,1,0:T(8,128)S(1)}) custom-call(s32[9]{0:T(128)S(1)} %get-tuple-element.22.refs_0_, bf16[64,8192]{1,0:T(8,128)(2,1)S(1)} %copy-done, bf16[128,1024]{1,0:T(8,128)(2,1)S(1)} %pad_maximum_fusion.1.refs_2_, bf16[64,1024]{1,0:T(8,128)(2,1)S(1)} %collective-permute-done.1.refs_3_, ...), custom_call_target="tpu_custom_call" | custom-call | flops 939524096 | bytes 65536 | tf_op jit(solution)/shard_map/pallas_call | solution.py:263
  42.7 0.0 collective-permute-done.15.refs_5_
  42.7 0.0 collective-permute-done.4.refs_2_
  42.8 1.3 %collective-permute-done.8.refs_3_ = bf16[64,1024]{1,0:T(8,128)(2,1)S(1)} collective-permute-done((bf16[64,1024]{1,0:T(8,128)(2,1)S(1)}, bf16[64,1024]{1,0:T(8,128)(2,1)S(1)}, u32[]{:S(2)}, u32[]{:S(2)}) %collective-permute-start.8) | collective-permute-done | bytes 131104 | tf_op jit(solution)/shard_map/ppermute | solution.py:282
  44.1 3.6 %collective-permute-start.17 = (bf16[256,1024]{1,0:T(8,128)(2,1)S(1)}, bf16[256,1024]{1,0:T(8,128)(2,1)S(1)}, u32[]{:S(2)}, u32[]{:S(2)}) collective-permute-start(bf16[256,1024]{1,0:T(8,128)(2,1)S(1)} %pad_maximum_fusion), channel_id=1, source_target_pairs={{0,4},{4,0},{8,12},{12,8},{16,20},{20,16},{24,28},{28,24},{32,36},... | collective-permute-start | bytes 1572872 | tf_op jit(solution)/shard_map/ppermute | solution.py:285
  47.6 1.5 %collective-permute-done.17.refs_6_ = bf16[256,1024]{1,0:T(8,128)(2,1)S(1)} collective-permute-done((bf16[256,1024]{1,0:T(8,128)(2,1)S(1)}, bf16[256,1024]{1,0:T(8,128)(2,1)S(1)}, u32[]{:S(2)}, u32[]{:S(2)}) %collective-permute-start.17) | collective-permute-done | bytes 524320 | tf_op jit(solution)/shard_map/ppermute | solution.py:285
  49.2 0.0 collective-permute-done.18.refs_10_
  49.2 0.0 collective-permute-done.19.refs_11_
  49.2 2.1 %shard_map.48 = bf16[64,8192]{1,0:T(8,128)(2,1)} custom-call(s32[9]{0:T(128)S(1)} %get-tuple-element.22.refs_0_, bf16[64,8192]{1,0:T(8,128)(2,1)S(1)} %copy-done, bf16[64,1024]{1,0:T(8,128)(2,1)S(1)} %collective-permute-done.4.refs_2_, bf16[64,1024]{1,0:T(8,128)(2,1)S(1)} %collective-permute-done.8.refs_3_, ...), custom_call_target="tpu_custom_call" | custom-call | flops 536870912 | bytes 65536 | tf_op jit(solution)/shard_map/pallas_call | solution.py:263
  (1 shorter events, 0.0 us)
Async XLA Ops:
  0.0 41.1 %copy-start = (bf16[64,8192]{1,0:T(8,128)(2,1)S(1)}, bf16[64,8192]{1,0:T(8,128)(2,1)}, u32[]{:S(2)}) copy-start(bf16[64,8192]{1,0:T(8,128)(2,1)} %refs_1_.2) | copy-start | bytes 3145732
  0.0 36.9 %collective-permute-start.16 = (bf16[64,8192]{1,0:T(8,128)(2,1)}, bf16[64,8192]{1,0:T(8,128)(2,1)S(1)}, u32[]{:S(2)}, u32[]{:S(2)}) collective-permute-start(bf16[64,8192]{1,0:T(8,128)(2,1)} %refs_1_.2), channel_id=1, source_target_pairs={{0,4},{4,0},{8,12},{12,8},{16,20},{20,16},{24,28},{28,24},{32,36},... | collective-permute-start | bytes 3145736 | tf_op jit(solution)/shard_map/ppermute | solution.py:285
  3.2 6.5 %collective-permute-start = (bf16[64,1024]{1,0:T(8,128)(2,1)}, bf16[64,1024]{1,0:T(8,128)(2,1)S(1)}, u32[]{:S(2)}, u32[]{:S(2)}) collective-permute-start(bf16[64,1024]{1,0:T(8,128)(2,1)} %param.5), channel_id=1, source_target_pairs={{0,64},{4,68},{8,72},{12,76},{16,80},{20,84},{24,88},{28,92},{32,9... | collective-permute-start | bytes 393224 | tf_op jit(solution)/shard_map/ppermute | solution.py:282
  3.2 15.0 %collective-permute-start.1 = (bf16[64,1024]{1,0:T(8,128)(2,1)}, bf16[64,1024]{1,0:T(8,128)(2,1)S(1)}, u32[]{:S(2)}, u32[]{:S(2)}) collective-permute-start(bf16[64,1024]{1,0:T(8,128)(2,1)} %param.5), channel_id=1, source_target_pairs={{0,8},{4,12},{8,16},{12,20},{16,24},{20,28},{24,32},{28,36},{32,40... | collective-permute-start | bytes 393224 | tf_op jit(solution)/shard_map/ppermute | solution.py:282
  4.4 13.8 %collective-permute-start.12 = (bf16[64,1024]{1,0:T(8,128)(2,1)}, bf16[64,1024]{1,0:T(8,128)(2,1)S(1)}, u32[]{:S(2)}, u32[]{:S(2)}) collective-permute-start(bf16[64,1024]{1,0:T(8,128)(2,1)} %param.6), channel_id=1, source_target_pairs={{0,64},{4,68},{8,72},{12,76},{16,80},{20,84},{24,88},{28,92},{32,9... | collective-permute-start | bytes 393224 | tf_op jit(solution)/shard_map/ppermute | solution.py:282
  5.7 14.0 %collective-permute-start.5 = (bf16[64,1024]{1,0:T(8,128)(2,1)}, bf16[64,1024]{1,0:T(8,128)(2,1)S(1)}, u32[]{:S(2)}, u32[]{:S(2)}) collective-permute-start(bf16[64,1024]{1,0:T(8,128)(2,1)} %param.6), channel_id=1, source_target_pairs={{0,8},{4,12},{8,16},{12,20},{16,24},{20,28},{24,32},{28,36},{32,40... | collective-permute-start | bytes 393224 | tf_op jit(solution)/shard_map/ppermute | solution.py:282
  9.8 10.0 %collective-permute-start.9 = (bf16[64,1024]{1,0:T(8,128)(2,1)S(1)}, bf16[64,1024]{1,0:T(8,128)(2,1)S(1)}, u32[]{:S(2)}, u32[]{:S(2)}) collective-permute-start(bf16[64,1024]{1,0:T(8,128)(2,1)S(1)} %collective-permute-done.refs_5_), channel_id=1, source_target_pairs={{0,248},{4,252},{8,0},{12,4},{16,8},{20,12},{24,16},{28,20},{32,24... | collective-permute-start | bytes 393224 | tf_op jit(solution)/shard_map/ppermute | solution.py:282
  18.2 6.3 %collective-permute-start.13 = (bf16[64,1024]{1,0:T(8,128)(2,1)S(1)}, bf16[64,1024]{1,0:T(8,128)(2,1)S(1)}, u32[]{:S(2)}, u32[]{:S(2)}) collective-permute-start(bf16[64,1024]{1,0:T(8,128)(2,1)S(1)} %collective-permute-done.12.refs_6_), channel_id=1, source_target_pairs={{0,248},{4,252},{8,0},{12,4},{16,8},{20,12},{24,16},{28,20},{32,24... | collective-permute-start | bytes 393224 | tf_op jit(solution)/shard_map/ppermute | solution.py:282
  18.2 7.9 %collective-permute-start.2 = (bf16[64,1024]{1,0:T(8,128)(2,1)S(1)}, bf16[64,1024]{1,0:T(8,128)(2,1)S(1)}, u32[]{:S(2)}, u32[]{:S(2)}) collective-permute-start(bf16[64,1024]{1,0:T(8,128)(2,1)S(1)} %collective-permute-done.1.refs_3_), channel_id=1, source_target_pairs={{0,8},{4,12},{8,16},{12,20},{16,24},{20,28},{24,32},{28,36},{32,40... | collective-permute-start | bytes 393224 | tf_op jit(solution)/shard_map/ppermute | solution.py:282
  19.7 8.9 %collective-permute-start.6 = (bf16[64,1024]{1,0:T(8,128)(2,1)S(1)}, bf16[64,1024]{1,0:T(8,128)(2,1)S(1)}, u32[]{:S(2)}, u32[]{:S(2)}) collective-permute-start(bf16[64,1024]{1,0:T(8,128)(2,1)S(1)} %collective-permute-done.5.refs_4_), channel_id=1, source_target_pairs={{0,8},{4,12},{8,16},{12,20},{16,24},{20,28},{24,32},{28,36},{32,40... | collective-permute-start | bytes 393224 | tf_op jit(solution)/shard_map/ppermute | solution.py:282
  19.8 8.8 %collective-permute-start.10 = (bf16[64,1024]{1,0:T(8,128)(2,1)S(1)}, bf16[64,1024]{1,0:T(8,128)(2,1)S(1)}, u32[]{:S(2)}, u32[]{:S(2)}) collective-permute-start(bf16[64,1024]{1,0:T(8,128)(2,1)S(1)} %collective-permute-done.9.refs_9_), channel_id=1, source_target_pairs={{0,248},{4,252},{8,0},{12,4},{16,8},{20,12},{24,16},{28,20},{32,24... | collective-permute-start | bytes 393224 | tf_op jit(solution)/shard_map/ppermute | solution.py:282
  24.5 8.9 %collective-permute-start.14 = (bf16[64,1024]{1,0:T(8,128)(2,1)S(1)}, bf16[64,1024]{1,0:T(8,128)(2,1)S(1)}, u32[]{:S(2)}, u32[]{:S(2)}) collective-permute-start(bf16[64,1024]{1,0:T(8,128)(2,1)S(1)} %collective-permute-done.13.refs_10_), channel_id=1, source_target_pairs={{0,248},{4,252},{8,0},{12,4},{16,8},{20,12},{24,16},{28,20},{32,24... | collective-permute-start | bytes 393224 | tf_op jit(solution)/shard_map/ppermute | solution.py:282
  26.1 8.4 %collective-permute-start.3 = (bf16[64,1024]{1,0:T(8,128)(2,1)S(1)}, bf16[64,1024]{1,0:T(8,128)(2,1)S(1)}, u32[]{:S(2)}, u32[]{:S(2)}) collective-permute-start(bf16[64,1024]{1,0:T(8,128)(2,1)S(1)} %collective-permute-done.2.refs_7_), channel_id=1, source_target_pairs={{0,8},{4,12},{8,16},{12,20},{16,24},{20,28},{24,32},{28,36},{32,40... | collective-permute-start | bytes 393224 | tf_op jit(solution)/shard_map/ppermute | solution.py:282
  28.6 8.3 %collective-permute-start.7 = (bf16[64,1024]{1,0:T(8,128)(2,1)S(1)}, bf16[64,1024]{1,0:T(8,128)(2,1)S(1)}, u32[]{:S(2)}, u32[]{:S(2)}) collective-permute-start(bf16[64,1024]{1,0:T(8,128)(2,1)S(1)} %collective-permute-done.6.refs_8_), channel_id=1, source_target_pairs={{0,8},{4,12},{8,16},{12,20},{16,24},{20,28},{24,32},{28,36},{32,40... | collective-permute-start | bytes 393224 | tf_op jit(solution)/shard_map/ppermute | solution.py:282
  28.6 12.4 %collective-permute-start.11 = (bf16[64,1024]{1,0:T(8,128)(2,1)S(1)}, bf16[64,1024]{1,0:T(8,128)(2,1)S(1)}, u32[]{:S(2)}, u32[]{:S(2)}) collective-permute-start(bf16[64,1024]{1,0:T(8,128)(2,1)S(1)} %collective-permute-done.10.refs_13_), channel_id=1, source_target_pairs={{0,248},{4,252},{8,0},{12,4},{16,8},{20,12},{24,16},{28,20},{32,24... | collective-permute-start | bytes 393224 | tf_op jit(solution)/shard_map/ppermute | solution.py:282
  33.4 9.3 %collective-permute-start.15 = (bf16[64,1024]{1,0:T(8,128)(2,1)S(1)}, bf16[64,1024]{1,0:T(8,128)(2,1)S(1)}, u32[]{:S(2)}, u32[]{:S(2)}) collective-permute-start(bf16[64,1024]{1,0:T(8,128)(2,1)S(1)} %collective-permute-done.14.refs_14_), channel_id=1, source_target_pairs={{0,248},{4,252},{8,0},{12,4},{16,8},{20,12},{24,16},{28,20},{32,24... | collective-permute-start | bytes 393224 | tf_op jit(solution)/shard_map/ppermute | solution.py:282
  34.5 8.2 %collective-permute-start.4 = (bf16[64,1024]{1,0:T(8,128)(2,1)S(1)}, bf16[64,1024]{1,0:T(8,128)(2,1)S(1)}, u32[]{:S(2)}, u32[]{:S(2)}) collective-permute-start(bf16[64,1024]{1,0:T(8,128)(2,1)S(1)} %collective-permute-done.3.refs_11_), channel_id=1, source_target_pairs={{0,8},{4,12},{8,16},{12,20},{16,24},{20,28},{24,32},{28,36},{32,40... | collective-permute-start | bytes 393224 | tf_op jit(solution)/shard_map/ppermute | solution.py:282
  36.9 7.1 %collective-permute-start.8 = (bf16[64,1024]{1,0:T(8,128)(2,1)S(1)}, bf16[64,1024]{1,0:T(8,128)(2,1)S(1)}, u32[]{:S(2)}, u32[]{:S(2)}) collective-permute-start(bf16[64,1024]{1,0:T(8,128)(2,1)S(1)} %collective-permute-done.7.refs_12_), channel_id=1, source_target_pairs={{0,8},{4,12},{8,16},{12,20},{16,24},{20,28},{24,32},{28,36},{32,40... | collective-permute-start | bytes 393224 | tf_op jit(solution)/shard_map/ppermute | solution.py:282
  38.5 10.7 %collective-permute-start.18 = (bf16[640,512]{1,0:T(8,128)(2,1)S(1)}, bf16[640,512]{1,0:T(8,128)(2,1)S(1)}, u32[]{:S(2)}, u32[]{:S(2)}) collective-permute-start(bf16[640,512]{1,0:T(8,128)(2,1)S(1)} %get-tuple-element.26), channel_id=1, source_target_pairs={{0,4},{4,0},{8,12},{12,8},{16,20},{20,16},{24,28},{28,24},{32,36},... | collective-permute-start | bytes 1966088 | tf_op jit(solution)/shard_map/ppermute | solution.py:285
  41.0 8.2 %collective-permute-start.19 = (bf16[640,512]{1,0:T(8,128)(2,1)S(1)}, bf16[640,512]{1,0:T(8,128)(2,1)S(1)}, u32[]{:S(2)}, u32[]{:S(2)}) collective-permute-start(bf16[640,512]{1,0:T(8,128)(2,1)S(1)} %get-tuple-element.27), channel_id=1, source_target_pairs={{0,4},{4,0},{8,12},{12,8},{16,20},{20,16},{24,28},{28,24},{32,36},... | collective-permute-start | bytes 1966088 | tf_op jit(solution)/shard_map/ppermute | solution.py:285
  44.1 5.1 %collective-permute-start.17 = (bf16[256,1024]{1,0:T(8,128)(2,1)S(1)}, bf16[256,1024]{1,0:T(8,128)(2,1)S(1)}, u32[]{:S(2)}, u32[]{:S(2)}) collective-permute-start(bf16[256,1024]{1,0:T(8,128)(2,1)S(1)} %pad_maximum_fusion), channel_id=1, source_target_pairs={{0,4},{4,0},{8,12},{12,8},{16,20},{20,16},{24,28},{28,24},{32,36},... | collective-permute-start | bytes 1572872 | tf_op jit(solution)/shard_map/ppermute | solution.py:285

commit v9 on v7

--- a/solution.py
+++ b/solution.py
@@ -194,7 +194,7 @@
             result = result + lent[i][j * DH : (j + 1) * DH, :].astype(jnp.float32) * (got * share)
             if some:
                 result = result + part * share
-            result = result.T.astype(jnp.bfloat16)
+            result = result.T.astype(jnp.bfloat16) if some else result.astype(jnp.bfloat16).T
             for g in range(GROUP):
                 staged[:, h * WIDE + g * DH : h * WIDE + (g + 1) * DH] = result[g * ROWS : (g + 1) * ROWS, :]
             copies.append(pltpu.make_async_copy(staged.at[:, wide], out_ref.at[:, wide], sems.at[h]))

time: 51.6 us -> 51.5 us (level)
  no operation moved by 1% of the time
where the time goes in v9:
time: 51.5 us; the launch traced here: 51.4 us
  starting transfers between devices  33.2 us (64%)
  waiting for transfers between devices  10.2 us (20%)
  Pallas kernels  6.04 us (12%)
  other arithmetic  1.75 us (3%)
    ppermute x16, starting transfers between devices, send(): return lax.ppermute(block, 'seq', chip_route(ahead))  23.3 us
    ppermute x4, starting transfers between devices, swap(): return lax.ppermute(block, 'seq', SIBLING)  9.91 us
    ppermute x16, waiting for transfers between devices, send(): return lax.ppermute(block, 'seq', chip_route(ahead))  8.65 us
    pallas_call x3, Pallas kernels, flash(): pl.pallas_call(functools.partial(flash_kernel, tuple(places), kind), out_...  6.04 us
    ppermute x4, waiting for transfers between devices, swap(): return lax.ppermute(block, 'seq', SIBLING)  1.54 us
  transfers between devices with their start and end apart: 20, of which 5 were waited for; matrix products, arithmetic and copies ran while one was open for 3% of the time, Pallas kernels for 8%

profile of v9, /device:TPU:1, one launch (start us, length us, event | category | flops | bytes accessed | tf_op | source)
XLA Modules:
  0.0 51.4 jit_solution(14839181289893790646)
XLA Ops:
  0.0 0.0 copy-start
  0.0 3.2 %collective-permute-start.16 = (bf16[64,8192]{1,0:T(8,128)(2,1)}, bf16[64,8192]{1,0:T(8,128)(2,1)S(1)}, u32[]{:S(2)}, u32[]{:S(2)}) collective-permute-start(bf16[64,8192]{1,0:T(8,128)(2,1)} %refs_1_.2), channel_id=1, source_target_pairs={{0,4},{4,0},{8,12},{12,8},{16,20},{20,16},{24,28},{28,24},{32,36},... | collective-permute-start | bytes 3145736 | tf_op jit(solution)/shard_map/ppermute | solution.py:283
  3.2 0.0 collective-permute-start
  3.2 1.2 %collective-permute-start.1 = (bf16[64,1024]{1,0:T(8,128)(2,1)}, bf16[64,1024]{1,0:T(8,128)(2,1)S(1)}, u32[]{:S(2)}, u32[]{:S(2)}) collective-permute-start(bf16[64,1024]{1,0:T(8,128)(2,1)} %param.5), channel_id=1, source_target_pairs={{0,8},{4,12},{8,16},{12,20},{16,24},{20,28},{24,32},{28,36},{32,40... | collective-permute-start | bytes 393224 | tf_op jit(solution)/shard_map/ppermute | solution.py:280
  4.4 1.3 %collective-permute-start.12 = (bf16[64,1024]{1,0:T(8,128)(2,1)}, bf16[64,1024]{1,0:T(8,128)(2,1)S(1)}, u32[]{:S(2)}, u32[]{:S(2)}) collective-permute-start(bf16[64,1024]{1,0:T(8,128)(2,1)} %param.6), channel_id=1, source_target_pairs={{0,64},{4,68},{8,72},{12,76},{16,80},{20,84},{24,88},{28,92},{32,9... | collective-permute-start | bytes 393224 | tf_op jit(solution)/shard_map/ppermute | solution.py:280
  5.7 1.6 %collective-permute-start.5 = (bf16[64,1024]{1,0:T(8,128)(2,1)}, bf16[64,1024]{1,0:T(8,128)(2,1)S(1)}, u32[]{:S(2)}, u32[]{:S(2)}) collective-permute-start(bf16[64,1024]{1,0:T(8,128)(2,1)} %param.6), channel_id=1, source_target_pairs={{0,8},{4,12},{8,16},{12,20},{16,24},{20,28},{24,32},{28,36},{32,40... | collective-permute-start | bytes 393224 | tf_op jit(solution)/shard_map/ppermute | solution.py:280
  7.4 1.0 %pad_maximum_fusion.1.refs_2_ = bf16[128,1024]{1,0:T(8,128)(2,1)S(1)} fusion(bf16[64,1024]{1,0:T(8,128)(2,1)} %param.6, bf16[64,1024]{1,0:T(8,128)(2,1)} %param.5), kind=kLoop, calls=%fused_computation.1 | loop fusion | flops 524288 | bytes 524288 | tf_op jit(solution)/shard_map/concatenate | solution.py:287
  8.4 0.7 %pad_add_fusion.1 = (s32[9]{0:T(128)S(1)}, s32[9]{0:T(128)S(1)}) fusion(s32[1]{0:T(128)S(6)} %sub.3, s32[8]{0:T(128)} %param.7, s32[1]{0:T(128)} %bitcast), kind=kLoop, calls=%fused_computation.3 | loop fusion | flops 18 | bytes 112 | tf_op jit(solution)/shard_map/concatenate | solution.py:277
  9.1 0.7 %collective-permute-done.refs_5_ = bf16[64,1024]{1,0:T(8,128)(2,1)S(1)} collective-permute-done((bf16[64,1024]{1,0:T(8,128)(2,1)}, bf16[64,1024]{1,0:T(8,128)(2,1)S(1)}, u32[]{:S(2)}, u32[]{:S(2)}) %collective-permute-start) | collective-permute-done | bytes 131104 | tf_op jit(solution)/shard_map/ppermute | solution.py:280
  9.8 5.0 %collective-permute-start.9 = (bf16[64,1024]{1,0:T(8,128)(2,1)S(1)}, bf16[64,1024]{1,0:T(8,128)(2,1)S(1)}, u32[]{:S(2)}, u32[]{:S(2)}) collective-permute-start(bf16[64,1024]{1,0:T(8,128)(2,1)S(1)} %collective-permute-done.refs_5_), channel_id=1, source_target_pairs={{0,248},{4,252},{8,0},{12,4},{16,8},{20,12},{24,16},{28,20},{32,24... | collective-permute-start | bytes 393224 | tf_op jit(solution)/shard_map/ppermute | solution.py:280
  14.8 3.4 %collective-permute-done.12.refs_6_ = bf16[64,1024]{1,0:T(8,128)(2,1)S(1)} collective-permute-done((bf16[64,1024]{1,0:T(8,128)(2,1)}, bf16[64,1024]{1,0:T(8,128)(2,1)S(1)}, u32[]{:S(2)}, u32[]{:S(2)}) %collective-permute-start.12) | collective-permute-done | bytes 131104 | tf_op jit(solution)/shard_map/ppermute | solution.py:280
  18.2 0.0 collective-permute-start.13
  18.2 0.0 collective-permute-done.1.refs_3_
  18.2 1.5 %collective-permute-start.2 = (bf16[64,1024]{1,0:T(8,128)(2,1)S(1)}, bf16[64,1024]{1,0:T(8,128)(2,1)S(1)}, u32[]{:S(2)}, u32[]{:S(2)}) collective-permute-start(bf16[64,1024]{1,0:T(8,128)(2,1)S(1)} %collective-permute-done.1.refs_3_), channel_id=1, source_target_pairs={{0,8},{4,12},{8,16},{12,20},{16,24},{20,28},{24,32},{28,36},{32,40... | collective-permute-start | bytes 393224 | tf_op jit(solution)/shard_map/ppermute | solution.py:280
  19.7 0.0 collective-permute-done.5.refs_4_
  19.7 0.1 collective-permute-start.6
  19.8 0.0 collective-permute-done.9.refs_9_
  19.8 4.7 %collective-permute-start.10 = (bf16[64,1024]{1,0:T(8,128)(2,1)S(1)}, bf16[64,1024]{1,0:T(8,128)(2,1)S(1)}, u32[]{:S(2)}, u32[]{:S(2)}) collective-permute-start(bf16[64,1024]{1,0:T(8,128)(2,1)S(1)} %collective-permute-done.9.refs_9_), channel_id=1, source_target_pairs={{0,248},{4,252},{8,0},{12,4},{16,8},{20,12},{24,16},{28,20},{32,24... | collective-permute-start | bytes 393224 | tf_op jit(solution)/shard_map/ppermute | solution.py:280
  24.5 0.0 collective-permute-done.13.refs_10_
  24.5 1.6 %collective-permute-start.14 = (bf16[64,1024]{1,0:T(8,128)(2,1)S(1)}, bf16[64,1024]{1,0:T(8,128)(2,1)S(1)}, u32[]{:S(2)}, u32[]{:S(2)}) collective-permute-start(bf16[64,1024]{1,0:T(8,128)(2,1)S(1)} %collective-permute-done.13.refs_10_), channel_id=1, source_target_pairs={{0,248},{4,252},{8,0},{12,4},{16,8},{20,12},{24,16},{28,20},{32,24... | collective-permute-start | bytes 393224 | tf_op jit(solution)/shard_map/ppermute | solution.py:280
  26.1 0.0 collective-permute-done.2.refs_7_
  26.1 0.0 collective-permute-start.3
  26.1 2.5 %collective-permute-done.6.refs_8_ = bf16[64,1024]{1,0:T(8,128)(2,1)S(1)} collective-permute-done((bf16[64,1024]{1,0:T(8,128)(2,1)S(1)}, bf16[64,1024]{1,0:T(8,128)(2,1)S(1)}, u32[]{:S(2)}, u32[]{:S(2)}) %collective-permute-start.6) | collective-permute-done | bytes 131104 | tf_op jit(solution)/shard_map/ppermute | solution.py:280
  28.6 0.0 collective-permute-start.7
  28.6 0.0 collective-permute-done.10.refs_13_
  28.6 4.8 %collective-permute-start.11 = (bf16[64,1024]{1,0:T(8,128)(2,1)S(1)}, bf16[64,1024]{1,0:T(8,128)(2,1)S(1)}, u32[]{:S(2)}, u32[]{:S(2)}) collective-permute-start(bf16[64,1024]{1,0:T(8,128)(2,1)S(1)} %collective-permute-done.10.refs_13_), channel_id=1, source_target_pairs={{0,248},{4,252},{8,0},{12,4},{16,8},{20,12},{24,16},{28,20},{32,24... | collective-permute-start | bytes 393224 | tf_op jit(solution)/shard_map/ppermute | solution.py:280
  33.4 0.0 collective-permute-done.14.refs_14_
  33.4 1.2 %collective-permute-start.15 = (bf16[64,1024]{1,0:T(8,128)(2,1)S(1)}, bf16[64,1024]{1,0:T(8,128)(2,1)S(1)}, u32[]{:S(2)}, u32[]{:S(2)}) collective-permute-start(bf16[64,1024]{1,0:T(8,128)(2,1)S(1)} %collective-permute-done.14.refs_14_), channel_id=1, source_target_pairs={{0,248},{4,252},{8,0},{12,4},{16,8},{20,12},{24,16},{28,20},{32,24... | collective-permute-start | bytes 393224 | tf_op jit(solution)/shard_map/ppermute | solution.py:280
  34.5 0.0 collective-permute-done.3.refs_11_
  34.5 0.3 collective-permute-start.4
  34.9 2.0 %collective-permute-done.7.refs_12_ = bf16[64,1024]{1,0:T(8,128)(2,1)S(1)} collective-permute-done((bf16[64,1024]{1,0:T(8,128)(2,1)S(1)}, bf16[64,1024]{1,0:T(8,128)(2,1)S(1)}, u32[]{:S(2)}, u32[]{:S(2)}) %collective-permute-start.7) | collective-permute-done | bytes 131104 | tf_op jit(solution)/shard_map/ppermute | solution.py:280
  36.9 0.0 collective-permute-start.8
  36.9 0.0 collective-permute-done.16.refs_1_
  36.9 1.6 %shard_map.46 = (bf16[640,512]{1,0:T(8,128)(2,1)S(1)}, bf16[640,512]{1,0:T(8,128)(2,1)S(1)}) custom-call(s32[9]{0:T(128)S(1)} %get-tuple-element.24.refs_0_, bf16[64,8192]{1,0:T(8,128)(2,1)S(1)} %collective-permute-done.16.refs_1_, bf16[128,1024]{1,0:T(8,128)(2,1)S(1)} %pad_maximum_fusion.1.refs_2_, bf16[64,1024]{1,0:T(8,128)(2,1)S(1)} %collective-permute-done.1.refs_3_, ...), custom_call_target="tpu_custom_call" | custom-call | flops 939524096 | bytes 65536 | tf_op jit(solution)/shard_map/pallas_call | solution.py:261
  38.5 3.2 %collective-permute-start.18 = (bf16[640,512]{1,0:T(8,128)(2,1)S(1)}, bf16[640,512]{1,0:T(8,128)(2,1)S(1)}, u32[]{:S(2)}, u32[]{:S(2)}) collective-permute-start(bf16[640,512]{1,0:T(8,128)(2,1)S(1)} %get-tuple-element.26), channel_id=1, source_target_pairs={{0,4},{4,0},{8,12},{12,8},{16,20},{20,16},{24,28},{28,24},{32,36},... | collective-permute-start | bytes 1966088 | tf_op jit(solution)/shard_map/ppermute | solution.py:283
  41.7 0.0 collective-permute-done.11.refs_4_
  41.7 0.1 collective-permute-start.19
  41.8 0.0 copy-done
  41.8 2.4 %shard_map.47 = (f32[8,512]{1,0:T(8,128)S(1)}, f32[8,512]{1,0:T(8,128)S(1)}, f32[8,128,512]{2,1,0:T(8,128)S(1)}) custom-call(s32[9]{0:T(128)S(1)} %get-tuple-element.22.refs_0_, bf16[64,8192]{1,0:T(8,128)(2,1)S(1)} %copy-done, bf16[128,1024]{1,0:T(8,128)(2,1)S(1)} %pad_maximum_fusion.1.refs_2_, bf16[64,1024]{1,0:T(8,128)(2,1)S(1)} %collective-permute-done.1.refs_3_, ...), custom_call_target="tpu_custom_call" | custom-call | flops 939524096 | bytes 65536 | tf_op jit(solution)/shard_map/pallas_call | solution.py:261
  44.2 0.0 collective-permute-done.15.refs_5_
  44.2 0.0 collective-permute-done.4.refs_2_
  44.2 0.0 collective-permute-done.8.refs_3_
  44.3 3.4 %collective-permute-start.17 = (bf16[256,1024]{1,0:T(8,128)(2,1)S(1)}, bf16[256,1024]{1,0:T(8,128)(2,1)S(1)}, u32[]{:S(2)}, u32[]{:S(2)}) collective-permute-start(bf16[256,1024]{1,0:T(8,128)(2,1)S(1)} %pad_maximum_fusion), channel_id=1, source_target_pairs={{0,4},{4,0},{8,12},{12,8},{16,20},{20,16},{24,28},{28,24},{32,36},... | collective-permute-start | bytes 1572872 | tf_op jit(solution)/shard_map/ppermute | solution.py:283
  47.6 1.5 %collective-permute-done.17.refs_6_ = bf16[256,1024]{1,0:T(8,128)(2,1)S(1)} collective-permute-done((bf16[256,1024]{1,0:T(8,128)(2,1)S(1)}, bf16[256,1024]{1,0:T(8,128)(2,1)S(1)}, u32[]{:S(2)}, u32[]{:S(2)}) %collective-permute-start.17) | collective-permute-done | bytes 524320 | tf_op jit(solution)/shard_map/ppermute | solution.py:283
  49.2 0.0 collective-permute-done.18.refs_10_
  49.2 0.0 collective-permute-done.19.refs_11_
  49.2 2.0 %shard_map.48 = bf16[64,8192]{1,0:T(8,128)(2,1)} custom-call(s32[9]{0:T(128)S(1)} %get-tuple-element.22.refs_0_, bf16[64,8192]{1,0:T(8,128)(2,1)S(1)} %copy-done, bf16[64,1024]{1,0:T(8,128)(2,1)S(1)} %collective-permute-done.4.refs_2_, bf16[64,1024]{1,0:T(8,128)(2,1)S(1)} %collective-permute-done.8.refs_3_, ...), custom_call_target="tpu_custom_call" | custom-call | flops 536870912 | bytes 65536 | tf_op jit(solution)/shard_map/pallas_call | solution.py:261
  (1 shorter events, 0.0 us)
Async XLA Ops:
  0.0 41.8 %copy-start = (bf16[64,8192]{1,0:T(8,128)(2,1)S(1)}, bf16[64,8192]{1,0:T(8,128)(2,1)}, u32[]{:S(2)}) copy-start(bf16[64,8192]{1,0:T(8,128)(2,1)} %refs_1_.2) | copy-start | bytes 3145732
  0.0 36.9 %collective-permute-start.16 = (bf16[64,8192]{1,0:T(8,128)(2,1)}, bf16[64,8192]{1,0:T(8,128)(2,1)S(1)}, u32[]{:S(2)}, u32[]{:S(2)}) collective-permute-start(bf16[64,8192]{1,0:T(8,128)(2,1)} %refs_1_.2), channel_id=1, source_target_pairs={{0,4},{4,0},{8,12},{12,8},{16,20},{20,16},{24,28},{28,24},{32,36},... | collective-permute-start | bytes 3145736 | tf_op jit(solution)/shard_map/ppermute | solution.py:283
  3.2 6.5 %collective-permute-start = (bf16[64,1024]{1,0:T(8,128)(2,1)}, bf16[64,1024]{1,0:T(8,128)(2,1)S(1)}, u32[]{:S(2)}, u32[]{:S(2)}) collective-permute-start(bf16[64,1024]{1,0:T(8,128)(2,1)} %param.5), channel_id=1, source_target_pairs={{0,64},{4,68},{8,72},{12,76},{16,80},{20,84},{24,88},{28,92},{32,9... | collective-permute-start | bytes 393224 | tf_op jit(solution)/shard_map/ppermute | solution.py:280
  3.2 15.0 %collective-permute-start.1 = (bf16[64,1024]{1,0:T(8,128)(2,1)}, bf16[64,1024]{1,0:T(8,128)(2,1)S(1)}, u32[]{:S(2)}, u32[]{:S(2)}) collective-permute-start(bf16[64,1024]{1,0:T(8,128)(2,1)} %param.5), channel_id=1, source_target_pairs={{0,8},{4,12},{8,16},{12,20},{16,24},{20,28},{24,32},{28,36},{32,40... | collective-permute-start | bytes 393224 | tf_op jit(solution)/shard_map/ppermute | solution.py:280
  4.4 13.8 %collective-permute-start.12 = (bf16[64,1024]{1,0:T(8,128)(2,1)}, bf16[64,1024]{1,0:T(8,128)(2,1)S(1)}, u32[]{:S(2)}, u32[]{:S(2)}) collective-permute-start(bf16[64,1024]{1,0:T(8,128)(2,1)} %param.6), channel_id=1, source_target_pairs={{0,64},{4,68},{8,72},{12,76},{16,80},{20,84},{24,88},{28,92},{32,9... | collective-permute-start | bytes 393224 | tf_op jit(solution)/shard_map/ppermute | solution.py:280
  5.7 14.0 %collective-permute-start.5 = (bf16[64,1024]{1,0:T(8,128)(2,1)}, bf16[64,1024]{1,0:T(8,128)(2,1)S(1)}, u32[]{:S(2)}, u32[]{:S(2)}) collective-permute-start(bf16[64,1024]{1,0:T(8,128)(2,1)} %param.6), channel_id=1, source_target_pairs={{0,8},{4,12},{8,16},{12,20},{16,24},{20,28},{24,32},{28,36},{32,40... | collective-permute-start | bytes 393224 | tf_op jit(solution)/shard_map/ppermute | solution.py:280
  9.8 10.0 %collective-permute-start.9 = (bf16[64,1024]{1,0:T(8,128)(2,1)S(1)}, bf16[64,1024]{1,0:T(8,128)(2,1)S(1)}, u32[]{:S(2)}, u32[]{:S(2)}) collective-permute-start(bf16[64,1024]{1,0:T(8,128)(2,1)S(1)} %collective-permute-done.refs_5_), channel_id=1, source_target_pairs={{0,248},{4,252},{8,0},{12,4},{16,8},{20,12},{24,16},{28,20},{32,24... | collective-permute-start | bytes 393224 | tf_op jit(solution)/shard_map/ppermute | solution.py:280
  18.2 6.3 %collective-permute-start.13 = (bf16[64,1024]{1,0:T(8,128)(2,1)S(1)}, bf16[64,1024]{1,0:T(8,128)(2,1)S(1)}, u32[]{:S(2)}, u32[]{:S(2)}) collective-permute-start(bf16[64,1024]{1,0:T(8,128)(2,1)S(1)} %collective-permute-done.12.refs_6_), channel_id=1, source_target_pairs={{0,248},{4,252},{8,0},{12,4},{16,8},{20,12},{24,16},{28,20},{32,24... | collective-permute-start | bytes 393224 | tf_op jit(solution)/shard_map/ppermute | solution.py:280
  18.2 7.9 %collective-permute-start.2 = (bf16[64,1024]{1,0:T(8,128)(2,1)S(1)}, bf16[64,1024]{1,0:T(8,128)(2,1)S(1)}, u32[]{:S(2)}, u32[]{:S(2)}) collective-permute-start(bf16[64,1024]{1,0:T(8,128)(2,1)S(1)} %collective-permute-done.1.refs_3_), channel_id=1, source_target_pairs={{0,8},{4,12},{8,16},{12,20},{16,24},{20,28},{24,32},{28,36},{32,40... | collective-permute-start | bytes 393224 | tf_op jit(solution)/shard_map/ppermute | solution.py:280
  19.7 8.9 %collective-permute-start.6 = (bf16[64,1024]{1,0:T(8,128)(2,1)S(1)}, bf16[64,1024]{1,0:T(8,128)(2,1)S(1)}, u32[]{:S(2)}, u32[]{:S(2)}) collective-permute-start(bf16[64,1024]{1,0:T(8,128)(2,1)S(1)} %collective-permute-done.5.refs_4_), channel_id=1, source_target_pairs={{0,8},{4,12},{8,16},{12,20},{16,24},{20,28},{24,32},{28,36},{32,40... | collective-permute-start | bytes 393224 | tf_op jit(solution)/shard_map/ppermute | solution.py:280
  19.8 8.8 %collective-permute-start.10 = (bf16[64,1024]{1,0:T(8,128)(2,1)S(1)}, bf16[64,1024]{1,0:T(8,128)(2,1)S(1)}, u32[]{:S(2)}, u32[]{:S(2)}) collective-permute-start(bf16[64,1024]{1,0:T(8,128)(2,1)S(1)} %collective-permute-done.9.refs_9_), channel_id=1, source_target_pairs={{0,248},{4,252},{8,0},{12,4},{16,8},{20,12},{24,16},{28,20},{32,24... | collective-permute-start | bytes 393224 | tf_op jit(solution)/shard_map/ppermute | solution.py:280
  24.5 8.9 %collective-permute-start.14 = (bf16[64,1024]{1,0:T(8,128)(2,1)S(1)}, bf16[64,1024]{1,0:T(8,128)(2,1)S(1)}, u32[]{:S(2)}, u32[]{:S(2)}) collective-permute-start(bf16[64,1024]{1,0:T(8,128)(2,1)S(1)} %collective-permute-done.13.refs_10_), channel_id=1, source_target_pairs={{0,248},{4,252},{8,0},{12,4},{16,8},{20,12},{24,16},{28,20},{32,24... | collective-permute-start | bytes 393224 | tf_op jit(solution)/shard_map/ppermute | solution.py:280
  26.1 8.4 %collective-permute-start.3 = (bf16[64,1024]{1,0:T(8,128)(2,1)S(1)}, bf16[64,1024]{1,0:T(8,128)(2,1)S(1)}, u32[]{:S(2)}, u32[]{:S(2)}) collective-permute-start(bf16[64,1024]{1,0:T(8,128)(2,1)S(1)} %collective-permute-done.2.refs_7_), channel_id=1, source_target_pairs={{0,8},{4,12},{8,16},{12,20},{16,24},{20,28},{24,32},{28,36},{32,40... | collective-permute-start | bytes 393224 | tf_op jit(solution)/shard_map/ppermute | solution.py:280
  28.6 8.3 %collective-permute-start.7 = (bf16[64,1024]{1,0:T(8,128)(2,1)S(1)}, bf16[64,1024]{1,0:T(8,128)(2,1)S(1)}, u32[]{:S(2)}, u32[]{:S(2)}) collective-permute-start(bf16[64,1024]{1,0:T(8,128)(2,1)S(1)} %collective-permute-done.6.refs_8_), channel_id=1, source_target_pairs={{0,8},{4,12},{8,16},{12,20},{16,24},{20,28},{24,32},{28,36},{32,40... | collective-permute-start | bytes 393224 | tf_op jit(solution)/shard_map/ppermute | solution.py:280
  28.6 13.1 %collective-permute-start.11 = (bf16[64,1024]{1,0:T(8,128)(2,1)S(1)}, bf16[64,1024]{1,0:T(8,128)(2,1)S(1)}, u32[]{:S(2)}, u32[]{:S(2)}) collective-permute-start(bf16[64,1024]{1,0:T(8,128)(2,1)S(1)} %collective-permute-done.10.refs_13_), channel_id=1, source_target_pairs={{0,248},{4,252},{8,0},{12,4},{16,8},{20,12},{24,16},{28,20},{32,24... | collective-permute-start | bytes 393224 | tf_op jit(solution)/shard_map/ppermute | solution.py:280
  33.4 10.8 %collective-permute-start.15 = (bf16[64,1024]{1,0:T(8,128)(2,1)S(1)}, bf16[64,1024]{1,0:T(8,128)(2,1)S(1)}, u32[]{:S(2)}, u32[]{:S(2)}) collective-permute-start(bf16[64,1024]{1,0:T(8,128)(2,1)S(1)} %collective-permute-done.14.refs_14_), channel_id=1, source_target_pairs={{0,248},{4,252},{8,0},{12,4},{16,8},{20,12},{24,16},{28,20},{32,24... | collective-permute-start | bytes 393224 | tf_op jit(solution)/shard_map/ppermute | solution.py:280
  34.5 9.7 %collective-permute-start.4 = (bf16[64,1024]{1,0:T(8,128)(2,1)S(1)}, bf16[64,1024]{1,0:T(8,128)(2,1)S(1)}, u32[]{:S(2)}, u32[]{:S(2)}) collective-permute-start(bf16[64,1024]{1,0:T(8,128)(2,1)S(1)} %collective-permute-done.3.refs_11_), channel_id=1, source_target_pairs={{0,8},{4,12},{8,16},{12,20},{16,24},{20,28},{24,32},{28,36},{32,40... | collective-permute-start | bytes 393224 | tf_op jit(solution)/shard_map/ppermute | solution.py:280
  36.9 7.3 %collective-permute-start.8 = (bf16[64,1024]{1,0:T(8,128)(2,1)S(1)}, bf16[64,1024]{1,0:T(8,128)(2,1)S(1)}, u32[]{:S(2)}, u32[]{:S(2)}) collective-permute-start(bf16[64,1024]{1,0:T(8,128)(2,1)S(1)} %collective-permute-done.7.refs_12_), channel_id=1, source_target_pairs={{0,8},{4,12},{8,16},{12,20},{16,24},{20,28},{24,32},{28,36},{32,40... | collective-permute-start | bytes 393224 | tf_op jit(solution)/shard_map/ppermute | solution.py:280
  38.5 10.7 %collective-permute-start.18 = (bf16[640,512]{1,0:T(8,128)(2,1)S(1)}, bf16[640,512]{1,0:T(8,128)(2,1)S(1)}, u32[]{:S(2)}, u32[]{:S(2)}) collective-permute-start(bf16[640,512]{1,0:T(8,128)(2,1)S(1)} %get-tuple-element.26), channel_id=1, source_target_pairs={{0,4},{4,0},{8,12},{12,8},{16,20},{20,16},{24,28},{28,24},{32,36},... | collective-permute-start | bytes 1966088 | tf_op jit(solution)/shard_map/ppermute | solution.py:283
  41.7 7.5 %collective-permute-start.19 = (bf16[640,512]{1,0:T(8,128)(2,1)S(1)}, bf16[640,512]{1,0:T(8,128)(2,1)S(1)}, u32[]{:S(2)}, u32[]{:S(2)}) collective-permute-start(bf16[640,512]{1,0:T(8,128)(2,1)S(1)} %get-tuple-element.27), channel_id=1, source_target_pairs={{0,4},{4,0},{8,12},{12,8},{16,20},{20,16},{24,28},{28,24},{32,36},... | collective-permute-start | bytes 1966088 | tf_op jit(solution)/shard_map/ppermute | solution.py:283
  44.3 4.9 %collective-permute-start.17 = (bf16[256,1024]{1,0:T(8,128)(2,1)S(1)}, bf16[256,1024]{1,0:T(8,128)(2,1)S(1)}, u32[]{:S(2)}, u32[]{:S(2)}) collective-permute-start(bf16[256,1024]{1,0:T(8,128)(2,1)S(1)} %pad_maximum_fusion), channel_id=1, source_target_pairs={{0,4},{4,0},{8,12},{12,8},{16,20},{20,16},{24,28},{28,24},{32,36},... | collective-permute-start | bytes 1572872 | tf_op jit(solution)/shard_map/ppermute | solution.py:283
